TPU v7x, 128 devices: a whole 4x4x4 slice. The times are simulated.
128 devices in a mesh: pipe: 4 (over z_hi, core), tensor: 4 (over x), dp: 8 (over z_lo, y).
Axes of the slice: x: 4, y: 4, z: 4 (z_hi: 2, z_lo: 2; z = z_hi * 2 + z_lo), core: 2. Of those that a mesh axis runs over, the one named last changes fastest.
Arguments:
- inputs: bfloat16 [2, 512, 4096], P(None, ('tensor', 'dp')), may hold values from -6 to 6
- weights: bfloat16 [2, 4, 4096, 4096], P(None, 'pipe', None, 'tensor'), may hold values from -0.09375 to 0.09375
- norm_gains: float32 [2, 4, 4096], P(None, 'pipe'), may hold values from 0.1 to 1.9
- cotangent: bfloat16 [2, 512, 4096], P(None, ('tensor', 'dp')), may hold values from -6 to 6
Outputs:
- act_factor: bfloat16 [4096, 2, 4, 4096], P(('tensor', 'dp'), None, 'pipe')
- grad_factor: bfloat16 [4096, 2, 4, 4096], P(('tensor', 'dp'), None, 'pipe')
All inputs are finite; a program needn't handle non-finite values.
Results may differ from a plain program's by a relative error of at most 0.025.
Values may be sent and summed in bfloat16 or wider, within the bound.
No kernel may reach another device: no remote copies, remote signals or barrier semaphores. Data moves between devices by JAX's collectives and lax.ppermute only.
A program may use at most 192 MiB of HBM per device.

v0:
```python
import jax
import jax.numpy as jnp
from jax import lax
from jax.sharding import Mesh
from jax.sharding import PartitionSpec as P

DP = ("dp_0", "dp_1")
TENSOR_DP = ("tensor", "dp_0", "dp_1")


EPSILON = 1e-05


def passed_along(array, axis, by):
    peers = lax.axis_size(axis)
    return lax.ppermute(array, axis, [(i, (i + by) % peers) for i in range(peers)])


def sum_in_order(tiles, axes, order):
    inside = tiles.shape[1:]
    tiles = tiles.reshape(*(lax.axis_size(a) for a in axes), *inside)
    tiles = jnp.moveaxis(tiles, order, range(len(axes))).reshape(-1, *inside)
    for k in order:
        tiles = lax.psum_scatter(tiles, axes[k], scatter_dimension=0, tiled=True)
    return tiles[0]


def in_blocks(array, dim, peers):
    shape = array.shape
    tiles = array.reshape(*shape[:dim], peers, shape[dim] // peers, *shape[dim + 1 :])
    return jnp.moveaxis(tiles, dim, 0)


def sum_by_axis(array, axes, order, dim):
    peers = lax.axis_size(axes)
    return sum_in_order(in_blocks(array, dim, peers), axes, order)


def from_everyone(array, axis):
    copies = jnp.broadcast_to(array, (lax.axis_size(axis), *array.shape))
    return lax.all_to_all(copies, axis, split_axis=0, concat_axis=0, tiled=True)


def in_order(tiles, dim):
    tiles = jnp.moveaxis(tiles, 0, dim)
    shape = tiles.shape
    return tiles.reshape(*shape[:dim], shape[dim] * shape[dim + 1], *shape[dim + 2 :])


def gather_directly(array, axis, dim):
    tiles = from_everyone(array, axis)
    return in_order(tiles, dim)


def sum_at_owner(array, axis, dim):
    peers = lax.axis_size(axis)
    tiles = lax.all_to_all(in_blocks(array, dim, peers), axis, 0, 0, tiled=True)
    return jnp.sum(tiles.astype(jnp.float32), axis=0)


def normalize(hidden, gain_row):
    hidden_wide = hidden.astype(jnp.float32)
    inverse_rms = lax.rsqrt(jnp.mean(hidden_wide * hidden_wide, axis=-1, keepdims=True) + EPSILON)
    normed = (hidden_wide * inverse_rms * gain_row).astype(jnp.bfloat16)
    return (hidden_wide, inverse_rms, normed)


def body(inputs, weights, norm_gains, cotangent):
    micro_count, shard_rows, features = inputs.shape
    slot_count = weights.shape[0]
    quarter = weights.shape[3]
    tensor_count = lax.axis_size("tensor")
    pipe_count = lax.axis_size("pipe")
    dp_count = lax.axis_size(DP)
    layer_count = slot_count * pipe_count
    section_index = lax.axis_index("pipe")
    column = lax.axis_index("tensor")
    tick_count = micro_count + layer_count - 1
    group_rows = tensor_count * shard_rows
    group_size = micro_count * group_rows
    stash_count = slot_count * micro_count + 1
    own_rows = quarter // dp_count
    inv_tokens = 1.0 / (micro_count * group_rows * dp_count)
    row_base = column * quarter
    normed_stash = jnp.zeros((stash_count, group_rows, features), jnp.bfloat16)
    hidden_stash = jnp.zeros((stash_count, shard_rows, features), jnp.bfloat16)
    grad_stash = jnp.zeros((stash_count, group_rows, features), jnp.bfloat16)
    received = jnp.zeros((shard_rows, features), jnp.bfloat16)
    for moment in range(tick_count):
        micro_index = (moment - section_index) % pipe_count
        layer_index = moment - micro_index
        usable = (micro_index < micro_count) & (layer_index >= 0) & (layer_index < layer_count)
        slot_index = jnp.clip(layer_index // pipe_count, 0, slot_count - 1)
        target = jnp.where(usable, slot_index * micro_count + micro_index, stash_count - 1)
        if moment < micro_count:
            current = jnp.where(section_index == 0, inputs[moment], received)
        else:
            current = received
        weight = lax.dynamic_index_in_dim(weights, slot_index, 0, keepdims=False)[0]
        gain_row = lax.dynamic_index_in_dim(norm_gains, slot_index, 0, keepdims=False)[0]
        hidden_wide, inverse_rms, normed = normalize(current, gain_row)
        gathered = lax.all_gather(normed, "tensor", axis=0, tiled=True)
        normed_stash = lax.dynamic_update_index_in_dim(normed_stash, gathered, target, 0)
        hidden_stash = lax.dynamic_update_index_in_dim(hidden_stash, current, target, 0)
        if moment + 1 < tick_count:
            active = usable & (layer_index + 1 < layer_count)
            product = lax.cond(
                active,
                lambda: jnp.dot(gathered, weight, preferred_element_type=jnp.float32).astype(
                    jnp.bfloat16
                ),
                lambda: jnp.zeros((group_rows, quarter), jnp.bfloat16),
            )
            returned = lax.all_to_all(product, "tensor", split_axis=0, concat_axis=1, tiled=True)
            following = (hidden_wide + returned.astype(jnp.float32)).astype(jnp.bfloat16)
            received = passed_along(following, "pipe", 1)
    act_tokens = normed_stash[: stash_count - 1].reshape(slot_count, group_size, features)

    def gram_rows(tokens_all, row_total):
        partials = []
        for slot_pick in range(slot_count):
            tokens_block = tokens_all[slot_pick]
            columns = lax.dynamic_slice_in_dim(tokens_block, row_base, row_total, 1)
            partials.append(
                lax.dot_general(
                    columns,
                    tokens_block,
                    (((0,), (0,)), ((), ())),
                    preferred_element_type=jnp.float32,
                )
                * inv_tokens
            )
        return jnp.stack(partials, 1)[:, :, None, :]

    act_factor = (
        sum_by_axis(
            gram_rows(act_tokens, own_rows * lax.axis_size(DP)).astype(jnp.bfloat16), DP, (1, 0), 0
        )
        .astype(jnp.float32)
        .astype(jnp.bfloat16)
    )
    received = jnp.zeros((shard_rows, features), jnp.bfloat16)
    for moment in range(tick_count):
        micro_index = (section_index + 1 - layer_count + moment) % pipe_count
        depth = moment - micro_index
        layer_index = layer_count - 1 - depth
        usable = (micro_index < micro_count) & (depth >= 0) & (depth < layer_count)
        slot_index = jnp.clip(layer_index // pipe_count, 0, slot_count - 1)
        target = jnp.where(usable, slot_index * micro_count + micro_index, stash_count - 1)
        if moment < micro_count:
            current = jnp.where(section_index == pipe_count - 1, cotangent[moment], received)
        else:
            current = received
        gathered = gather_directly(current, "tensor", 0)
        grad_stash = lax.dynamic_update_index_in_dim(grad_stash, gathered, target, 0)
        if moment + 1 < tick_count:
            active = usable & (layer_index > 0)
            weight = lax.dynamic_index_in_dim(weights, slot_index, 0, keepdims=False)[0]
            gain_row = lax.dynamic_index_in_dim(norm_gains, slot_index, 0, keepdims=False)[0]
            own_columns = lax.dynamic_slice_in_dim(gathered, row_base, quarter, 1)

            def partial_rows(
                row_start, row_total, own_columns=own_columns, weight=weight, active=active
            ):
                piece = own_columns
                return lax.cond(
                    active,
                    lambda: lax.dot_general(
                        piece, weight, (((1,), (1,)), ((), ())), preferred_element_type=jnp.float32
                    ),
                    lambda: jnp.zeros((row_total, features), jnp.float32),
                )

            back_sum = sum_at_owner(
                partial_rows(jnp.int32(0), shard_rows * lax.axis_size("tensor")).astype(
                    jnp.bfloat16
                ),
                "tensor",
                0,
            )
            stored = lax.dynamic_index_in_dim(hidden_stash, target, 0, keepdims=False)
            hidden_wide = stored.astype(jnp.float32)
            inverse_rms = lax.rsqrt(
                jnp.mean(hidden_wide * hidden_wide, axis=-1, keepdims=True) + EPSILON
            )
            scaled = gain_row * back_sum
            inner = jnp.mean(hidden_wide * scaled, axis=-1, keepdims=True)
            following = (
                current.astype(jnp.float32)
                + inverse_rms * scaled
                - inverse_rms**3 * hidden_wide * inner
            ).astype(jnp.bfloat16)
            received = passed_along(following, "pipe", -1)
    grad_tokens = grad_stash[: stash_count - 1].reshape(slot_count, group_size, features)
    grad_factor = lax.psum_scatter(
        gram_rows(grad_tokens, own_rows * lax.axis_size(DP)).astype(jnp.bfloat16),
        DP,
        scatter_dimension=0,
        tiled=True,
    )
    return (act_factor, grad_factor)


def solution(mesh):
    split = Mesh(
        mesh.devices.reshape(mesh.shape["pipe"], mesh.shape["tensor"], 2, 4),
        ("pipe", "tensor", "dp_0", "dp_1"),
    )
    placed = (
        P(None, TENSOR_DP, None),
        P(None, "pipe", None, "tensor"),
        P(None, "pipe", None),
        P(None, TENSOR_DP, None),
    )
    return jax.shard_map(
        body,
        mesh=split,
        in_specs=placed,
        out_specs=(P(TENSOR_DP, None, "pipe", None), P(TENSOR_DP, None, "pipe", None)),
        check_vma=False,
    )
```

profile of v0, /device:TPU:1, one launch (start us, length us, event | category | flops | bytes accessed | tf_op | source)
XLA Modules:
  0.0 863.8 jit_solution(3263074517311799120)
XLA Ops:
  11.8 12.8 %all_gather.27 = bf16[64,4096]{1,0:T(8,128)(2,1)} all-gather(bf16[16,4096]{1,0:T(8,128)(2,1)S(1)} %fusion.155), channel_id=1, replica_groups=mesh['pipe'=4,'tensor'=4,'dp_0'=2,'dp_1'=4] {'tensor'}, dimensions={0}, use_global_device_ids=true | all-gather | bytes 655360 | tf_op jit(solution)/shard_map/all_gather | solution.py:102
  33.5 8.3 collective-permute-start
  44.7 11.5 %all_gather.28 = bf16[64,4096]{1,0:T(8,128)(2,1)} all-gather(bf16[16,4096]{1,0:T(8,128)(2,1)S(1)} %fusion.127), channel_id=1, replica_groups=mesh['pipe'=4,'tensor'=4,'dp_0'=2,'dp_1'=4] {'tensor'}, dimensions={0}, use_global_device_ids=true | all-gather | bytes 655360 | tf_op jit(solution)/shard_map/all_gather | solution.py:102
  56.2 5.1 conditional.17
  56.2 5.1 fusion.16
  61.4 7.2 all_to_all.189
  70.9 7.7 collective-permute-done.1
  78.8 11.5 %all_gather.29 = bf16[64,4096]{1,0:T(8,128)(2,1)} all-gather(bf16[16,4096]{1,0:T(8,128)(2,1)S(1)} %fusion.131), channel_id=1, replica_groups=mesh['pipe'=4,'tensor'=4,'dp_0'=2,'dp_1'=4] {'tensor'}, dimensions={0}, use_global_device_ids=true | all-gather | bytes 655360 | tf_op jit(solution)/shard_map/all_gather | solution.py:102
  90.4 5.1 conditional.18
  90.4 5.1 fusion.26
  95.5 7.2 all_to_all.190
  107.9 11.5 %all_gather.30 = bf16[64,4096]{1,0:T(8,128)(2,1)} all-gather(bf16[16,4096]{1,0:T(8,128)(2,1)S(1)} %fusion.135), channel_id=1, replica_groups=mesh['pipe'=4,'tensor'=4,'dp_0'=2,'dp_1'=4] {'tensor'}, dimensions={0}, use_global_device_ids=true | all-gather | bytes 655360 | tf_op jit(solution)/shard_map/all_gather | solution.py:102
  119.4 7.3 all_to_all.191
  126.8 12.1 %collective-permute-start.3 = (bf16[16,4096]{1,0:T(8,128)(2,1)S(1)}, bf16[16,4096]{1,0:T(8,128)(2,1)S(1)}, u32[]{:S(2)}, u32[]{:S(2)}) collective-permute-start(bf16[16,4096]{1,0:T(8,128)(2,1)S(1)} %fusion.136), channel_id=1, source_target_pairs={{0,32},{32,64},{64,96},{96,0},{1,33},{33,65},{65,97},{97,1},{2,34}... | collective-permute-start | bytes 393224 | tf_op jit(solution)/shard_map/ppermute | solution.py:16
  141.1 10.6 %all_gather.31 = bf16[64,4096]{1,0:T(8,128)(2,1)} all-gather(bf16[16,4096]{1,0:T(8,128)(2,1)S(1)} %fusion.139), channel_id=1, replica_groups=mesh['pipe'=4,'tensor'=4,'dp_0'=2,'dp_1'=4] {'tensor'}, dimensions={0}, use_global_device_ids=true | all-gather | bytes 655360 | tf_op jit(solution)/shard_map/all_gather | solution.py:102
  163.2 8.1 collective-permute-start.4
  176.4 11.5 %all_gather.32 = bf16[64,4096]{1,0:T(8,128)(2,1)} all-gather(bf16[16,4096]{1,0:T(8,128)(2,1)S(1)} %fusion.143), channel_id=1, replica_groups=mesh['pipe'=4,'tensor'=4,'dp_0'=2,'dp_1'=4] {'tensor'}, dimensions={0}, use_global_device_ids=true | all-gather | bytes 655360 | tf_op jit(solution)/shard_map/all_gather | solution.py:102
  187.9 6.3 conditional.21
  188.5 5.8 fusion.56
  207.0 7.8 collective-permute-done.5
  216.2 11.5 %all_gather.33 = bf16[64,4096]{1,0:T(8,128)(2,1)} all-gather(bf16[16,4096]{1,0:T(8,128)(2,1)S(1)} %fusion.147), channel_id=1, replica_groups=mesh['pipe'=4,'tensor'=4,'dp_0'=2,'dp_1'=4] {'tensor'}, dimensions={0}, use_global_device_ids=true | all-gather | bytes 655360 | tf_op jit(solution)/shard_map/all_gather | solution.py:102
  227.8 5.8 conditional.22
  227.8 5.8 fusion.66
  250.4 11.5 %all_gather.34 = bf16[64,4096]{1,0:T(8,128)(2,1)} all-gather(bf16[16,4096]{1,0:T(8,128)(2,1)S(1)} %fusion.151), channel_id=1, replica_groups=mesh['pipe'=4,'tensor'=4,'dp_0'=2,'dp_1'=4] {'tensor'}, dimensions={0}, use_global_device_ids=true | all-gather | bytes 655360 | tf_op jit(solution)/shard_map/all_gather | solution.py:102
  273.3 10.4 %collective-permute-start.7 = (bf16[16,4096]{1,0:T(8,128)(2,1)S(1)}, bf16[16,4096]{1,0:T(8,128)(2,1)S(1)}, u32[]{:S(2)}, u32[]{:S(2)}) collective-permute-start(bf16[16,4096]{1,0:T(8,128)(2,1)S(1)} %fusion.152), channel_id=1, source_target_pairs={{0,32},{32,64},{64,96},{96,0},{1,33},{33,65},{65,97},{97,1},{2,34}... | collective-permute-start | bytes 393224 | tf_op jit(solution)/shard_map/ppermute | solution.py:16
  287.2 11.1 %all_gather.35 = bf16[64,4096]{1,0:T(8,128)(2,1)S(1)} all-gather(bf16[16,4096]{1,0:T(8,128)(2,1)S(1)} %fusion.124), channel_id=1, replica_groups=mesh['pipe'=4,'tensor'=4,'dp_0'=2,'dp_1'=4] {'tensor'}, dimensions={0}, use_global_device_ids=true | all-gather | bytes 655360 | tf_op jit(solution)/shard_map/all_gather | solution.py:102
  304.9 6.6 copy.39
  317.6 6.8 all-to-all-done.8
  329.0 6.9 all-to-all-done.9
  336.6 6.4 collective-permute-start.8
  343.1 6.3 collective-permute-done.8
  354.4 9.4 %all-to-all-done.10 = bf16[4,16,4096]{2,1,0:T(8,128)(2,1)} async-done(((bf16[4,16,4096]{2,1,0:T(8,128)(2,1)}), bf16[4,16,4096]{2,1,0:T(8,128)(2,1)}, u32[]{:S(2)}, u32[]{:S(2)}) %all-to-all-start.10) | async-done | bytes 524320 | tf_op jit(solution)/shard_map/all_to_all | solution.py:41
  368.2 8.0 all-to-all-done.11
  379.1 6.3 collective-permute-done.9
  390.4 7.6 all-to-all-done.12
  398.0 7.0 conditional.26
  398.0 7.0 fusion.90
  408.7 6.9 all-to-all-done.13
  416.0 5.9 collective-permute-done.10
  426.9 7.0 all-to-all-done.14
  433.9 7.0 conditional.27
  433.9 7.0 fusion.95
  444.5 6.9 all-to-all-done.15
  452.1 5.9 collective-permute-done.11
  463.0 7.0 all-to-all-done.16
  474.3 6.9 all-to-all-done.17
  493.9 6.3 all-to-all-done.18
  505.2 7.0 all-to-all-done.19
  517.7 6.4 collective-permute-done.13
  530.1 5.9 all-to-all-done.20
  536.0 6.9 conditional.30
  536.0 6.9 fusion.110
  548.2 6.8 all-to-all-done.21
  568.5 5.9 all-to-all-done.22
  574.4 7.2 conditional.31
  574.6 7.0 fusion.115
  586.8 5.9 all-to-all-done.23
  595.4 4.8 collective-permute-done.15
  605.6 5.8 all-to-all-done.24
  616.4 6.8 pad_maximum_fusion
  624.0 169.5 %reduce-scatter.8.cloned.1.call-done = bf16[128,2,1,4096]{3,0,2,1:T(8,128)(2,1)} async-done(((bf16[1024,2,1,4096]{3,0,2,1:T(8,128)(2,1)}), bf16[128,2,1,4096]{3,0,2,1:T(8,128)(2,1)}) %reduce-scatter.8.cloned.1.call-update) | async-done | bytes 2097168 | tf_op jit(solution)/shard_map/reduce_scatter | solution.py:195
  793.5 5.1 copy.41
  798.6 53.0 %reduce-scatter.6.cloned.1.call-done = bf16[1,128,2,1,4096]{4,1,3,2,0:T(8,128)(2,1)} async-done(((bf16[2,128,2,1,4096]{4,1,3,2,0:T(8,128)(2,1)}), bf16[1,128,2,1,4096]{4,1,3,2,0:T(8,128)(2,1)}) %reduce-scatter.6.cloned.1.call-update) | async-done | bytes 2097168 | tf_op jit(solution)/shard_map/reduce_scatter | solution.py:24
  851.6 5.1 copy.40
  (246 shorter events, 217.5 us)
Async XLA Ops:
  7.2 26.3 %copy-start.8 = (bf16[2,16,4096]{2,1,0:T(8,128)(2,1)S(1)}, bf16[2,16,4096]{2,1,0:T(8,128)(2,1)}, u32[]{:S(2)}) copy-start(bf16[2,16,4096]{2,1,0:T(8,128)(2,1)} %param.36) | copy-start | bytes 786436
  25.3 8.1 all-to-all-start
  33.5 10.9 %collective-permute-start = (bf16[16,4096]{1,0:T(8,128)(2,1)S(1)}, bf16[16,4096]{1,0:T(8,128)(2,1)S(1)}, u32[]{:S(2)}, u32[]{:S(2)}) collective-permute-start(bf16[16,4096]{1,0:T(8,128)(2,1)S(1)} %fusion.156), channel_id=1, source_target_pairs={{0,32},{32,64},{64,96},{96,0},{1,33},{33,65},{65,97},{97,1},{2,34}... | collective-permute-start | bytes 393224 | tf_op jit(solution)/shard_map/ppermute | solution.py:16
  68.7 9.9 %collective-permute-start.1 = (bf16[16,4096]{1,0:T(8,128)(2,1)S(1)}, bf16[16,4096]{1,0:T(8,128)(2,1)S(1)}, u32[]{:S(2)}, u32[]{:S(2)}) collective-permute-start(bf16[16,4096]{1,0:T(8,128)(2,1)S(1)} %fusion.128), channel_id=1, source_target_pairs={{0,32},{32,64},{64,96},{96,0},{1,33},{33,65},{65,97},{97,1},{2,34}... | collective-permute-start | bytes 393224 | tf_op jit(solution)/shard_map/ppermute | solution.py:16
  102.8 4.8 collective-permute-start.2
  126.8 14.0 %collective-permute-start.3 = (bf16[16,4096]{1,0:T(8,128)(2,1)S(1)}, bf16[16,4096]{1,0:T(8,128)(2,1)S(1)}, u32[]{:S(2)}, u32[]{:S(2)}) collective-permute-start(bf16[16,4096]{1,0:T(8,128)(2,1)S(1)} %fusion.136), channel_id=1, source_target_pairs={{0,32},{32,64},{64,96},{96,0},{1,33},{33,65},{65,97},{97,1},{2,34}... | collective-permute-start | bytes 393224 | tf_op jit(solution)/shard_map/ppermute | solution.py:16
  140.8 11.6 %copy-start = (bf16[16,4096]{1,0:T(8,128)(2,1)}, bf16[16,4096]{1,0:T(8,128)(2,1)S(1)}, u32[]{:S(2)}) copy-start(bf16[16,4096]{1,0:T(8,128)(2,1)S(1)} %collective-permute-done.3) | copy-start | bytes 393220
  152.4 8.8 %all-to-all-start.4 = ((bf16[4,16,1024]{2,1,0:T(8,128)(2,1)}), bf16[4,16,1024]{2,1,0:T(8,128)(2,1)}, u32[]{:S(2)}, u32[]{:S(2)}) async-start(bf16[4,16,1024]{2,1,0:T(8,128)(2,1)} %bitcast.53), calls=%async_computation.4 | async-start | bytes 262144 | tf_op jit(solution)/shard_map/all_to_all | solution.py:114
  163.2 11.8 %collective-permute-start.4 = (bf16[16,4096]{1,0:T(8,128)(2,1)S(1)}, bf16[16,4096]{1,0:T(8,128)(2,1)S(1)}, u32[]{:S(2)}, u32[]{:S(2)}) collective-permute-start(bf16[16,4096]{1,0:T(8,128)(2,1)S(1)} %fusion.140), channel_id=1, source_target_pairs={{0,32},{32,64},{64,96},{96,0},{1,33},{33,65},{65,97},{97,1},{2,34}... | collective-permute-start | bytes 393224 | tf_op jit(solution)/shard_map/ppermute | solution.py:16
  174.9 0.6 copy-start.2
  194.3 8.8 %all-to-all-start.5 = ((bf16[4,16,1024]{2,1,0:T(8,128)(2,1)}), bf16[4,16,1024]{2,1,0:T(8,128)(2,1)}, u32[]{:S(2)}, u32[]{:S(2)}) async-start(bf16[4,16,1024]{2,1,0:T(8,128)(2,1)} %bitcast.333), calls=%async_computation.5 | async-start | bytes 262144 | tf_op jit(solution)/shard_map/all_to_all | solution.py:114
  205.0 9.8 %collective-permute-start.5 = (bf16[16,4096]{1,0:T(8,128)(2,1)S(1)}, bf16[16,4096]{1,0:T(8,128)(2,1)S(1)}, u32[]{:S(2)}, u32[]{:S(2)}) collective-permute-start(bf16[16,4096]{1,0:T(8,128)(2,1)S(1)} %fusion.144), channel_id=1, source_target_pairs={{0,32},{32,64},{64,96},{96,0},{1,33},{33,65},{65,97},{97,1},{2,34}... | collective-permute-start | bytes 393224 | tf_op jit(solution)/shard_map/ppermute | solution.py:16
  214.7 0.6 copy-start.4
  233.5 8.8 %all-to-all-start.6 = ((bf16[4,16,1024]{2,1,0:T(8,128)(2,1)}), bf16[4,16,1024]{2,1,0:T(8,128)(2,1)}, u32[]{:S(2)}, u32[]{:S(2)}) async-start(bf16[4,16,1024]{2,1,0:T(8,128)(2,1)} %bitcast.334), calls=%async_computation.6 | async-start | bytes 262144 | tf_op jit(solution)/shard_map/all_to_all | solution.py:114
  244.3 4.6 collective-permute-start.6
  248.9 0.7 copy-start.6
  262.6 8.8 %all-to-all-start.7 = ((bf16[4,16,1024]{2,1,0:T(8,128)(2,1)}), bf16[4,16,1024]{2,1,0:T(8,128)(2,1)}, u32[]{:S(2)}, u32[]{:S(2)}) async-start(bf16[4,16,1024]{2,1,0:T(8,128)(2,1)} %bitcast.335), calls=%async_computation.7 | async-start | bytes 262144 | tf_op jit(solution)/shard_map/all_to_all | solution.py:114
  266.6 357.1 %reduce-scatter.4.cloned.1.call-start = ((), (), s32[]{:S(2)}) async-start(), calls=%async_computation.28 | async-start | bytes 20971520 | tf_op jit(solution)/shard_map/reduce_scatter | solution.py:24
  273.3 12.3 %collective-permute-start.7 = (bf16[16,4096]{1,0:T(8,128)(2,1)S(1)}, bf16[16,4096]{1,0:T(8,128)(2,1)S(1)}, u32[]{:S(2)}, u32[]{:S(2)}) collective-permute-start(bf16[16,4096]{1,0:T(8,128)(2,1)S(1)} %fusion.152), channel_id=1, source_target_pairs={{0,32},{32,64},{64,96},{96,0},{1,33},{33,65},{65,97},{97,1},{2,34}... | collective-permute-start | bytes 393224 | tf_op jit(solution)/shard_map/ppermute | solution.py:16
  285.7 0.7 copy-start.9
  311.5 0.9 copy-start.11
  311.5 24.4 %copy-start.1 = (bf16[16,4096]{1,0:T(8,128)(2,1)S(1)}, bf16[16,4096]{1,0:T(8,128)(2,1)}, u32[]{:S(2)}) copy-start(bf16[16,4096]{1,0:T(8,128)(2,1)} %copy-done) | copy-start | bytes 393220
  311.5 24.4 %copy-start.3 = (bf16[16,4096]{1,0:T(8,128)(2,1)S(1)}, bf16[16,4096]{1,0:T(8,128)(2,1)}, u32[]{:S(2)}) copy-start(bf16[16,4096]{1,0:T(8,128)(2,1)} %copy-done.2) | copy-start | bytes 393220
  311.5 24.5 %copy-start.5 = (bf16[16,4096]{1,0:T(8,128)(2,1)S(1)}, bf16[16,4096]{1,0:T(8,128)(2,1)}, u32[]{:S(2)}) copy-start(bf16[16,4096]{1,0:T(8,128)(2,1)} %copy-done.4) | copy-start | bytes 393220
  311.6 24.5 %copy-start.7 = (bf16[16,4096]{1,0:T(8,128)(2,1)S(1)}, bf16[16,4096]{1,0:T(8,128)(2,1)}, u32[]{:S(2)}) copy-start(bf16[16,4096]{1,0:T(8,128)(2,1)} %copy-done.6) | copy-start | bytes 393220
  311.6 24.5 %copy-start.10 = (bf16[16,4096]{1,0:T(8,128)(2,1)S(1)}, bf16[16,4096]{1,0:T(8,128)(2,1)}, u32[]{:S(2)}) copy-start(bf16[16,4096]{1,0:T(8,128)(2,1)} %copy-done.9) | copy-start | bytes 393220
  313.3 11.1 %all-to-all-start.8 = ((bf16[4,16,4096]{2,1,0:T(8,128)(2,1)}), bf16[4,16,4096]{2,1,0:T(8,128)(2,1)}, u32[]{:S(2)}, u32[]{:S(2)}) async-start(bf16[4,16,4096]{2,1,0:T(8,128)(2,1)} %broadcast_in_dim.147), calls=%async_computation.10 | async-start | bytes 1048576 | tf_op jit(solution)/shard_map/all_to_all | solution.py:41
  325.4 10.4 %all-to-all-start.9 = ((bf16[4,16,4096]{2,1,0:T(8,128)(2,1)}), bf16[4,16,4096]{2,1,0:T(8,128)(2,1)S(1)}, u32[]{:S(2)}, u32[]{:S(2)}) async-start(bf16[4,16,4096]{2,1,0:T(8,128)(2,1)} %bitcast.89), calls=%async_computation.11 | async-start | bytes 1048576 | tf_op jit(solution)/shard_map/all_to_all | solution.py:57
  335.9 40.4 %copy-start.18 = (f32[1,1,4096]{2,1,0:T(1,128)S(1)}, f32[1,1,4096]{2,1,0:T(1,128)}, u32[]{:S(2)}) copy-start(f32[1,1,4096]{2,1,0:T(1,128)} %get-tuple-element.518) | copy-start | bytes 49156
  336.6 12.8 %collective-permute-start.8 = (bf16[16,4096]{1,0:T(8,128)(2,1)S(1)}, bf16[16,4096]{1,0:T(8,128)(2,1)S(1)}, u32[]{:S(2)}, u32[]{:S(2)}) collective-permute-start(bf16[16,4096]{1,0:T(8,128)(2,1)S(1)} %fusion.160), channel_id=1, source_target_pairs={{0,96},{32,0},{64,32},{96,64},{1,97},{33,1},{65,33},{97,65},{2,98}... | collective-permute-start | bytes 393224 | tf_op jit(solution)/shard_map/ppermute | solution.py:16
  350.3 13.5 %all-to-all-start.10 = ((bf16[4,16,4096]{2,1,0:T(8,128)(2,1)}), bf16[4,16,4096]{2,1,0:T(8,128)(2,1)}, u32[]{:S(2)}, u32[]{:S(2)}) async-start(bf16[4,16,4096]{2,1,0:T(8,128)(2,1)} %broadcast_in_dim.158), calls=%async_computation.12 | async-start | bytes 1048576 | tf_op jit(solution)/shard_map/all_to_all | solution.py:41
  364.6 51.0 %copy-start.17 = (f32[1,1,4096]{2,1,0:T(1,128)S(1)}, f32[1,1,4096]{2,1,0:T(1,128)}, u32[]{:S(2)}) copy-start(f32[1,1,4096]{2,1,0:T(1,128)} %get-tuple-element.517) | copy-start | bytes 49156
  364.6 11.7 %all-to-all-start.11 = ((bf16[4,16,4096]{2,1,0:T(8,128)(2,1)}), bf16[4,16,4096]{2,1,0:T(8,128)(2,1)S(1)}, u32[]{:S(2)}, u32[]{:S(2)}) async-start(bf16[4,16,4096]{2,1,0:T(8,128)(2,1)} %bitcast.94), calls=%async_computation.13 | async-start | bytes 1048576 | tf_op jit(solution)/shard_map/all_to_all | solution.py:57
  376.7 8.7 %collective-permute-start.9 = (bf16[16,4096]{1,0:T(8,128)(2,1)S(1)}, bf16[16,4096]{1,0:T(8,128)(2,1)S(1)}, u32[]{:S(2)}, u32[]{:S(2)}) collective-permute-start(bf16[16,4096]{1,0:T(8,128)(2,1)S(1)} %fusion.165), channel_id=1, source_target_pairs={{0,96},{32,0},{64,32},{96,64},{1,97},{33,1},{65,33},{97,65},{2,98}... | collective-permute-start | bytes 393224 | tf_op jit(solution)/shard_map/ppermute | solution.py:16
  386.2 11.8 %all-to-all-start.12 = ((bf16[4,16,4096]{2,1,0:T(8,128)(2,1)}), bf16[4,16,4096]{2,1,0:T(8,128)(2,1)}, u32[]{:S(2)}, u32[]{:S(2)}) async-start(bf16[4,16,4096]{2,1,0:T(8,128)(2,1)} %broadcast_in_dim.160), calls=%async_computation.14 | async-start | bytes 1048576 | tf_op jit(solution)/shard_map/all_to_all | solution.py:41
  405.0 46.4 %copy-start.16 = (f32[1,1,4096]{2,1,0:T(1,128)S(1)}, f32[1,1,4096]{2,1,0:T(1,128)}, u32[]{:S(2)}) copy-start(f32[1,1,4096]{2,1,0:T(1,128)} %get-tuple-element.516) | copy-start | bytes 49156
  405.0 10.5 %all-to-all-start.13 = ((bf16[4,16,4096]{2,1,0:T(8,128)(2,1)}), bf16[4,16,4096]{2,1,0:T(8,128)(2,1)S(1)}, u32[]{:S(2)}, u32[]{:S(2)}) async-start(bf16[4,16,4096]{2,1,0:T(8,128)(2,1)} %bitcast.99), calls=%async_computation.15 | async-start | bytes 1048576 | tf_op jit(solution)/shard_map/all_to_all | solution.py:57
  416.0 6.0 collective-permute-start.10
  422.8 11.1 %all-to-all-start.14 = ((bf16[4,16,4096]{2,1,0:T(8,128)(2,1)}), bf16[4,16,4096]{2,1,0:T(8,128)(2,1)}, u32[]{:S(2)}, u32[]{:S(2)}) async-start(bf16[4,16,4096]{2,1,0:T(8,128)(2,1)} %broadcast_in_dim.162), calls=%async_computation.16 | async-start | bytes 1048576 | tf_op jit(solution)/shard_map/all_to_all | solution.py:41
  440.9 40.4 %copy-start.15 = (f32[1,1,4096]{2,1,0:T(1,128)S(1)}, f32[1,1,4096]{2,1,0:T(1,128)}, u32[]{:S(2)}) copy-start(f32[1,1,4096]{2,1,0:T(1,128)} %get-tuple-element.515) | copy-start | bytes 49156
  440.9 10.5 %all-to-all-start.15 = ((bf16[4,16,4096]{2,1,0:T(8,128)(2,1)}), bf16[4,16,4096]{2,1,0:T(8,128)(2,1)S(1)}, u32[]{:S(2)}, u32[]{:S(2)}) async-start(bf16[4,16,4096]{2,1,0:T(8,128)(2,1)} %bitcast.104), calls=%async_computation.17 | async-start | bytes 1048576 | tf_op jit(solution)/shard_map/all_to_all | solution.py:57
  451.8 6.2 collective-permute-start.11
  458.8 11.2 %all-to-all-start.16 = ((bf16[4,16,4096]{2,1,0:T(8,128)(2,1)}), bf16[4,16,4096]{2,1,0:T(8,128)(2,1)}, u32[]{:S(2)}, u32[]{:S(2)}) async-start(bf16[4,16,4096]{2,1,0:T(8,128)(2,1)} %broadcast_in_dim.164), calls=%async_computation.18 | async-start | bytes 1048576 | tf_op jit(solution)/shard_map/all_to_all | solution.py:41
  470.8 10.4 %all-to-all-start.17 = ((bf16[4,16,4096]{2,1,0:T(8,128)(2,1)}), bf16[4,16,4096]{2,1,0:T(8,128)(2,1)S(1)}, u32[]{:S(2)}, u32[]{:S(2)}) async-start(bf16[4,16,4096]{2,1,0:T(8,128)(2,1)} %bitcast.109), calls=%async_computation.19 | async-start | bytes 1048576 | tf_op jit(solution)/shard_map/all_to_all | solution.py:57
  481.6 6.0 collective-permute-start.12
  485.5 27.8 %copy-start.14 = (f32[1,1,4096]{2,1,0:T(1,128)S(1)}, f32[1,1,4096]{2,1,0:T(1,128)}, u32[]{:S(2)}) copy-start(f32[1,1,4096]{2,1,0:T(1,128)} %get-tuple-element.514) | copy-start | bytes 49156
  488.4 11.8 %all-to-all-start.18 = ((bf16[4,16,4096]{2,1,0:T(8,128)(2,1)}), bf16[4,16,4096]{2,1,0:T(8,128)(2,1)}, u32[]{:S(2)}, u32[]{:S(2)}) async-start(bf16[4,16,4096]{2,1,0:T(8,128)(2,1)} %broadcast_in_dim.166), calls=%async_computation.20 | async-start | bytes 1048576 | tf_op jit(solution)/shard_map/all_to_all | solution.py:41
  501.0 11.1 %all-to-all-start.19 = ((bf16[4,16,4096]{2,1,0:T(8,128)(2,1)}), bf16[4,16,4096]{2,1,0:T(8,128)(2,1)}, u32[]{:S(2)}, u32[]{:S(2)}) async-start(bf16[4,16,4096]{2,1,0:T(8,128)(2,1)} %bitcast.317), calls=%async_computation.21 | async-start | bytes 1048576 | tf_op jit(solution)/shard_map/all_to_all | solution.py:57
  505.2 50.9 %copy-start.13 = (f32[1,1,4096]{2,1,0:T(1,128)S(1)}, f32[1,1,4096]{2,1,0:T(1,128)}, u32[]{:S(2)}) copy-start(f32[1,1,4096]{2,1,0:T(1,128)} %get-tuple-element.529) | copy-start | bytes 49156
  513.6 10.4 %collective-permute-start.13 = (bf16[16,4096]{1,0:T(8,128)(2,1)S(1)}, bf16[16,4096]{1,0:T(8,128)(2,1)S(1)}, u32[]{:S(2)}, u32[]{:S(2)}) collective-permute-start(bf16[16,4096]{1,0:T(8,128)(2,1)S(1)} %fusion.185), channel_id=1, source_target_pairs={{0,96},{32,0},{64,32},{96,64},{1,97},{33,1},{65,33},{97,65},{2,98}... | collective-permute-start | bytes 393224 | tf_op jit(solution)/shard_map/ppermute | solution.py:16
  524.9 11.1 %all-to-all-start.20 = ((bf16[4,16,4096]{2,1,0:T(8,128)(2,1)}), bf16[4,16,4096]{2,1,0:T(8,128)(2,1)}, u32[]{:S(2)}, u32[]{:S(2)}) async-start(bf16[4,16,4096]{2,1,0:T(8,128)(2,1)} %broadcast_in_dim.168), calls=%async_computation.22 | async-start | bytes 1048576 | tf_op jit(solution)/shard_map/all_to_all | solution.py:41
  542.9 12.0 %all-to-all-start.21 = ((bf16[4,16,4096]{2,1,0:T(8,128)(2,1)}), bf16[4,16,4096]{2,1,0:T(8,128)(2,1)}, u32[]{:S(2)}, u32[]{:S(2)}) async-start(bf16[4,16,4096]{2,1,0:T(8,128)(2,1)} %bitcast.318), calls=%async_computation.23 | async-start | bytes 1048576 | tf_op jit(solution)/shard_map/all_to_all | solution.py:57
  556.3 37.6 %copy-start.12 = (f32[1,1,4096]{2,1,0:T(1,128)S(1)}, f32[1,1,4096]{2,1,0:T(1,128)}, u32[]{:S(2)}) copy-start(f32[1,1,4096]{2,1,0:T(1,128)} %get-tuple-element.513) | copy-start | bytes 49156
  556.5 6.0 collective-permute-start.14
  563.3 11.1 %all-to-all-start.22 = ((bf16[4,16,4096]{2,1,0:T(8,128)(2,1)}), bf16[4,16,4096]{2,1,0:T(8,128)(2,1)}, u32[]{:S(2)}, u32[]{:S(2)}) async-start(bf16[4,16,4096]{2,1,0:T(8,128)(2,1)} %broadcast_in_dim.170), calls=%async_computation.24 | async-start | bytes 1048576 | tf_op jit(solution)/shard_map/all_to_all | solution.py:41
  581.6 11.1 %all-to-all-start.23 = ((bf16[4,16,4096]{2,1,0:T(8,128)(2,1)}), bf16[4,16,4096]{2,1,0:T(8,128)(2,1)}, u32[]{:S(2)}, u32[]{:S(2)}) async-start(bf16[4,16,4096]{2,1,0:T(8,128)(2,1)} %bitcast.319), calls=%async_computation.25 | async-start | bytes 1048576 | tf_op jit(solution)/shard_map/all_to_all | solution.py:57
  594.2 6.0 collective-permute-start.15
  601.0 10.4 %all-to-all-start.24 = ((bf16[4,16,4096]{2,1,0:T(8,128)(2,1)}), bf16[4,16,4096]{2,1,0:T(8,128)(2,1)S(1)}, u32[]{:S(2)}, u32[]{:S(2)}) async-start(bf16[4,16,4096]{2,1,0:T(8,128)(2,1)} %broadcast_in_dim.172), calls=%async_computation.26 | async-start | bytes 1048576 | tf_op jit(solution)/shard_map/all_to_all | solution.py:41
  604.5 189.0 %reduce-scatter.8.cloned.1.call-start = ((), (), s32[]{:S(2)}) async-start(), calls=%async_computation.30 | async-start | bytes 18874368 | tf_op jit(solution)/shard_map/reduce_scatter | solution.py:195
  623.3 228.4 %reduce-scatter.6.cloned.1.call-start = ((), (), s32[]{:S(2)}) async-start(), calls=%async_computation.29 | async-start | bytes 6291456 | tf_op jit(solution)/shard_map/reduce_scatter | solution.py:24
Sparse Core Ops, SparseCore 0:
  311.6 150.7 reduce-scatter.3
  623.4 170.0 reduce-scatter.7
  796.0 55.5 reduce-scatter.5
where the time goes:
time: 875 us; the launch traced here: 864 us
  waiting for transfers between devices  431 us (49%)
  starting transfers between devices  148 us (17%)
  blocking collectives  126 us (14%)
  matrix products  59.3 us (7%)
  local copies, waits for them, and re-layouts  53.1 us (6%)
  other arithmetic  29.8 us (3%)
  between operations  16.2 us (2%)
    reduce_scatter x1, waiting for transfers between devices, body(): lax.psum_scatter(gram_rows(grad_tokens, own_rows * lax.axis_size(DP)).ast...  170 us
    all_gather x9, blocking collectives, body(): gathered = lax.all_gather(normed, 'tensor', axis=0, tiled=True)  104 us
    ppermute x16, waiting for transfers between devices, passed_along(): lax.ppermute(array, axis, [(i, (i + by) % peers) for i in range(peers)])  71.8 us
    all_to_all x9, waiting for transfers between devices, from_everyone(): return lax.all_to_all(copies, axis, split_axis=0, concat_axis=0, tiled=True)  61.6 us
    ppermute x16, starting transfers between devices, passed_along(): lax.ppermute(array, axis, [(i, (i + by) % peers) for i in range(peers)])  61.6 us
    all_to_all x8, waiting for transfers between devices, sum_at_owner(): tiles = lax.all_to_all(in_blocks(array, dim, peers), axis, 0, 0, tiled=True)  55.3 us
    reduce_scatter x2, waiting for transfers between devices, sum_in_order(): tiles = lax.psum_scatter(tiles, axes[k], scatter_dimension=0, tiled=True)  53.1 us
    all_to_all x9, starting transfers between devices, from_everyone(): return lax.all_to_all(copies, axis, split_axis=0, concat_axis=0, tiled=True)  36.6 us
  transfers between devices with their start and end apart: 41, of which 40 were waited for; matrix products, arithmetic and copies ran while one was open for 9% of the time, Pallas kernels for 0%

commit v1 on v0

v1 whole, which is shorter than its diff:
```python
import functools

import jax
import jax.numpy as jnp
from jax import lax
from jax.experimental import pallas as pl
from jax.experimental.pallas import tpu as pltpu
from jax.sharding import Mesh
from jax.sharding import PartitionSpec as P

DP = ("dp_0", "dp_1")
TENSOR_DP = ("tensor", "dp_0", "dp_1")
AXES = ("pipe", "tensor", "dp_0", "dp_1")
SIZES = (4, 4, 2, 4)
EPSILON = 1e-05
PIPES = 4
LAYERS = 8
STREAMS = 2
LAST = LAYERS - 1
F32 = jnp.float32
BF16 = jnp.bfloat16
ANYWHERE = pl.BlockSpec(memory_space=pl.ANY)


def flat(place):
    index = 0
    for size, at in zip(SIZES, place):
        index = index * size + at
    return index


def permuted(array, target):
    pairs = []
    for pipe in range(SIZES[0]):
        for tensor in range(SIZES[1]):
            for z in range(SIZES[2]):
                for y in range(SIZES[3]):
                    there = target(pipe, tensor, z, y)
                    if there is not None:
                        pairs.append((flat((pipe, tensor, z, y)), flat(there)))
    return lax.ppermute(array, AXES, pairs)


def forward_moves(tick):
    moves = {}
    for stream in range(STREAMS):
        layer = tick - stream
        if 0 <= layer < LAST:
            source = layer % PIPES
            moves[source] = ((layer + 1) % PIPES, source % 2)
    return moves


def backward_moves(tick):
    moves = {}
    for stream in range(STREAMS):
        layer = 2 * LAST + stream - tick
        if 1 <= layer <= LAST:
            source = layer % PIPES
            moves[source] = ((layer - 1) % PIPES, 1 - source % 2)
    return moves


def fan_out(arrays, moves):
    received = []
    for step, array in enumerate(arrays):

        def target(pipe, tensor, z, y, step=step):
            if pipe not in moves:
                return None
            there, flip = moves[pipe]
            return (there, (tensor + step) % SIZES[1], z ^ flip, y)

        received.append(permuted(array, target))
    return received


def forward_place(tick, pipe):
    stream = lax.rem(tick - pipe + PIPES, PIPES)
    layer = tick - stream
    active = (stream < STREAMS) & (layer >= 0) & (layer < LAYERS)
    slot = jnp.where(active & (layer >= PIPES), 1, 0)
    return active, slot, jnp.where(active, stream, 0), active & (layer < LAST)


def backward_place(tick, pipe):
    stream = lax.rem(pipe + tick + 2 * PIPES - 2 * LAST % PIPES, PIPES)
    layer = 2 * LAST + stream - tick
    active = (stream < STREAMS) & (layer >= 0) & (layer < LAYERS)
    slot = jnp.where(active & (layer >= PIPES), 1, 0)
    return active, slot, jnp.where(active, stream, 0), active & (layer > 0)


def turned(index, count=4):
    return lax.rem(index + count, count)


def ingest(meta, arrays):
    rows, features = arrays[0].shape
    half = rows // 2
    quarter = features // 4

    def kernel(meta_ref, *refs):
        sources, (hidden_ref, cotangent_ref) = refs[:4], refs[4:]
        tensor = meta_ref[1]
        for step in range(4):
            row = pl.multiple_of(turned(tensor - step) * half, half)
            for stream in range(2):
                for turn in range(4):
                    column = pl.multiple_of(turned(tensor - turn) * quarter, quarter)
                    piece = sources[step][stream * half : (stream + 1) * half, pl.ds(column, quarter)]
                    hidden_ref[stream, turn, pl.ds(row, half), :] = piece
                    if turn == 0:
                        cotangent_ref[stream, pl.ds(row, half), :] = piece.astype(F32)

    whole = pl.BlockSpec(memory_space=pltpu.VMEM)
    return pl.pallas_call(
        kernel,
        in_specs=[pl.BlockSpec(memory_space=pltpu.SMEM)] + [whole] * 4,
        out_specs=[whole, whole],
        out_shape=[
            jax.ShapeDtypeStruct((2, 4, 4 * half, quarter), BF16),
            jax.ShapeDtypeStruct((2, 4 * half, quarter), F32),
        ],
        name="ingest",
    )(meta, *arrays)


def forward_step(tick, meta, blocks, gains, weights, hidden_stash, normed_stash):
    rows, quarter = blocks[0].shape
    features = 4 * quarter

    def kernel(meta_ref, b0, b1, b2, b3, gain_ref, weight_ref, *refs):
        next_ref, hidden_ref, normed_ref, normed, total = refs[-5:]
        turn = pl.program_id(0)
        tensor = meta_ref[1]
        active, slot, _, multiplies = forward_place(tick, meta_ref[0])
        ins = (b0, b1, b2, b3)

        @pl.when(active & (turn == 0))
        def _():
            squares = 0.0
            for ref in ins:
                wide = ref[...].astype(F32)
                squares = squares + jnp.sum(wide * wide, axis=-1, keepdims=True)
            scale = lax.rsqrt(squares * (1.0 / features) + EPSILON)
            for k, ref in enumerate(ins):
                gain = gain_ref[slot, pl.ds(turned(tensor - k), 1), :]
                normed[k] = (ref[...].astype(F32) * scale * gain).astype(BF16)
                hidden_ref[0, k] = ref[...]
            normed_ref[0] = normed[0]

        @pl.when(multiplies)
        def _():
            part = jnp.dot(normed[turn], weight_ref[0], preferred_element_type=F32)

            @pl.when(turn == 0)
            def _():
                total[...] = part

            @pl.when(turn > 0)
            def _():
                total[...] += part

        @pl.when(multiplies & (turn == 3))
        def _():
            rounded = total[...].astype(BF16).astype(F32)
            next_ref[...] = (b0[...].astype(F32) + rounded).astype(BF16)

    def weight_at(turn, meta_ref):
        _, slot, _, multiplies = forward_place(tick, meta_ref[0])
        return slot, jnp.where(multiplies, turned(meta_ref[1] - turn), 0), 0

    def stash_at(turn, meta_ref):
        active, slot, stream, _ = forward_place(tick, meta_ref[0])
        return jnp.where(active, slot * 2 + stream, 4)

    block = pl.BlockSpec((rows, quarter), lambda turn, meta_ref: (0, 0))
    stashes = [] if hidden_stash is None else [hidden_stash, normed_stash]
    return pl.pallas_call(
        kernel,
        grid_spec=pltpu.PrefetchScalarGridSpec(
            num_scalar_prefetch=1,
            grid=(4,),
            in_specs=[block] * 4
            + [
                pl.BlockSpec((2, 4, quarter), lambda turn, meta_ref: (0, 0, 0)),
                pl.BlockSpec((1, quarter, quarter), weight_at),
            ]
            + [ANYWHERE] * len(stashes),
            out_specs=[
                block,
                pl.BlockSpec((1, 4, rows, quarter), lambda turn, m: (stash_at(turn, m), 0, 0, 0)),
                pl.BlockSpec((1, rows, quarter), lambda turn, m: (stash_at(turn, m), 0, 0)),
            ],
            scratch_shapes=[pltpu.VMEM((4, rows, quarter), BF16), pltpu.VMEM((rows, quarter), F32)],
        ),
        out_shape=[
            jax.ShapeDtypeStruct((rows, quarter), BF16),
            jax.ShapeDtypeStruct((5, 4, rows, quarter), BF16),
            jax.ShapeDtypeStruct((5, rows, quarter), BF16),
        ],
        input_output_aliases={7: 1, 8: 2} if stashes else {},
        compiler_params=pltpu.CompilerParams(vmem_limit_bytes=24 << 20),
        cost_estimate=pl.CostEstimate(
            flops=2 * rows * features * quarter, bytes_accessed=2 * features * quarter, transcendentals=0
        ),
        name="forward_step",
    )(meta, *blocks, gains, weights, *stashes)


def backward_step(tick, meta, own, others, gains, weights, hidden_stash, grad_stash):
    rows, quarter = own.shape
    features = 4 * quarter

    def kernel(meta_ref, own_ref, c1, c2, c3, gain_ref, weight_ref, hidden_ref, *refs):
        own_out, o1, o2, o3, grad_ref, delta, scaled, inner = refs[-8:]
        turn = pl.program_id(0)
        tensor = meta_ref[1]
        active, slot, _, multiplies = backward_place(tick, meta_ref[0])

        @pl.when(active & (turn == 0))
        def _():
            total = own_ref[...]
            for ref in (c1, c2, c3):
                total = total + ref[...].astype(F32)
            delta[...] = total.astype(BF16)
            grad_ref[0] = total.astype(BF16)

        @pl.when(multiplies)
        def _():
            part = lax.dot_general(
                delta[...], weight_ref[0], (((1,), (1,)), ((), ())), preferred_element_type=F32
            )
            gain = gain_ref[slot, pl.ds(turned(tensor + turn), 1), :]
            back = part.astype(BF16).astype(F32) * gain
            scaled[turn] = back
            hidden = hidden_ref[0, turned(-turn)].astype(F32)
            sums = jnp.broadcast_to(jnp.sum(hidden * back, axis=-1, keepdims=True), inner.shape)

            @pl.when(turn == 0)
            def _():
                inner[...] = sums

            @pl.when(turn > 0)
            def _():
                inner[...] += sums

        @pl.when(multiplies & (turn == 3))
        def _():
            squares = 0.0
            for k in range(4):
                wide = hidden_ref[0, k].astype(F32)
                squares = squares + jnp.sum(wide * wide, axis=-1, keepdims=True)
            scale = lax.rsqrt(squares * (1.0 / features) + EPSILON)
            slope = scale * scale * scale * (inner[:, :1] * (1.0 / features))
            for k, ref in enumerate((own_out, o1, o2, o3)):
                change = scale * scaled[k] - slope * hidden_ref[0, (4 - k) % 4].astype(F32)
                if k == 0:
                    ref[...] = delta[...].astype(F32) + change
                else:
                    ref[...] = change.astype(BF16)

    def weight_at(turn, meta_ref):
        _, slot, _, multiplies = backward_place(tick, meta_ref[0])
        return slot, jnp.where(multiplies, turned(meta_ref[1] + turn), 0), 0

    def stash_at(turn, meta_ref, idle):
        active, slot, stream, _ = backward_place(tick, meta_ref[0])
        return jnp.where(active, slot * 2 + stream, idle)

    block = pl.BlockSpec((rows, quarter), lambda turn, meta_ref: (0, 0))
    stashes = [] if grad_stash is None else [grad_stash]
    return pl.pallas_call(
        kernel,
        grid_spec=pltpu.PrefetchScalarGridSpec(
            num_scalar_prefetch=1,
            grid=(4,),
            in_specs=[block] * 4
            + [
                pl.BlockSpec((2, 4, quarter), lambda turn, meta_ref: (0, 0, 0)),
                pl.BlockSpec((1, quarter, quarter), weight_at),
                pl.BlockSpec((1, 4, rows, quarter), lambda turn, m: (stash_at(turn, m, 0), 0, 0, 0)),
            ]
            + [ANYWHERE] * len(stashes),
            out_specs=[block] * 4
            + [pl.BlockSpec((1, rows, quarter), lambda turn, m: (stash_at(turn, m, 4), 0, 0))],
            scratch_shapes=[
                pltpu.VMEM((rows, quarter), BF16),
                pltpu.VMEM((4, rows, quarter), F32),
                pltpu.VMEM((rows, 128), F32),
            ],
        ),
        out_shape=[jax.ShapeDtypeStruct((rows, quarter), F32)]
        + [jax.ShapeDtypeStruct((rows, quarter), BF16)] * 3
        + [jax.ShapeDtypeStruct((5, rows, quarter), BF16)],
        input_output_aliases={8: 4} if stashes else {},
        compiler_params=pltpu.CompilerParams(vmem_limit_bytes=24 << 20),
        cost_estimate=pl.CostEstimate(
            flops=2 * rows * features * quarter, bytes_accessed=2 * features * quarter, transcendentals=0
        ),
        name="backward_step",
    )(meta, own, *others, gains, weights, hidden_stash, *stashes)


def gram(meta, tokens, picked, inv_tokens):
    slots, count, quarter = tokens.shape
    own = picked.shape[-1]

    def kernel(meta_ref, tokens_ref, picked_ref, *outs):
        for step, out in enumerate(outs):
            left = picked_ref[0, turned(meta_ref[1] + step)]
            product = lax.dot_general(
                left, tokens_ref[0], (((0,), (0,)), ((), ())), preferred_element_type=F32
            )
            out[0] = (product * inv_tokens).astype(BF16)

    return pl.pallas_call(
        kernel,
        grid_spec=pltpu.PrefetchScalarGridSpec(
            num_scalar_prefetch=1,
            grid=(slots,),
            in_specs=[
                pl.BlockSpec((1, count, quarter), lambda s, m: (s, 0, 0)),
                pl.BlockSpec((1, 4, count, own), lambda s, m: (s, 0, 0, 0)),
            ],
            out_specs=[pl.BlockSpec((1, own, quarter), lambda s, m: (s, 0, 0))] * 4,
        ),
        out_shape=[jax.ShapeDtypeStruct((slots, own, quarter), BF16)] * 4,
        compiler_params=pltpu.CompilerParams(vmem_limit_bytes=32 << 20),
        cost_estimate=pl.CostEstimate(
            flops=2 * slots * count * 4 * own * quarter,
            bytes_accessed=2 * slots * (count * quarter + 8 * own * quarter),
            transcendentals=0,
        ),
        name="gram",
    )(meta, tokens, picked)


def share_columns(blocks):
    return [blocks[0]] + [
        permuted(block, lambda p, t, z, y, k=k: (p, (t + k) % SIZES[1], z, y))
        for k, block in enumerate(blocks)
        if k
    ]


def assemble(meta, first, second):
    own, quarter = first[0].shape

    def kernel(meta_ref, *refs):
        out = refs[8]
        tensor = meta_ref[1]
        for step in range(4):
            column = pl.multiple_of(turned(tensor - step) * quarter, quarter)
            out[:, :, pl.ds(column, quarter)] = jnp.stack([refs[step][...], refs[4 + step][...]], 1)

    whole = pl.BlockSpec(memory_space=pltpu.VMEM)
    return pl.pallas_call(
        kernel,
        in_specs=[pl.BlockSpec(memory_space=pltpu.SMEM)] + [whole] * 8,
        out_specs=whole,
        out_shape=jax.ShapeDtypeStruct((own, 2, 4 * quarter), BF16),
        compiler_params=pltpu.CompilerParams(vmem_limit_bytes=32 << 20),
        name="assemble",
    )(meta, *first, *second)


def body(inputs, weights, norm_gains, cotangent):
    micro_count, shard_rows, features = inputs.shape
    quarter = weights.shape[3]
    pipe = lax.axis_index("pipe")
    tensor = lax.axis_index("tensor")
    group = lax.axis_index(DP)
    own_rows = quarter // lax.axis_size(DP)
    inv_tokens = 1.0 / (micro_count * shard_rows * lax.axis_size(TENSOR_DP))
    meta = jnp.stack([pipe, tensor]).astype(jnp.int32)
    weights = weights.reshape(weights.shape[0], features, quarter)
    gains = norm_gains.reshape(norm_gains.shape[0], 4, quarter)

    def start_target(step):
        def target(p, t, z, y):
            if p == 0 and step:
                return (p, (t + step) % SIZES[1], z, y)
            if p == LAST % PIPES:
                return (p, (t + step) % SIZES[1], 1 - z, y)
            return None

        return target

    given = jnp.where(pipe == LAST % PIPES, cotangent, inputs).reshape(-1, features)
    arrived = [permuted(given, start_target(step)) for step in range(4)]
    arrived[0] = jnp.where(pipe == 0, given, arrived[0])
    first_blocks, last_deltas = ingest(meta, arrived)

    def gather_group(rows):
        return lax.all_gather(rows, DP, axis=0, tiled=True)

    def pick(tokens):
        mine = lax.dynamic_slice_in_dim(tokens, group * own_rows, own_rows, 1)
        return lax.all_gather(mine, "tensor", axis=0, tiled=False)

    def factor_blocks(tokens_list):
        tokens = jnp.stack(tokens_list)
        picked = jnp.stack([pick(one) for one in tokens_list])
        return share_columns(gram(meta, tokens, picked, inv_tokens))

    hidden_stash = normed_stash = grad_stash = None
    zeros = jnp.zeros(first_blocks.shape[2:], BF16)
    received = [first_blocks[0, k] for k in range(4)]
    back = [jnp.zeros(first_blocks.shape[2:], F32), zeros, zeros, zeros]
    act_tokens = []
    for tick in range(2 * LAST + STREAMS):
        if tick <= LAST + 1:
            blocks = received
            if 0 < tick < STREAMS:
                blocks = [jnp.where(pipe == 0, first_blocks[tick, k], received[k]) for k in range(4)]
            following, hidden_stash, normed_stash = forward_step(
                tick, meta, blocks, gains, weights, hidden_stash, normed_stash
            )
            if tick <= LAST:
                received = fan_out([following] * 4, forward_moves(tick))
            if tick == PIPES:
                act_tokens.append(gather_group(normed_stash[:2].reshape(-1, quarter)))
            if tick == 2 * PIPES:
                act_tokens.append(gather_group(normed_stash[2:4].reshape(-1, quarter)))
        if tick >= LAST:
            own = back[0]
            if tick < LAST + STREAMS:
                own = jnp.where(pipe == LAST % PIPES, last_deltas[tick - LAST], own)
            *sent, grad_stash = backward_step(
                tick, meta, own, back[1:], gains, weights, hidden_stash, grad_stash
            )
            if tick < 2 * LAST + STREAMS - 1:
                back = fan_out(sent, backward_moves(tick))
            if tick == LAST + PIPES:
                late_tokens = gather_group(grad_stash[2:4].reshape(-1, quarter))
    act_blocks = factor_blocks(act_tokens)
    act_factor = assemble(meta, [b[0] for b in act_blocks], [b[1] for b in act_blocks])
    late = factor_blocks([late_tokens])
    early = factor_blocks([gather_group(grad_stash[:2].reshape(-1, quarter))])
    grad_factor = assemble(meta, [b[0] for b in early], [b[0] for b in late])
    shape = (own_rows, 2, 1, features)
    return (act_factor.reshape(shape), grad_factor.reshape(shape))


def solution(mesh):
    split = Mesh(mesh.devices.reshape(SIZES), AXES)
    placed = (
        P(None, TENSOR_DP, None),
        P(None, "pipe", None, "tensor"),
        P(None, "pipe", None),
        P(None, TENSOR_DP, None),
    )
    return jax.shard_map(
        body,
        mesh=split,
        in_specs=placed,
        out_specs=(P(TENSOR_DP, None, "pipe", None), P(TENSOR_DP, None, "pipe", None)),
        check_vma=False,
    )
```

time: 875 us -> 669 us (0.76); the launches traced: 864 us -> 667 us
  waiting for transfers between devices: 431 us -> 207 us
  starting transfers between devices: 148 us -> 328 us
  blocking collectives: 126 us -> 0 us
  matrix products: 59.3 us -> 0 us
  Pallas kernels: 0 us -> 57.9 us
  other arithmetic: 29.8 us -> 10.2 us
    ppermute x16 -> x77, starting transfers between devices: 61.6 us -> 328 us  [permuted(): return lax.ppermute(array, AXES, pairs)]
    reduce_scatter x3 -> x0, waiting for transfers between devices: 223 us -> none  [the longest x1 170 us: body(): lax.psum_scatter(gram_rows(grad_tokens, own_rows * lax.axis_size(DP)).ast...]
    all_to_all x22 -> x0, waiting for transfers between devices: 136 us -> none  [the longest x9 61.6 us: from_everyone(): return lax.all_to_all(copies, axis, split_axis=0, concat_axis=0, tiled=True)]
    all_gather x9 -> x0, blocking collectives: 104 us -> none  [body(): gathered = lax.all_gather(normed, 'tensor', axis=0, tiled=True)]
    all_gather x0 -> x8, waiting for transfers between devices: none -> 102 us  [the longest x4 71.2 us: pick(): return lax.all_gather(mine, 'tensor', axis=0, tiled=False)]
    all_to_all x22 -> x0, starting transfers between devices: 85.9 us -> none  [the longest x9 36.6 us: from_everyone(): return lax.all_to_all(copies, axis, split_axis=0, concat_axis=0, tiled=True)]
    dot_general x12 -> x0, matrix products: 59.3 us -> none  [the longest x4 27.9 us: partial_rows(): lax.dot_general(piece, weight, (((1,), (1,)), ((), ())), preferred_elemen...]
    pallas_call x0 -> x24, Pallas kernels: none -> 57.9 us  [the longest x9 22.4 us: backward_step(): pl.pallas_call(kernel, grid_spec=pltpu.PrefetchScalarGridSpec(num_scalar_...]
  transfers between devices with their start and end apart: 41 -> 85, of which waited for: 40 -> 33; matrix products, arithmetic and copies ran while one was open for 9% -> 3% of each run, Pallas kernels for 0% -> 6%
where the time goes in v1:
time: 669 us; the launch traced here: 667 us
  starting transfers between devices  328 us (49%)
  waiting for transfers between devices  207 us (31%)
  Pallas kernels  57.9 us (9%)
  local copies, waits for them, and re-layouts  48.5 us (7%)
  between operations  15.2 us (2%)
  other arithmetic  10.2 us (2%)
    ppermute x77, starting transfers between devices, permuted(): return lax.ppermute(array, AXES, pairs)  328 us
    ppermute x77, waiting for transfers between devices, permuted(): return lax.ppermute(array, AXES, pairs)  105 us
    all_gather x4, waiting for transfers between devices, pick(): return lax.all_gather(mine, 'tensor', axis=0, tiled=False)  71.2 us
    unnamed x50, local copies, waits for them, and re-layouts  34.2 us
    all_gather x4, waiting for transfers between devices, gather_group(): return lax.all_gather(rows, DP, axis=0, tiled=True)  30.9 us
    pallas_call x9, Pallas kernels, backward_step(): pl.pallas_call(kernel, grid_spec=pltpu.PrefetchScalarGridSpec(num_scalar_...  22.4 us
    pallas_call x9, Pallas kernels, forward_step(): pl.pallas_call(kernel, grid_spec=pltpu.PrefetchScalarGridSpec(num_scalar_...  16.1 us
  transfers between devices with their start and end apart: 85, of which 33 were waited for; matrix products, arithmetic and copies ran while one was open for 3% of the time, Pallas kernels for 6%

profile of v1, /device:TPU:1, one launch (start us, length us, event | category | flops | bytes accessed | tf_op | source)
XLA Modules:
  0.0 666.9 jit_solution(1301238872256638400)
XLA Ops:
  9.6 15.3 %collective-permute-start.2 = (bf16[32,4096]{1,0:T(8,128)(2,1)S(1)}, bf16[32,4096]{1,0:T(8,128)(2,1)S(1)}, u32[]{:S(2)}, u32[]{:S(2)}) collective-permute-start(bf16[32,4096]{1,0:T(8,128)(2,1)S(1)} %bitcast.109), channel_id=1, source_target_pairs={{0,16},{1,17},{2,18},{3,19},{4,20},{5,21},{6,22},{7,23},{8,24},{9,... | collective-permute-start | bytes 786440 | tf_op jit(solution)/shard_map/ppermute | solution.py:41
  24.9 9.9 %collective-permute-start.3 = (bf16[32,4096]{1,0:T(8,128)(2,1)S(1)}, bf16[32,4096]{1,0:T(8,128)(2,1)S(1)}, u32[]{:S(2)}, u32[]{:S(2)}) collective-permute-start(bf16[32,4096]{1,0:T(8,128)(2,1)S(1)} %bitcast.110), channel_id=1, source_target_pairs={{0,24},{1,25},{2,26},{3,27},{4,28},{5,29},{6,30},{7,31},{8,0},{9,1... | collective-permute-start | bytes 786440 | tf_op jit(solution)/shard_map/ppermute | solution.py:41
  38.6 2.5 ingest.1
  42.3 5.8 copy-done
  54.7 2.6 collective-permute-done.4
  57.3 5.0 collective-permute-done.5
  64.4 3.0 forward_step.10
  75.2 2.5 collective-permute-done.11.b3
  77.7 3.6 collective-permute-done.9.b1
  81.3 3.0 forward_step.11
  84.3 4.0 collective-permute-start.12
  89.7 2.9 collective-permute-start.14
  96.5 11.6 %collective-permute-start.16 = (bf16[64,1024]{1,0:T(8,128)(2,1)S(1)}, bf16[64,1024]{1,0:T(8,128)(2,1)S(1)}, u32[]{:S(2)}, u32[]{:S(2)}) collective-permute-start(bf16[64,1024]{1,0:T(8,128)(2,1)S(1)} %get-tuple-element.93), channel_id=1, source_target_pairs={{64,96},{65,97},{66,98},{67,99},{68,100},{69,101},{70,102},{71,103... | collective-permute-start | bytes 393224 | tf_op jit(solution)/shard_map/ppermute | solution.py:41
  108.1 10.2 %collective-permute-start.17 = (bf16[64,1024]{1,0:T(8,128)(2,1)S(1)}, bf16[64,1024]{1,0:T(8,128)(2,1)S(1)}, u32[]{:S(2)}, u32[]{:S(2)}) collective-permute-start(bf16[64,1024]{1,0:T(8,128)(2,1)S(1)} %get-tuple-element.93), channel_id=1, source_target_pairs={{64,104},{65,105},{66,106},{67,107},{68,108},{69,109},{70,110},{71... | collective-permute-start | bytes 393224 | tf_op jit(solution)/shard_map/ppermute | solution.py:41
  118.3 10.2 %collective-permute-start.18 = (bf16[64,1024]{1,0:T(8,128)(2,1)S(1)}, bf16[64,1024]{1,0:T(8,128)(2,1)S(1)}, u32[]{:S(2)}, u32[]{:S(2)}) collective-permute-start(bf16[64,1024]{1,0:T(8,128)(2,1)S(1)} %get-tuple-element.93), channel_id=1, source_target_pairs={{64,112},{65,113},{66,114},{67,115},{68,116},{69,117},{70,118},{71... | collective-permute-start | bytes 393224 | tf_op jit(solution)/shard_map/ppermute | solution.py:41
  128.5 10.2 %collective-permute-start.19 = (bf16[64,1024]{1,0:T(8,128)(2,1)S(1)}, bf16[64,1024]{1,0:T(8,128)(2,1)S(1)}, u32[]{:S(2)}, u32[]{:S(2)}) collective-permute-start(bf16[64,1024]{1,0:T(8,128)(2,1)S(1)} %get-tuple-element.93), channel_id=1, source_target_pairs={{64,120},{65,121},{66,122},{67,123},{68,124},{69,125},{70,126},{71... | collective-permute-start | bytes 393224 | tf_op jit(solution)/shard_map/ppermute | solution.py:41
  140.2 16.9 %collective-permute-start.20 = (bf16[64,1024]{1,0:T(8,128)(2,1)S(1)}, bf16[64,1024]{1,0:T(8,128)(2,1)S(1)}, u32[]{:S(2)}, u32[]{:S(2)}) collective-permute-start(bf16[64,1024]{1,0:T(8,128)(2,1)S(1)} %get-tuple-element.97), channel_id=1, source_target_pairs={{0,32},{1,33},{2,34},{3,35},{4,36},{5,37},{6,38},{7,39},{8,40},{9,... | collective-permute-start | bytes 393224 | tf_op jit(solution)/shard_map/ppermute | solution.py:41
  157.1 9.9 %collective-permute-start.21 = (bf16[64,1024]{1,0:T(8,128)(2,1)S(1)}, bf16[64,1024]{1,0:T(8,128)(2,1)S(1)}, u32[]{:S(2)}, u32[]{:S(2)}) collective-permute-start(bf16[64,1024]{1,0:T(8,128)(2,1)S(1)} %get-tuple-element.97), channel_id=1, source_target_pairs={{0,40},{1,41},{2,42},{3,43},{4,44},{5,45},{6,46},{7,47},{8,48},{9,... | collective-permute-start | bytes 393224 | tf_op jit(solution)/shard_map/ppermute | solution.py:41
  167.1 9.9 %collective-permute-start.22 = (bf16[64,1024]{1,0:T(8,128)(2,1)S(1)}, bf16[64,1024]{1,0:T(8,128)(2,1)S(1)}, u32[]{:S(2)}, u32[]{:S(2)}) collective-permute-start(bf16[64,1024]{1,0:T(8,128)(2,1)S(1)} %get-tuple-element.97), channel_id=1, source_target_pairs={{0,48},{1,49},{2,50},{3,51},{4,52},{5,53},{6,54},{7,55},{8,56},{9,... | collective-permute-start | bytes 393224 | tf_op jit(solution)/shard_map/ppermute | solution.py:41
  177.0 9.9 %collective-permute-start.23 = (bf16[64,1024]{1,0:T(8,128)(2,1)S(1)}, bf16[64,1024]{1,0:T(8,128)(2,1)S(1)}, u32[]{:S(2)}, u32[]{:S(2)}) collective-permute-start(bf16[64,1024]{1,0:T(8,128)(2,1)S(1)} %get-tuple-element.97), channel_id=1, source_target_pairs={{0,56},{1,57},{2,58},{3,59},{4,60},{5,61},{6,62},{7,63},{8,32},{9,... | collective-permute-start | bytes 393224 | tf_op jit(solution)/shard_map/ppermute | solution.py:41
  187.0 4.9 collective-permute-done.23.b3
  191.9 5.8 copy-done.2
  197.6 3.0 forward_step.14
  210.6 3.3 collective-permute-done.26.b2
  214.6 3.0 forward_step.15
  217.6 3.6 collective-permute-start.28
  221.2 2.7 collective-permute-start.29
  223.8 2.4 collective-permute-start.30
  241.9 5.8 copy-done.3
  253.6 29.4 %collective-permute-done.44.c1 = bf16[64,1024]{1,0:T(8,128)(2,1)S(1)} collective-permute-done((bf16[64,1024]{1,0:T(8,128)(2,1)S(1)}, bf16[64,1024]{1,0:T(8,128)(2,1)S(1)}, u32[]{:S(2)}, u32[]{:S(2)}) %collective-permute-start.44) | collective-permute-done | bytes 131104 | tf_op jit(solution)/shard_map/ppermute | solution.py:41
  283.3 4.5 backward_step.11
  295.5 3.8 collective-permute-done.48.c1
  299.3 2.6 collective-permute-done.49.c2
  303.0 4.5 backward_step.12
  307.5 7.5 %collective-permute-start.51 = (f32[64,1024]{1,0:T(8,128)S(1)}, f32[64,1024]{1,0:T(8,128)S(1)}, u32[]{:S(2)}, u32[]{:S(2)}) collective-permute-start(f32[64,1024]{1,0:T(8,128)S(1)} %get-tuple-element.130), channel_id=1, source_target_pairs={{0,100},{1,101},{2,102},{3,103},{4,96},{5,97},{6,98},{7,99},{8,108... | collective-permute-start | bytes 786440 | tf_op jit(solution)/shard_map/ppermute | solution.py:41
  315.0 9.5 %collective-permute-start.52 = (bf16[64,1024]{1,0:T(8,128)(2,1)S(1)}, bf16[64,1024]{1,0:T(8,128)(2,1)S(1)}, u32[]{:S(2)}, u32[]{:S(2)}) collective-permute-start(bf16[64,1024]{1,0:T(8,128)(2,1)S(1)} %get-tuple-element.131), channel_id=1, source_target_pairs={{0,108},{1,109},{2,110},{3,111},{4,104},{5,105},{6,106},{7,107},{8... | collective-permute-start | bytes 393224 | tf_op jit(solution)/shard_map/ppermute | solution.py:41
  324.6 9.5 %collective-permute-start.53 = (bf16[64,1024]{1,0:T(8,128)(2,1)S(1)}, bf16[64,1024]{1,0:T(8,128)(2,1)S(1)}, u32[]{:S(2)}, u32[]{:S(2)}) collective-permute-start(bf16[64,1024]{1,0:T(8,128)(2,1)S(1)} %get-tuple-element.132), channel_id=1, source_target_pairs={{0,116},{1,117},{2,118},{3,119},{4,112},{5,113},{6,114},{7,115},{8... | collective-permute-start | bytes 393224 | tf_op jit(solution)/shard_map/ppermute | solution.py:41
  334.1 9.5 %collective-permute-start.54 = (bf16[64,1024]{1,0:T(8,128)(2,1)S(1)}, bf16[64,1024]{1,0:T(8,128)(2,1)S(1)}, u32[]{:S(2)}, u32[]{:S(2)}) collective-permute-start(bf16[64,1024]{1,0:T(8,128)(2,1)S(1)} %get-tuple-element.133), channel_id=1, source_target_pairs={{0,124},{1,125},{2,126},{3,127},{4,120},{5,121},{6,122},{7,123},{8... | collective-permute-start | bytes 393224 | tf_op jit(solution)/shard_map/ppermute | solution.py:41
  349.4 15.3 %collective-permute-start.55 = (f32[64,1024]{1,0:T(8,128)}, f32[64,1024]{1,0:T(8,128)S(1)}, u32[]{:S(2)}, u32[]{:S(2)}) collective-permute-start(f32[64,1024]{1,0:T(8,128)} %copy-done.14), channel_id=1, source_target_pairs={{0,100},{1,101},{2,102},{3,103},{4,96},{5,97},{6,98},{7,99},{8,108... | collective-permute-start | bytes 786440 | tf_op jit(solution)/shard_map/ppermute | solution.py:41
  364.7 9.9 %collective-permute-start.56 = (bf16[64,1024]{1,0:T(8,128)(2,1)}, bf16[64,1024]{1,0:T(8,128)(2,1)S(1)}, u32[]{:S(2)}, u32[]{:S(2)}) collective-permute-start(bf16[64,1024]{1,0:T(8,128)(2,1)} %copy-done.18), channel_id=1, source_target_pairs={{0,108},{1,109},{2,110},{3,111},{4,104},{5,105},{6,106},{7,107},{8... | collective-permute-start | bytes 393224 | tf_op jit(solution)/shard_map/ppermute | solution.py:41
  374.6 9.9 %collective-permute-start.57 = (bf16[64,1024]{1,0:T(8,128)(2,1)}, bf16[64,1024]{1,0:T(8,128)(2,1)S(1)}, u32[]{:S(2)}, u32[]{:S(2)}) collective-permute-start(bf16[64,1024]{1,0:T(8,128)(2,1)} %copy-done.17), channel_id=1, source_target_pairs={{0,116},{1,117},{2,118},{3,119},{4,112},{5,113},{6,114},{7,115},{8... | collective-permute-start | bytes 393224 | tf_op jit(solution)/shard_map/ppermute | solution.py:41
  384.6 9.9 %collective-permute-start.58 = (bf16[64,1024]{1,0:T(8,128)(2,1)S(1)}, bf16[64,1024]{1,0:T(8,128)(2,1)S(1)}, u32[]{:S(2)}, u32[]{:S(2)}) collective-permute-start(bf16[64,1024]{1,0:T(8,128)(2,1)S(1)} %get-tuple-element.138), channel_id=1, source_target_pairs={{0,124},{1,125},{2,126},{3,127},{4,120},{5,121},{6,122},{7,123},{8... | collective-permute-start | bytes 393224 | tf_op jit(solution)/shard_map/ppermute | solution.py:41
  394.6 5.8 copy-done.4
  406.2 14.7 %collective-permute-done.60.c1 = bf16[64,1024]{1,0:T(8,128)(2,1)S(1)} collective-permute-done((bf16[64,1024]{1,0:T(8,128)(2,1)S(1)}, bf16[64,1024]{1,0:T(8,128)(2,1)S(1)}, u32[]{:S(2)}, u32[]{:S(2)}) %collective-permute-start.60) | collective-permute-done | bytes 131104 | tf_op jit(solution)/shard_map/ppermute | solution.py:41
  421.0 4.6 collective-permute-done.61.c2
  425.8 4.5 backward_step.15
  438.1 3.8 collective-permute-done.64.c1
  441.9 2.8 collective-permute-done.65.c2
  446.0 4.5 backward_step.16
  466.4 30.8 %all-gather.17.cloned.1.call-done = bf16[1024,1024]{1,0:T(8,128)(2,1)} async-done(((bf16[128,1024]{1,0:T(8,128)(2,1)}), bf16[1024,1024]{1,0:T(8,128)(2,1)}) %all-gather.17.cloned.1.call-update) | async-done | bytes 2097168 | tf_op jit(solution)/shard_map/all_gather | solution.py:397
  498.9 4.0 pad_maximum_fusion.tokens_ref
  502.9 23.5 %all-gather.21.cloned.1.call-done = bf16[4096,128]{1,0:T(8,128)(2,1)} async-done(((bf16[1024,128]{1,0:T(8,128)(2,1)}), bf16[4096,128]{1,0:T(8,128)(2,1)}) %all-gather.21.cloned.1.call-update) | async-done | bytes 1048592 | tf_op jit(solution)/shard_map/all_gather | solution.py:401
  526.4 26.4 %all-gather.23.cloned.1.call-done = bf16[4096,128]{1,0:T(8,128)(2,1)} async-done(((bf16[1024,128]{1,0:T(8,128)(2,1)}), bf16[4096,128]{1,0:T(8,128)(2,1)}) %all-gather.23.cloned.1.call-update) | async-done | bytes 1048592 | tf_op jit(solution)/shard_map/all_gather | solution.py:401
  555.6 3.2 gram.3
  561.1 10.0 %collective-permute-start.36 = (bf16[2,128,1024]{2,1,0:T(8,128)(2,1)S(1)}, bf16[2,128,1024]{2,1,0:T(8,128)(2,1)}, u32[]{:S(2)}, u32[]{:S(2)}) collective-permute-start(bf16[2,128,1024]{2,1,0:T(8,128)(2,1)S(1)} %get-tuple-element.110), channel_id=1, source_target_pairs={{0,8},{1,9},{2,10},{3,11},{4,12},{5,13},{6,14},{7,15},{8,16},{9,17... | collective-permute-start | bytes 1572872 | tf_op jit(solution)/shard_map/ppermute | solution.py:41
  571.1 21.3 %all-gather.27.cloned.1.call-done = bf16[4096,128]{1,0:T(8,128)(2,1)} async-done(((bf16[1024,128]{1,0:T(8,128)(2,1)}), bf16[4096,128]{1,0:T(8,128)(2,1)}) %all-gather.27.cloned.1.call-update) | async-done | bytes 1048592 | tf_op jit(solution)/shard_map/all_gather | solution.py:401
  597.5 9.5 %collective-permute-start.74 = (bf16[1,128,1024]{2,1,0:T(8,128)(2,1)}, bf16[1,128,1024]{2,1,0:T(8,128)(2,1)S(1)}, u32[]{:S(2)}, u32[]{:S(2)}) collective-permute-start(bf16[1,128,1024]{2,1,0:T(8,128)(2,1)} %get-tuple-element.161), channel_id=1, source_target_pairs={{0,8},{1,9},{2,10},{3,11},{4,12},{5,13},{6,14},{7,15},{8,16},{9,17... | collective-permute-start | bytes 786440 | tf_op jit(solution)/shard_map/ppermute | solution.py:41
  608.0 9.0 %collective-permute-start.75 = (bf16[1,128,1024]{2,1,0:T(8,128)(2,1)}, bf16[1,128,1024]{2,1,0:T(8,128)(2,1)S(1)}, u32[]{:S(2)}, u32[]{:S(2)}) collective-permute-start(bf16[1,128,1024]{2,1,0:T(8,128)(2,1)} %get-tuple-element.162), channel_id=1, source_target_pairs={{0,16},{1,17},{2,18},{3,19},{4,20},{5,21},{6,22},{7,23},{8,24},{9,... | collective-permute-start | bytes 786440 | tf_op jit(solution)/shard_map/ppermute | solution.py:41
  617.0 8.9 %collective-permute-start.76 = (bf16[1,128,1024]{2,1,0:T(8,128)(2,1)S(1)}, bf16[1,128,1024]{2,1,0:T(8,128)(2,1)S(1)}, u32[]{:S(2)}, u32[]{:S(2)}) collective-permute-start(bf16[1,128,1024]{2,1,0:T(8,128)(2,1)S(1)} %get-tuple-element.163), channel_id=1, source_target_pairs={{0,24},{1,25},{2,26},{3,27},{4,28},{5,29},{6,30},{7,31},{8,0},{9,1... | collective-permute-start | bytes 786440 | tf_op jit(solution)/shard_map/ppermute | solution.py:41
  630.6 9.8 %collective-permute-start.71 = (bf16[1,128,1024]{2,1,0:T(8,128)(2,1)S(1)}, bf16[1,128,1024]{2,1,0:T(8,128)(2,1)S(1)}, u32[]{:S(2)}, u32[]{:S(2)}) collective-permute-start(bf16[1,128,1024]{2,1,0:T(8,128)(2,1)S(1)} %get-tuple-element.157), channel_id=1, source_target_pairs={{0,8},{1,9},{2,10},{3,11},{4,12},{5,13},{6,14},{7,15},{8,16},{9,17... | collective-permute-start | bytes 786440 | tf_op jit(solution)/shard_map/ppermute | solution.py:41
  640.3 2.9 collective-permute-start.72
  646.3 4.8 assemble.2
  651.1 4.2 collective-permute-done.72
  655.2 4.8 assemble.3
  (212 shorter events, 128.6 us)
Async XLA Ops:
  7.2 453.8 %all-gather.13.cloned.1.call-start = ((), (), s32[]{:S(2)}) async-start(), calls=%async_computation | async-start | bytes 2359296 | tf_op jit(solution)/shard_map/all_gather | solution.py:397
  8.2 28.1 %collective-permute-start = (bf16[32,4096]{1,0:T(8,128)(2,1)S(1)}, bf16[32,4096]{1,0:T(8,128)(2,1)S(1)}, u32[]{:S(2)}, u32[]{:S(2)}) collective-permute-start(bf16[32,4096]{1,0:T(8,128)(2,1)S(1)} %bitcast.107), channel_id=1, source_target_pairs={{96,100},{97,101},{98,102},{99,103},{100,96},{101,97},{102,98},{10... | collective-permute-start | bytes 786440 | tf_op jit(solution)/shard_map/ppermute | solution.py:41
  8.9 28.2 %collective-permute-start.1 = (bf16[32,4096]{1,0:T(8,128)(2,1)S(1)}, bf16[32,4096]{1,0:T(8,128)(2,1)S(1)}, u32[]{:S(2)}, u32[]{:S(2)}) collective-permute-start(bf16[32,4096]{1,0:T(8,128)(2,1)S(1)} %bitcast.108), channel_id=1, source_target_pairs={{0,8},{1,9},{2,10},{3,11},{4,12},{5,13},{6,14},{7,15},{8,16},{9,17... | collective-permute-start | bytes 786440 | tf_op jit(solution)/shard_map/ppermute | solution.py:41
  9.6 27.5 %collective-permute-start.2 = (bf16[32,4096]{1,0:T(8,128)(2,1)S(1)}, bf16[32,4096]{1,0:T(8,128)(2,1)S(1)}, u32[]{:S(2)}, u32[]{:S(2)}) collective-permute-start(bf16[32,4096]{1,0:T(8,128)(2,1)S(1)} %bitcast.109), channel_id=1, source_target_pairs={{0,16},{1,17},{2,18},{3,19},{4,20},{5,21},{6,22},{7,23},{8,24},{9,... | collective-permute-start | bytes 786440 | tf_op jit(solution)/shard_map/ppermute | solution.py:41
  24.9 12.2 %collective-permute-start.3 = (bf16[32,4096]{1,0:T(8,128)(2,1)S(1)}, bf16[32,4096]{1,0:T(8,128)(2,1)S(1)}, u32[]{:S(2)}, u32[]{:S(2)}) collective-permute-start(bf16[32,4096]{1,0:T(8,128)(2,1)S(1)} %bitcast.110), channel_id=1, source_target_pairs={{0,24},{1,25},{2,26},{3,27},{4,28},{5,29},{6,30},{7,31},{8,0},{9,1... | collective-permute-start | bytes 786440 | tf_op jit(solution)/shard_map/ppermute | solution.py:41
  48.7 8.6 %collective-permute-start.4 = (bf16[64,1024]{1,0:T(8,128)(2,1)S(1)}, bf16[64,1024]{1,0:T(8,128)(2,1)S(1)}, u32[]{:S(2)}, u32[]{:S(2)}) collective-permute-start(bf16[64,1024]{1,0:T(8,128)(2,1)S(1)} %get-tuple-element.84), channel_id=1, source_target_pairs={{0,32},{1,33},{2,34},{3,35},{4,36},{5,37},{6,38},{7,39},{8,40},{9,... | collective-permute-start | bytes 393224 | tf_op jit(solution)/shard_map/ppermute | solution.py:41
  50.3 12.0 %collective-permute-start.5 = (bf16[64,1024]{1,0:T(8,128)(2,1)S(1)}, bf16[64,1024]{1,0:T(8,128)(2,1)S(1)}, u32[]{:S(2)}, u32[]{:S(2)}) collective-permute-start(bf16[64,1024]{1,0:T(8,128)(2,1)S(1)} %get-tuple-element.84), channel_id=1, source_target_pairs={{0,40},{1,41},{2,42},{3,43},{4,44},{5,45},{6,46},{7,47},{8,48},{9,... | collective-permute-start | bytes 393224 | tf_op jit(solution)/shard_map/ppermute | solution.py:41
  51.9 12.4 %collective-permute-start.6 = (bf16[64,1024]{1,0:T(8,128)(2,1)S(1)}, bf16[64,1024]{1,0:T(8,128)(2,1)S(1)}, u32[]{:S(2)}, u32[]{:S(2)}) collective-permute-start(bf16[64,1024]{1,0:T(8,128)(2,1)S(1)} %get-tuple-element.84), channel_id=1, source_target_pairs={{0,48},{1,49},{2,50},{3,51},{4,52},{5,53},{6,54},{7,55},{8,56},{9,... | collective-permute-start | bytes 393224 | tf_op jit(solution)/shard_map/ppermute | solution.py:41
  53.4 10.9 %collective-permute-start.7 = (bf16[64,1024]{1,0:T(8,128)(2,1)S(1)}, bf16[64,1024]{1,0:T(8,128)(2,1)S(1)}, u32[]{:S(2)}, u32[]{:S(2)}) collective-permute-start(bf16[64,1024]{1,0:T(8,128)(2,1)S(1)} %get-tuple-element.84), channel_id=1, source_target_pairs={{0,56},{1,57},{2,58},{3,59},{4,60},{5,61},{6,62},{7,63},{8,32},{9,... | collective-permute-start | bytes 393224 | tf_op jit(solution)/shard_map/ppermute | solution.py:41
  69.4 8.3 %collective-permute-start.11 = (bf16[64,1024]{1,0:T(8,128)(2,1)S(1)}, bf16[64,1024]{1,0:T(8,128)(2,1)S(1)}, u32[]{:S(2)}, u32[]{:S(2)}) collective-permute-start(bf16[64,1024]{1,0:T(8,128)(2,1)S(1)} %get-tuple-element.87), channel_id=1, source_target_pairs={{0,56},{1,57},{2,58},{3,59},{4,60},{5,61},{6,62},{7,63},{8,32},{9,... | collective-permute-start | bytes 393224 | tf_op jit(solution)/shard_map/ppermute | solution.py:41
  73.2 8.1 %collective-permute-start.9 = (bf16[64,1024]{1,0:T(8,128)(2,1)S(1)}, bf16[64,1024]{1,0:T(8,128)(2,1)S(1)}, u32[]{:S(2)}, u32[]{:S(2)}) collective-permute-start(bf16[64,1024]{1,0:T(8,128)(2,1)S(1)} %get-tuple-element.87), channel_id=1, source_target_pairs={{0,40},{1,41},{2,42},{3,43},{4,44},{5,45},{6,46},{7,47},{8,48},{9,... | collective-permute-start | bytes 393224 | tf_op jit(solution)/shard_map/ppermute | solution.py:41
  84.3 9.6 %collective-permute-start.12 = (bf16[64,1024]{1,0:T(8,128)(2,1)S(1)}, bf16[64,1024]{1,0:T(8,128)(2,1)S(1)}, u32[]{:S(2)}, u32[]{:S(2)}) collective-permute-start(bf16[64,1024]{1,0:T(8,128)(2,1)S(1)} %get-tuple-element.90), channel_id=1, source_target_pairs={{32,68},{33,69},{34,70},{35,71},{36,64},{37,65},{38,66},{39,67},{4... | collective-permute-start | bytes 393224 | tf_op jit(solution)/shard_map/ppermute | solution.py:41
  96.5 42.1 %collective-permute-start.16 = (bf16[64,1024]{1,0:T(8,128)(2,1)S(1)}, bf16[64,1024]{1,0:T(8,128)(2,1)S(1)}, u32[]{:S(2)}, u32[]{:S(2)}) collective-permute-start(bf16[64,1024]{1,0:T(8,128)(2,1)S(1)} %get-tuple-element.93), channel_id=1, source_target_pairs={{64,96},{65,97},{66,98},{67,99},{68,100},{69,101},{70,102},{71,103... | collective-permute-start | bytes 393224 | tf_op jit(solution)/shard_map/ppermute | solution.py:41
  108.1 30.6 %collective-permute-start.17 = (bf16[64,1024]{1,0:T(8,128)(2,1)S(1)}, bf16[64,1024]{1,0:T(8,128)(2,1)S(1)}, u32[]{:S(2)}, u32[]{:S(2)}) collective-permute-start(bf16[64,1024]{1,0:T(8,128)(2,1)S(1)} %get-tuple-element.93), channel_id=1, source_target_pairs={{64,104},{65,105},{66,106},{67,107},{68,108},{69,109},{70,110},{71... | collective-permute-start | bytes 393224 | tf_op jit(solution)/shard_map/ppermute | solution.py:41
  118.3 20.4 %collective-permute-start.18 = (bf16[64,1024]{1,0:T(8,128)(2,1)S(1)}, bf16[64,1024]{1,0:T(8,128)(2,1)S(1)}, u32[]{:S(2)}, u32[]{:S(2)}) collective-permute-start(bf16[64,1024]{1,0:T(8,128)(2,1)S(1)} %get-tuple-element.93), channel_id=1, source_target_pairs={{64,112},{65,113},{66,114},{67,115},{68,116},{69,117},{70,118},{71... | collective-permute-start | bytes 393224 | tf_op jit(solution)/shard_map/ppermute | solution.py:41
  128.5 10.2 %collective-permute-start.19 = (bf16[64,1024]{1,0:T(8,128)(2,1)S(1)}, bf16[64,1024]{1,0:T(8,128)(2,1)S(1)}, u32[]{:S(2)}, u32[]{:S(2)}) collective-permute-start(bf16[64,1024]{1,0:T(8,128)(2,1)S(1)} %get-tuple-element.93), channel_id=1, source_target_pairs={{64,120},{65,121},{66,122},{67,123},{68,124},{69,125},{70,126},{71... | collective-permute-start | bytes 393224 | tf_op jit(solution)/shard_map/ppermute | solution.py:41
  140.2 322.7 %all-gather.15.cloned.1.call-start = ((), (), s32[]{:S(2)}) async-start(), calls=%async_computation.1 | async-start | bytes 2359296 | tf_op jit(solution)/shard_map/all_gather | solution.py:397
  140.2 46.7 %collective-permute-start.20 = (bf16[64,1024]{1,0:T(8,128)(2,1)S(1)}, bf16[64,1024]{1,0:T(8,128)(2,1)S(1)}, u32[]{:S(2)}, u32[]{:S(2)}) collective-permute-start(bf16[64,1024]{1,0:T(8,128)(2,1)S(1)} %get-tuple-element.97), channel_id=1, source_target_pairs={{0,32},{1,33},{2,34},{3,35},{4,36},{5,37},{6,38},{7,39},{8,40},{9,... | collective-permute-start | bytes 393224 | tf_op jit(solution)/shard_map/ppermute | solution.py:41
  157.1 29.8 %collective-permute-start.21 = (bf16[64,1024]{1,0:T(8,128)(2,1)S(1)}, bf16[64,1024]{1,0:T(8,128)(2,1)S(1)}, u32[]{:S(2)}, u32[]{:S(2)}) collective-permute-start(bf16[64,1024]{1,0:T(8,128)(2,1)S(1)} %get-tuple-element.97), channel_id=1, source_target_pairs={{0,40},{1,41},{2,42},{3,43},{4,44},{5,45},{6,46},{7,47},{8,48},{9,... | collective-permute-start | bytes 393224 | tf_op jit(solution)/shard_map/ppermute | solution.py:41
  167.1 19.9 %collective-permute-start.22 = (bf16[64,1024]{1,0:T(8,128)(2,1)S(1)}, bf16[64,1024]{1,0:T(8,128)(2,1)S(1)}, u32[]{:S(2)}, u32[]{:S(2)}) collective-permute-start(bf16[64,1024]{1,0:T(8,128)(2,1)S(1)} %get-tuple-element.97), channel_id=1, source_target_pairs={{0,48},{1,49},{2,50},{3,51},{4,52},{5,53},{6,54},{7,55},{8,56},{9,... | collective-permute-start | bytes 393224 | tf_op jit(solution)/shard_map/ppermute | solution.py:41
  177.0 14.8 %collective-permute-start.23 = (bf16[64,1024]{1,0:T(8,128)(2,1)S(1)}, bf16[64,1024]{1,0:T(8,128)(2,1)S(1)}, u32[]{:S(2)}, u32[]{:S(2)}) collective-permute-start(bf16[64,1024]{1,0:T(8,128)(2,1)S(1)} %get-tuple-element.97), channel_id=1, source_target_pairs={{0,56},{1,57},{2,58},{3,59},{4,60},{5,61},{6,62},{7,63},{8,32},{9,... | collective-permute-start | bytes 393224 | tf_op jit(solution)/shard_map/ppermute | solution.py:41
  204.5 9.4 %collective-permute-start.26 = (bf16[64,1024]{1,0:T(8,128)(2,1)S(1)}, bf16[64,1024]{1,0:T(8,128)(2,1)S(1)}, u32[]{:S(2)}, u32[]{:S(2)}) collective-permute-start(bf16[64,1024]{1,0:T(8,128)(2,1)S(1)} %get-tuple-element.99), channel_id=1, source_target_pairs={{0,48},{1,49},{2,50},{3,51},{4,52},{5,53},{6,54},{7,55},{8,56},{9,... | collective-permute-start | bytes 393224 | tf_op jit(solution)/shard_map/ppermute | solution.py:41
  206.4 8.1 %collective-permute-start.27 = (bf16[64,1024]{1,0:T(8,128)(2,1)S(1)}, bf16[64,1024]{1,0:T(8,128)(2,1)S(1)}, u32[]{:S(2)}, u32[]{:S(2)}) collective-permute-start(bf16[64,1024]{1,0:T(8,128)(2,1)S(1)} %get-tuple-element.99), channel_id=1, source_target_pairs={{0,56},{1,57},{2,58},{3,59},{4,60},{5,61},{6,62},{7,63},{8,32},{9,... | collective-permute-start | bytes 393224 | tf_op jit(solution)/shard_map/ppermute | solution.py:41
  217.6 10.9 %collective-permute-start.28 = (bf16[64,1024]{1,0:T(8,128)(2,1)S(1)}, bf16[64,1024]{1,0:T(8,128)(2,1)S(1)}, u32[]{:S(2)}, u32[]{:S(2)}) collective-permute-start(bf16[64,1024]{1,0:T(8,128)(2,1)S(1)} %get-tuple-element.102), channel_id=1, source_target_pairs={{32,68},{33,69},{34,70},{35,71},{36,64},{37,65},{38,66},{39,67},{4... | collective-permute-start | bytes 393224 | tf_op jit(solution)/shard_map/ppermute | solution.py:41
  237.9 226.8 %all-gather.19.cloned.1.call-start = ((), (), s32[]{:S(2)}) async-start(), calls=%async_computation.3 | async-start | bytes 2359296 | tf_op jit(solution)/shard_map/all_gather | solution.py:397
  248.4 34.9 %collective-permute-start.43 = (f32[64,1024]{1,0:T(8,128)S(1)}, f32[64,1024]{1,0:T(8,128)S(1)}, u32[]{:S(2)}, u32[]{:S(2)}) collective-permute-start(f32[64,1024]{1,0:T(8,128)S(1)} %get-tuple-element.120), channel_id=1, source_target_pairs={{64,36},{65,37},{66,38},{67,39},{68,32},{69,33},{70,34},{71,35},{7... | collective-permute-start | bytes 786440 | tf_op jit(solution)/shard_map/ppermute | solution.py:41
  249.7 33.3 %collective-permute-start.44 = (bf16[64,1024]{1,0:T(8,128)(2,1)S(1)}, bf16[64,1024]{1,0:T(8,128)(2,1)S(1)}, u32[]{:S(2)}, u32[]{:S(2)}) collective-permute-start(bf16[64,1024]{1,0:T(8,128)(2,1)S(1)} %get-tuple-element.121), channel_id=1, source_target_pairs={{64,44},{65,45},{66,46},{67,47},{68,40},{69,41},{70,42},{71,43},{7... | collective-permute-start | bytes 393224 | tf_op jit(solution)/shard_map/ppermute | solution.py:41
  251.0 32.0 %collective-permute-start.45 = (bf16[64,1024]{1,0:T(8,128)(2,1)S(1)}, bf16[64,1024]{1,0:T(8,128)(2,1)S(1)}, u32[]{:S(2)}, u32[]{:S(2)}) collective-permute-start(bf16[64,1024]{1,0:T(8,128)(2,1)S(1)} %get-tuple-element.122), channel_id=1, source_target_pairs={{64,52},{65,53},{66,54},{67,55},{68,48},{69,49},{70,50},{71,51},{7... | collective-permute-start | bytes 393224 | tf_op jit(solution)/shard_map/ppermute | solution.py:41
  252.3 31.0 %collective-permute-start.46 = (bf16[64,1024]{1,0:T(8,128)(2,1)S(1)}, bf16[64,1024]{1,0:T(8,128)(2,1)S(1)}, u32[]{:S(2)}, u32[]{:S(2)}) collective-permute-start(bf16[64,1024]{1,0:T(8,128)(2,1)S(1)} %get-tuple-element.123), channel_id=1, source_target_pairs={{64,60},{65,61},{66,62},{67,63},{68,56},{69,57},{70,58},{71,59},{7... | collective-permute-start | bytes 393224 | tf_op jit(solution)/shard_map/ppermute | solution.py:41
  287.8 15.2 %collective-permute-start.47 = (f32[64,1024]{1,0:T(8,128)S(1)}, f32[64,1024]{1,0:T(8,128)S(1)}, u32[]{:S(2)}, u32[]{:S(2)}) collective-permute-start(f32[64,1024]{1,0:T(8,128)S(1)} %get-tuple-element.125), channel_id=1, source_target_pairs={{32,0},{33,1},{34,2},{35,3},{36,4},{37,5},{38,6},{39,7},{40,8},{41... | collective-permute-start | bytes 786440 | tf_op jit(solution)/shard_map/ppermute | solution.py:41
  289.7 9.6 %collective-permute-start.48 = (bf16[64,1024]{1,0:T(8,128)(2,1)S(1)}, bf16[64,1024]{1,0:T(8,128)(2,1)S(1)}, u32[]{:S(2)}, u32[]{:S(2)}) collective-permute-start(bf16[64,1024]{1,0:T(8,128)(2,1)S(1)} %get-tuple-element.126), channel_id=1, source_target_pairs={{32,8},{33,9},{34,10},{35,11},{36,12},{37,13},{38,14},{39,15},{40,... | collective-permute-start | bytes 393224 | tf_op jit(solution)/shard_map/ppermute | solution.py:41
  291.6 10.3 %collective-permute-start.49 = (bf16[64,1024]{1,0:T(8,128)(2,1)S(1)}, bf16[64,1024]{1,0:T(8,128)(2,1)S(1)}, u32[]{:S(2)}, u32[]{:S(2)}) collective-permute-start(bf16[64,1024]{1,0:T(8,128)(2,1)S(1)} %get-tuple-element.127), channel_id=1, source_target_pairs={{32,16},{33,17},{34,18},{35,19},{36,20},{37,21},{38,22},{39,23},{4... | collective-permute-start | bytes 393224 | tf_op jit(solution)/shard_map/ppermute | solution.py:41
  293.6 9.4 %collective-permute-start.50 = (bf16[64,1024]{1,0:T(8,128)(2,1)S(1)}, bf16[64,1024]{1,0:T(8,128)(2,1)S(1)}, u32[]{:S(2)}, u32[]{:S(2)}) collective-permute-start(bf16[64,1024]{1,0:T(8,128)(2,1)S(1)} %get-tuple-element.128), channel_id=1, source_target_pairs={{32,24},{33,25},{34,26},{35,27},{36,28},{37,29},{38,30},{39,31},{4... | collective-permute-start | bytes 393224 | tf_op jit(solution)/shard_map/ppermute | solution.py:41
  307.5 38.4 %collective-permute-start.51 = (f32[64,1024]{1,0:T(8,128)S(1)}, f32[64,1024]{1,0:T(8,128)S(1)}, u32[]{:S(2)}, u32[]{:S(2)}) collective-permute-start(f32[64,1024]{1,0:T(8,128)S(1)} %get-tuple-element.130), channel_id=1, source_target_pairs={{0,100},{1,101},{2,102},{3,103},{4,96},{5,97},{6,98},{7,99},{8,108... | collective-permute-start | bytes 786440 | tf_op jit(solution)/shard_map/ppermute | solution.py:41
  315.0 28.7 %collective-permute-start.52 = (bf16[64,1024]{1,0:T(8,128)(2,1)S(1)}, bf16[64,1024]{1,0:T(8,128)(2,1)S(1)}, u32[]{:S(2)}, u32[]{:S(2)}) collective-permute-start(bf16[64,1024]{1,0:T(8,128)(2,1)S(1)} %get-tuple-element.131), channel_id=1, source_target_pairs={{0,108},{1,109},{2,110},{3,111},{4,104},{5,105},{6,106},{7,107},{8... | collective-permute-start | bytes 393224 | tf_op jit(solution)/shard_map/ppermute | solution.py:41
  324.6 19.1 %collective-permute-start.53 = (bf16[64,1024]{1,0:T(8,128)(2,1)S(1)}, bf16[64,1024]{1,0:T(8,128)(2,1)S(1)}, u32[]{:S(2)}, u32[]{:S(2)}) collective-permute-start(bf16[64,1024]{1,0:T(8,128)(2,1)S(1)} %get-tuple-element.132), channel_id=1, source_target_pairs={{0,116},{1,117},{2,118},{3,119},{4,112},{5,113},{6,114},{7,115},{8... | collective-permute-start | bytes 393224 | tf_op jit(solution)/shard_map/ppermute | solution.py:41
  334.1 11.7 %collective-permute-start.54 = (bf16[64,1024]{1,0:T(8,128)(2,1)S(1)}, bf16[64,1024]{1,0:T(8,128)(2,1)S(1)}, u32[]{:S(2)}, u32[]{:S(2)}) collective-permute-start(bf16[64,1024]{1,0:T(8,128)(2,1)S(1)} %get-tuple-element.133), channel_id=1, source_target_pairs={{0,124},{1,125},{2,126},{3,127},{4,120},{5,121},{6,122},{7,123},{8... | collective-permute-start | bytes 393224 | tf_op jit(solution)/shard_map/ppermute | solution.py:41
  349.3 147.9 %all-gather.17.cloned.1.call-start = ((), (), s32[]{:S(2)}) async-start(), calls=%async_computation.2 | async-start | bytes 2359296 | tf_op jit(solution)/shard_map/all_gather | solution.py:397
  349.4 45.2 %collective-permute-start.55 = (f32[64,1024]{1,0:T(8,128)}, f32[64,1024]{1,0:T(8,128)S(1)}, u32[]{:S(2)}, u32[]{:S(2)}) collective-permute-start(f32[64,1024]{1,0:T(8,128)} %copy-done.14), channel_id=1, source_target_pairs={{0,100},{1,101},{2,102},{3,103},{4,96},{5,97},{6,98},{7,99},{8,108... | collective-permute-start | bytes 786440 | tf_op jit(solution)/shard_map/ppermute | solution.py:41
  364.7 29.8 %collective-permute-start.56 = (bf16[64,1024]{1,0:T(8,128)(2,1)}, bf16[64,1024]{1,0:T(8,128)(2,1)S(1)}, u32[]{:S(2)}, u32[]{:S(2)}) collective-permute-start(bf16[64,1024]{1,0:T(8,128)(2,1)} %copy-done.18), channel_id=1, source_target_pairs={{0,108},{1,109},{2,110},{3,111},{4,104},{5,105},{6,106},{7,107},{8... | collective-permute-start | bytes 393224 | tf_op jit(solution)/shard_map/ppermute | solution.py:41
  374.6 19.9 %collective-permute-start.57 = (bf16[64,1024]{1,0:T(8,128)(2,1)}, bf16[64,1024]{1,0:T(8,128)(2,1)S(1)}, u32[]{:S(2)}, u32[]{:S(2)}) collective-permute-start(bf16[64,1024]{1,0:T(8,128)(2,1)} %copy-done.17), channel_id=1, source_target_pairs={{0,116},{1,117},{2,118},{3,119},{4,112},{5,113},{6,114},{7,115},{8... | collective-permute-start | bytes 393224 | tf_op jit(solution)/shard_map/ppermute | solution.py:41
  384.6 10.0 %collective-permute-start.58 = (bf16[64,1024]{1,0:T(8,128)(2,1)S(1)}, bf16[64,1024]{1,0:T(8,128)(2,1)S(1)}, u32[]{:S(2)}, u32[]{:S(2)}) collective-permute-start(bf16[64,1024]{1,0:T(8,128)(2,1)S(1)} %get-tuple-element.138), channel_id=1, source_target_pairs={{0,124},{1,125},{2,126},{3,127},{4,120},{5,121},{6,122},{7,123},{8... | collective-permute-start | bytes 393224 | tf_op jit(solution)/shard_map/ppermute | solution.py:41
  401.0 24.8 %collective-permute-start.59 = (f32[64,1024]{1,0:T(8,128)S(1)}, f32[64,1024]{1,0:T(8,128)S(1)}, u32[]{:S(2)}, u32[]{:S(2)}) collective-permute-start(f32[64,1024]{1,0:T(8,128)S(1)} %get-tuple-element.140), channel_id=1, source_target_pairs={{64,36},{65,37},{66,38},{67,39},{68,32},{69,33},{70,34},{71,35},{7... | collective-permute-start | bytes 786440 | tf_op jit(solution)/shard_map/ppermute | solution.py:41
  402.3 18.6 %collective-permute-start.60 = (bf16[64,1024]{1,0:T(8,128)(2,1)S(1)}, bf16[64,1024]{1,0:T(8,128)(2,1)S(1)}, u32[]{:S(2)}, u32[]{:S(2)}) collective-permute-start(bf16[64,1024]{1,0:T(8,128)(2,1)S(1)} %get-tuple-element.141), channel_id=1, source_target_pairs={{64,44},{65,45},{66,46},{67,47},{68,40},{69,41},{70,42},{71,43},{7... | collective-permute-start | bytes 393224 | tf_op jit(solution)/shard_map/ppermute | solution.py:41
  403.6 21.9 %collective-permute-start.61 = (bf16[64,1024]{1,0:T(8,128)(2,1)S(1)}, bf16[64,1024]{1,0:T(8,128)(2,1)S(1)}, u32[]{:S(2)}, u32[]{:S(2)}) collective-permute-start(bf16[64,1024]{1,0:T(8,128)(2,1)S(1)} %get-tuple-element.142), channel_id=1, source_target_pairs={{64,52},{65,53},{66,54},{67,55},{68,48},{69,49},{70,50},{71,51},{7... | collective-permute-start | bytes 393224 | tf_op jit(solution)/shard_map/ppermute | solution.py:41
  404.9 20.9 %collective-permute-start.62 = (bf16[64,1024]{1,0:T(8,128)(2,1)S(1)}, bf16[64,1024]{1,0:T(8,128)(2,1)S(1)}, u32[]{:S(2)}, u32[]{:S(2)}) collective-permute-start(bf16[64,1024]{1,0:T(8,128)(2,1)S(1)} %get-tuple-element.143), channel_id=1, source_target_pairs={{64,60},{65,61},{66,62},{67,63},{68,56},{69,57},{70,58},{71,59},{7... | collective-permute-start | bytes 393224 | tf_op jit(solution)/shard_map/ppermute | solution.py:41
  430.4 15.6 %collective-permute-start.63 = (f32[64,1024]{1,0:T(8,128)S(1)}, f32[64,1024]{1,0:T(8,128)S(1)}, u32[]{:S(2)}, u32[]{:S(2)}) collective-permute-start(f32[64,1024]{1,0:T(8,128)S(1)} %get-tuple-element.145), channel_id=1, source_target_pairs={{32,0},{33,1},{34,2},{35,3},{36,4},{37,5},{38,6},{39,7},{40,8},{41... | collective-permute-start | bytes 786440 | tf_op jit(solution)/shard_map/ppermute | solution.py:41
  432.3 9.6 %collective-permute-start.64 = (bf16[64,1024]{1,0:T(8,128)(2,1)S(1)}, bf16[64,1024]{1,0:T(8,128)(2,1)S(1)}, u32[]{:S(2)}, u32[]{:S(2)}) collective-permute-start(bf16[64,1024]{1,0:T(8,128)(2,1)S(1)} %get-tuple-element.146), channel_id=1, source_target_pairs={{32,8},{33,9},{34,10},{35,11},{36,12},{37,13},{38,14},{39,15},{40,... | collective-permute-start | bytes 393224 | tf_op jit(solution)/shard_map/ppermute | solution.py:41
  434.2 10.4 %collective-permute-start.65 = (bf16[64,1024]{1,0:T(8,128)(2,1)S(1)}, bf16[64,1024]{1,0:T(8,128)(2,1)S(1)}, u32[]{:S(2)}, u32[]{:S(2)}) collective-permute-start(bf16[64,1024]{1,0:T(8,128)(2,1)S(1)} %get-tuple-element.147), channel_id=1, source_target_pairs={{32,16},{33,17},{34,18},{35,19},{36,20},{37,21},{38,22},{39,23},{4... | collective-permute-start | bytes 393224 | tf_op jit(solution)/shard_map/ppermute | solution.py:41
  436.1 9.8 %collective-permute-start.66 = (bf16[64,1024]{1,0:T(8,128)(2,1)S(1)}, bf16[64,1024]{1,0:T(8,128)(2,1)S(1)}, u32[]{:S(2)}, u32[]{:S(2)}) collective-permute-start(bf16[64,1024]{1,0:T(8,128)(2,1)S(1)} %get-tuple-element.148), channel_id=1, source_target_pairs={{32,24},{33,25},{34,26},{35,27},{36,28},{37,29},{38,30},{39,31},{4... | collective-permute-start | bytes 393224 | tf_op jit(solution)/shard_map/ppermute | solution.py:41
  450.5 8.1 %collective-permute-start.67 = (f32[64,1024]{1,0:T(8,128)S(1)}, f32[64,1024]{1,0:T(8,128)S(1)}, u32[]{:S(2)}, u32[]{:S(2)}) collective-permute-start(f32[64,1024]{1,0:T(8,128)S(1)} %get-tuple-element.150), channel_id=1, source_target_pairs={{32,0},{33,1},{34,2},{35,3},{36,4},{37,5},{38,6},{39,7},{40,8},{41... | collective-permute-start | bytes 786440 | tf_op jit(solution)/shard_map/ppermute | solution.py:41
  460.9 65.5 %all-gather.21.cloned.1.call-start = ((), (), s32[]{:S(2)}) async-start(), calls=%async_computation.4 | async-start | bytes 1310720 | tf_op jit(solution)/shard_map/all_gather | solution.py:401
  462.8 90.0 %all-gather.23.cloned.1.call-start = ((), (), s32[]{:S(2)}) async-start(), calls=%async_computation.5 | async-start | bytes 1310720 | tf_op jit(solution)/shard_map/all_gather | solution.py:401
  464.6 127.8 %all-gather.27.cloned.1.call-start = ((), (), s32[]{:S(2)}) async-start(), calls=%async_computation.7 | async-start | bytes 1310720 | tf_op jit(solution)/shard_map/all_gather | solution.py:401
  466.4 159.5 %all-gather.25.cloned.1.call-start = ((), (), s32[]{:S(2)}) async-start(), calls=%async_computation.6 | async-start | bytes 1310720 | tf_op jit(solution)/shard_map/all_gather | solution.py:401
  558.8 48.1 %collective-permute-start.38 = (bf16[2,128,1024]{2,1,0:T(8,128)(2,1)S(1)}, bf16[2,128,1024]{2,1,0:T(8,128)(2,1)}, u32[]{:S(2)}, u32[]{:S(2)}) collective-permute-start(bf16[2,128,1024]{2,1,0:T(8,128)(2,1)S(1)} %get-tuple-element.112), channel_id=1, source_target_pairs={{0,24},{1,25},{2,26},{3,27},{4,28},{5,29},{6,30},{7,31},{8,0},{9,1... | collective-permute-start | bytes 1572872 | tf_op jit(solution)/shard_map/ppermute | solution.py:41
  560.3 70.2 %collective-permute-start.37 = (bf16[2,128,1024]{2,1,0:T(8,128)(2,1)S(1)}, bf16[2,128,1024]{2,1,0:T(8,128)(2,1)}, u32[]{:S(2)}, u32[]{:S(2)}) collective-permute-start(bf16[2,128,1024]{2,1,0:T(8,128)(2,1)S(1)} %get-tuple-element.111), channel_id=1, source_target_pairs={{0,16},{1,17},{2,18},{3,19},{4,20},{5,21},{6,22},{7,23},{8,24},{9,... | collective-permute-start | bytes 1572872 | tf_op jit(solution)/shard_map/ppermute | solution.py:41
  561.1 79.3 %collective-permute-start.36 = (bf16[2,128,1024]{2,1,0:T(8,128)(2,1)S(1)}, bf16[2,128,1024]{2,1,0:T(8,128)(2,1)}, u32[]{:S(2)}, u32[]{:S(2)}) collective-permute-start(bf16[2,128,1024]{2,1,0:T(8,128)(2,1)S(1)} %get-tuple-element.110), channel_id=1, source_target_pairs={{0,8},{1,9},{2,10},{3,11},{4,12},{5,13},{6,14},{7,15},{8,16},{9,17... | collective-permute-start | bytes 1572872 | tf_op jit(solution)/shard_map/ppermute | solution.py:41
  597.5 45.8 %collective-permute-start.74 = (bf16[1,128,1024]{2,1,0:T(8,128)(2,1)}, bf16[1,128,1024]{2,1,0:T(8,128)(2,1)S(1)}, u32[]{:S(2)}, u32[]{:S(2)}) collective-permute-start(bf16[1,128,1024]{2,1,0:T(8,128)(2,1)} %get-tuple-element.161), channel_id=1, source_target_pairs={{0,8},{1,9},{2,10},{3,11},{4,12},{5,13},{6,14},{7,15},{8,16},{9,17... | collective-permute-start | bytes 786440 | tf_op jit(solution)/shard_map/ppermute | solution.py:41
  608.0 43.0 %collective-permute-start.75 = (bf16[1,128,1024]{2,1,0:T(8,128)(2,1)}, bf16[1,128,1024]{2,1,0:T(8,128)(2,1)S(1)}, u32[]{:S(2)}, u32[]{:S(2)}) collective-permute-start(bf16[1,128,1024]{2,1,0:T(8,128)(2,1)} %get-tuple-element.162), channel_id=1, source_target_pairs={{0,16},{1,17},{2,18},{3,19},{4,20},{5,21},{6,22},{7,23},{8,24},{9,... | collective-permute-start | bytes 786440 | tf_op jit(solution)/shard_map/ppermute | solution.py:41
  617.0 34.0 %collective-permute-start.76 = (bf16[1,128,1024]{2,1,0:T(8,128)(2,1)S(1)}, bf16[1,128,1024]{2,1,0:T(8,128)(2,1)S(1)}, u32[]{:S(2)}, u32[]{:S(2)}) collective-permute-start(bf16[1,128,1024]{2,1,0:T(8,128)(2,1)S(1)} %get-tuple-element.163), channel_id=1, source_target_pairs={{0,24},{1,25},{2,26},{3,27},{4,28},{5,29},{6,30},{7,31},{8,0},{9,1... | collective-permute-start | bytes 786440 | tf_op jit(solution)/shard_map/ppermute | solution.py:41
  630.6 20.5 %collective-permute-start.71 = (bf16[1,128,1024]{2,1,0:T(8,128)(2,1)S(1)}, bf16[1,128,1024]{2,1,0:T(8,128)(2,1)S(1)}, u32[]{:S(2)}, u32[]{:S(2)}) collective-permute-start(bf16[1,128,1024]{2,1,0:T(8,128)(2,1)S(1)} %get-tuple-element.157), channel_id=1, source_target_pairs={{0,8},{1,9},{2,10},{3,11},{4,12},{5,13},{6,14},{7,15},{8,16},{9,17... | collective-permute-start | bytes 786440 | tf_op jit(solution)/shard_map/ppermute | solution.py:41
  640.3 14.9 %collective-permute-start.72 = (bf16[1,128,1024]{2,1,0:T(8,128)(2,1)S(1)}, bf16[1,128,1024]{2,1,0:T(8,128)(2,1)S(1)}, u32[]{:S(2)}, u32[]{:S(2)}) collective-permute-start(bf16[1,128,1024]{2,1,0:T(8,128)(2,1)S(1)} %get-tuple-element.158), channel_id=1, source_target_pairs={{0,16},{1,17},{2,18},{3,19},{4,20},{5,21},{6,22},{7,23},{8,24},{9,... | collective-permute-start | bytes 786440 | tf_op jit(solution)/shard_map/ppermute | solution.py:41
  643.2 12.0 %collective-permute-start.73 = (bf16[1,128,1024]{2,1,0:T(8,128)(2,1)S(1)}, bf16[1,128,1024]{2,1,0:T(8,128)(2,1)S(1)}, u32[]{:S(2)}, u32[]{:S(2)}) collective-permute-start(bf16[1,128,1024]{2,1,0:T(8,128)(2,1)S(1)} %get-tuple-element.159), channel_id=1, source_target_pairs={{0,24},{1,25},{2,26},{3,27},{4,28},{5,29},{6,30},{7,31},{8,0},{9,1... | collective-permute-start | bytes 786440 | tf_op jit(solution)/shard_map/ppermute | solution.py:41
  (46 other events, 222.5 us)
Sparse Core Ops, SparseCore 0:
  140.3 45.5 all-gather.12
  238.0 46.4 all-gather.14
  349.5 43.9 all-gather.18
  461.0 36.1 all-gather.16
  499.3 27.0 all-gather.20
  528.5 24.2 all-gather.22
  554.5 37.8 all-gather.26
  594.0 30.9 all-gather.24

commit v2 on v1

--- a/solution.py
+++ b/solution.py
@@ -42,22 +42,14 @@
 
 
 def forward_moves(tick):
-    moves = {}
-    for stream in range(STREAMS):
-        layer = tick - stream
-        if 0 <= layer < LAST:
-            source = layer % PIPES
-            moves[source] = ((layer + 1) % PIPES, source % 2)
+    moves = {0: (1, 0), 2: (3, 0)}
+    moves.update({3: (0, 1)} if tick % PIPES in (0, 3) else {1: (2, 1)})
     return moves
 
 
 def backward_moves(tick):
-    moves = {}
-    for stream in range(STREAMS):
-        layer = 2 * LAST + stream - tick
-        if 1 <= layer <= LAST:
-            source = layer % PIPES
-            moves[source] = ((layer - 1) % PIPES, 1 - source % 2)
+    moves = {1: (0, 0), 3: (2, 0)}
+    moves.update({0: (3, 1)} if (2 * LAST - tick) % PIPES in (0, 3) else {2: (1, 1)})
     return moves
 
 
@@ -95,13 +87,44 @@
     return lax.rem(index + count, count)
 
 
+def held(weights, after):
+    pieces = 8
+    rows = weights.shape[1] // pieces
+
+    def kernel(source, *refs):
+        target, sems = refs[-2:]
+        copies = []
+        for slot in range(weights.shape[0]):
+            for k in range(pieces):
+                part = pl.ds(k * rows, rows)
+                copies.append(
+                    pltpu.make_async_copy(
+                        source.at[slot, part], target.at[slot, part], sems.at[slot, k]
+                    )
+                )
+        for copy in copies:
+            copy.start()
+        for copy in copies:
+            copy.wait()
+
+    return pl.pallas_call(
+        kernel,
+        in_specs=[ANYWHERE] * (1 + len(after)),
+        out_specs=pl.BlockSpec(memory_space=pltpu.VMEM),
+        out_shape=pltpu.VMEM(weights.shape, weights.dtype),
+        scratch_shapes=[pltpu.SemaphoreType.DMA((weights.shape[0], pieces))],
+        compiler_params=pltpu.CompilerParams(vmem_limit_bytes=17 << 20),
+        name="held",
+    )(pltpu.with_memory_space_constraint(weights, pltpu.HBM), *after)
+
+
 def ingest(meta, arrays):
     rows, features = arrays[0].shape
     half = rows // 2
     quarter = features // 4
 
     def kernel(meta_ref, *refs):
-        sources, (hidden_ref, cotangent_ref) = refs[:4], refs[4:]
+        sources, blocks, own_ref = refs[:4], refs[4:12], refs[12]
         tensor = meta_ref[1]
         for step in range(4):
             row = pl.multiple_of(turned(tensor - step) * half, half)
@@ -109,24 +132,23 @@
                 for turn in range(4):
                     column = pl.multiple_of(turned(tensor - turn) * quarter, quarter)
                     piece = sources[step][stream * half : (stream + 1) * half, pl.ds(column, quarter)]
-                    hidden_ref[stream, turn, pl.ds(row, half), :] = piece
+                    blocks[4 * stream + turn][pl.ds(row, half), :] = piece
                     if turn == 0:
-                        cotangent_ref[stream, pl.ds(row, half), :] = piece.astype(F32)
+                        own_ref[stream, pl.ds(row, half), :] = piece
 
     whole = pl.BlockSpec(memory_space=pltpu.VMEM)
     return pl.pallas_call(
         kernel,
         in_specs=[pl.BlockSpec(memory_space=pltpu.SMEM)] + [whole] * 4,
-        out_specs=[whole, whole],
-        out_shape=[
-            jax.ShapeDtypeStruct((2, 4, 4 * half, quarter), BF16),
-            jax.ShapeDtypeStruct((2, 4 * half, quarter), F32),
-        ],
+        out_specs=[whole] * 9,
+        out_shape=[jax.ShapeDtypeStruct((4 * half, quarter), BF16)] * 8
+        + [jax.ShapeDtypeStruct((2, 4 * half, quarter), BF16)],
+        compiler_params=pltpu.CompilerParams(vmem_limit_bytes=8 << 20),
         name="ingest",
     )(meta, *arrays)
 
 
-def forward_step(tick, meta, blocks, gains, weights, hidden_stash, normed_stash):
+def forward_step(tick, meta, blocks, firsts, gains, weights, hidden_stash, normed_stash, after=()):
     rows, quarter = blocks[0].shape
     features = 4 * quarter
 
@@ -135,19 +157,22 @@
         turn = pl.program_id(0)
         tensor = meta_ref[1]
         active, slot, _, multiplies = forward_place(tick, meta_ref[0])
-        ins = (b0, b1, b2, b3)
 
         @pl.when(active & (turn == 0))
         def _():
+            for k, ref in enumerate((b0, b1, b2, b3)):
+                block = ref[...]
+                if firsts:
+                    block = jnp.where(meta_ref[0] == 0, refs[k][...], block)
+                hidden_ref[0, k] = block
             squares = 0.0
-            for ref in ins:
-                wide = ref[...].astype(F32)
+            for k in range(4):
+                wide = hidden_ref[0, k].astype(F32)
                 squares = squares + jnp.sum(wide * wide, axis=-1, keepdims=True)
             scale = lax.rsqrt(squares * (1.0 / features) + EPSILON)
-            for k, ref in enumerate(ins):
+            for k in range(4):
                 gain = gain_ref[slot, pl.ds(turned(tensor - k), 1), :]
-                normed[k] = (ref[...].astype(F32) * scale * gain).astype(BF16)
-                hidden_ref[0, k] = ref[...]
+                normed[k] = (hidden_ref[0, k].astype(F32) * scale * gain).astype(BF16)
             normed_ref[0] = normed[0]
 
         @pl.when(multiplies)
@@ -165,7 +190,7 @@
         @pl.when(multiplies & (turn == 3))
         def _():
             rounded = total[...].astype(BF16).astype(F32)
-            next_ref[...] = (b0[...].astype(F32) + rounded).astype(BF16)
+            next_ref[...] = (hidden_ref[0, 0].astype(F32) + rounded).astype(BF16)
 
     def weight_at(turn, meta_ref):
         _, slot, _, multiplies = forward_place(tick, meta_ref[0])
@@ -187,7 +212,8 @@
                 pl.BlockSpec((2, 4, quarter), lambda turn, meta_ref: (0, 0, 0)),
                 pl.BlockSpec((1, quarter, quarter), weight_at),
             ]
-            + [ANYWHERE] * len(stashes),
+            + [block] * len(firsts)
+            + [ANYWHERE] * (len(stashes) + len(after)),
             out_specs=[
                 block,
                 pl.BlockSpec((1, 4, rows, quarter), lambda turn, m: (stash_at(turn, m), 0, 0, 0)),
@@ -200,26 +226,32 @@
             jax.ShapeDtypeStruct((5, 4, rows, quarter), BF16),
             jax.ShapeDtypeStruct((5, rows, quarter), BF16),
         ],
-        input_output_aliases={7: 1, 8: 2} if stashes else {},
-        compiler_params=pltpu.CompilerParams(vmem_limit_bytes=24 << 20),
+        input_output_aliases={7 + len(firsts): 1, 8 + len(firsts): 2} if stashes else {},
+        compiler_params=pltpu.CompilerParams(vmem_limit_bytes=16 << 20),
         cost_estimate=pl.CostEstimate(
             flops=2 * rows * features * quarter, bytes_accessed=2 * features * quarter, transcendentals=0
         ),
         name="forward_step",
-    )(meta, *blocks, gains, weights, *stashes)
-
-
-def backward_step(tick, meta, own, others, gains, weights, hidden_stash, grad_stash):
+    )(meta, *blocks, gains, weights, *firsts, *stashes, *after)
+
+
+def backward_step(tick, meta, given, own, others, gains, weights, hidden_stash, grad_stash, after=()):
     rows, quarter = own.shape
     features = 4 * quarter
 
-    def kernel(meta_ref, own_ref, c1, c2, c3, gain_ref, weight_ref, hidden_ref, *refs):
+    def kernel(meta_ref, given_ref, own_ref, c1, c2, c3, gain_ref, weight_ref, hidden_ref, *refs):
         own_out, o1, o2, o3, grad_ref, delta, scaled, inner = refs[-8:]
         turn = pl.program_id(0)
         tensor = meta_ref[1]
-        active, slot, _, multiplies = backward_place(tick, meta_ref[0])
-
-        @pl.when(active & (turn == 0))
+        active, slot, stream, multiplies = backward_place(tick, meta_ref[0])
+        starts = active & (tick < LAST + STREAMS) & (meta_ref[0] == LAST % PIPES)
+
+        @pl.when(starts & (turn == 0))
+        def _():
+            delta[...] = given_ref[stream]
+            grad_ref[0] = given_ref[stream]
+
+        @pl.when(active & jnp.logical_not(starts) & (turn == 0))
         def _():
             total = own_ref[...]
             for ref in (c1, c2, c3):
@@ -276,13 +308,14 @@
         grid_spec=pltpu.PrefetchScalarGridSpec(
             num_scalar_prefetch=1,
             grid=(4,),
-            in_specs=[block] * 4
+            in_specs=[pl.BlockSpec((2, rows, quarter), lambda turn, meta_ref: (0, 0, 0))]
+            + [block] * 4
             + [
                 pl.BlockSpec((2, 4, quarter), lambda turn, meta_ref: (0, 0, 0)),
                 pl.BlockSpec((1, quarter, quarter), weight_at),
                 pl.BlockSpec((1, 4, rows, quarter), lambda turn, m: (stash_at(turn, m, 0), 0, 0, 0)),
             ]
-            + [ANYWHERE] * len(stashes),
+            + [ANYWHERE] * (len(stashes) + len(after)),
             out_specs=[block] * 4
             + [pl.BlockSpec((1, rows, quarter), lambda turn, m: (stash_at(turn, m, 4), 0, 0))],
             scratch_shapes=[
@@ -294,55 +327,73 @@
         out_shape=[jax.ShapeDtypeStruct((rows, quarter), F32)]
         + [jax.ShapeDtypeStruct((rows, quarter), BF16)] * 3
         + [jax.ShapeDtypeStruct((5, rows, quarter), BF16)],
-        input_output_aliases={8: 4} if stashes else {},
-        compiler_params=pltpu.CompilerParams(vmem_limit_bytes=24 << 20),
+        input_output_aliases={9: 4} if stashes else {},
+        compiler_params=pltpu.CompilerParams(vmem_limit_bytes=16 << 20),
         cost_estimate=pl.CostEstimate(
             flops=2 * rows * features * quarter, bytes_accessed=2 * features * quarter, transcendentals=0
         ),
         name="backward_step",
-    )(meta, own, *others, gains, weights, hidden_stash, *stashes)
-
-
-def gram(meta, tokens, picked, inv_tokens):
-    slots, count, quarter = tokens.shape
-    own = picked.shape[-1]
-
-    def kernel(meta_ref, tokens_ref, picked_ref, *outs):
-        for step, out in enumerate(outs):
-            left = picked_ref[0, turned(meta_ref[1] + step)]
-            product = lax.dot_general(
-                left, tokens_ref[0], (((0,), (0,)), ((), ())), preferred_element_type=F32
-            )
-            out[0] = (product * inv_tokens).astype(BF16)
-
-    return pl.pallas_call(
-        kernel,
-        grid_spec=pltpu.PrefetchScalarGridSpec(
-            num_scalar_prefetch=1,
-            grid=(slots,),
-            in_specs=[
-                pl.BlockSpec((1, count, quarter), lambda s, m: (s, 0, 0)),
-                pl.BlockSpec((1, 4, count, own), lambda s, m: (s, 0, 0, 0)),
-            ],
-            out_specs=[pl.BlockSpec((1, own, quarter), lambda s, m: (s, 0, 0))] * 4,
-        ),
-        out_shape=[jax.ShapeDtypeStruct((slots, own, quarter), BF16)] * 4,
-        compiler_params=pltpu.CompilerParams(vmem_limit_bytes=32 << 20),
+    )(meta, given, own, *others, gains, weights, hidden_stash, *stashes, *after)
+
+
+def own_columns(meta, pieces, own):
+    rows = pieces[0].shape[0]
+
+    def kernel(meta_ref, *refs):
+        column = pl.multiple_of(meta_ref[2] * own, own)
+        for k, piece in enumerate(refs[:-1]):
+            refs[-1][k * rows : (k + 1) * rows, :] = piece[:, pl.ds(column, own)]
+
+    whole = pl.BlockSpec(memory_space=pltpu.VMEM)
+    return pl.pallas_call(
+        kernel,
+        in_specs=[pl.BlockSpec(memory_space=pltpu.SMEM)] + [whole] * len(pieces),
+        out_specs=whole,
+        out_shape=jax.ShapeDtypeStruct((rows * len(pieces), own), BF16),
+        compiler_params=pltpu.CompilerParams(vmem_limit_bytes=8 << 20),
+        name="own_columns",
+    )(meta, *pieces)
+
+
+def gram(pieces, picked, inv_tokens):
+    quarter = pieces[0].shape[-1]
+    count, own = picked[0].shape
+    starts = [0]
+    for piece in pieces:
+        starts.append(starts[-1] + piece.shape[0])
+
+    def kernel(*refs):
+        token_refs, picked_refs, outs = refs[: len(pieces)], refs[len(pieces) : -4], refs[-4:]
+        for left, out in zip(picked_refs, outs):
+            product = 0.0
+            for ref, start, stop in zip(token_refs, starts, starts[1:]):
+                product = product + lax.dot_general(
+                    left[start:stop, :], ref[...], (((0,), (0,)), ((), ())), preferred_element_type=F32
+                )
+            out[...] = (product * inv_tokens).astype(BF16)
+
+    whole = pl.BlockSpec(memory_space=pltpu.VMEM)
+    return pl.pallas_call(
+        kernel,
+        in_specs=[whole] * (len(pieces) + 4),
+        out_specs=[whole] * 4,
+        out_shape=[jax.ShapeDtypeStruct((own, quarter), BF16)] * 4,
+        compiler_params=pltpu.CompilerParams(vmem_limit_bytes=20 << 20),
         cost_estimate=pl.CostEstimate(
-            flops=2 * slots * count * 4 * own * quarter,
-            bytes_accessed=2 * slots * (count * quarter + 8 * own * quarter),
+            flops=2 * count * 4 * own * quarter,
+            bytes_accessed=2 * (count * quarter + 8 * own * quarter),
             transcendentals=0,
         ),
         name="gram",
-    )(meta, tokens, picked)
+    )(*pieces, *picked)
+
+
+def shifted(array, x=0, y=0, z=0):
+    return permuted(array, lambda p, t, u, v: (p, (t + x) % SIZES[1], u ^ z, (v + y) % SIZES[3]))
 
 
 def share_columns(blocks):
-    return [blocks[0]] + [
-        permuted(block, lambda p, t, z, y, k=k: (p, (t + k) % SIZES[1], z, y))
-        for k, block in enumerate(blocks)
-        if k
-    ]
+    return [blocks[0]] + [shifted(blocks[4 - k], x=k) for k in (1, 2, 3)]
 
 
 def assemble(meta, first, second):
@@ -361,7 +412,7 @@
         in_specs=[pl.BlockSpec(memory_space=pltpu.SMEM)] + [whole] * 8,
         out_specs=whole,
         out_shape=jax.ShapeDtypeStruct((own, 2, 4 * quarter), BF16),
-        compiler_params=pltpu.CompilerParams(vmem_limit_bytes=32 << 20),
+        compiler_params=pltpu.CompilerParams(vmem_limit_bytes=20 << 20),
         name="assemble",
     )(meta, *first, *second)
 
@@ -374,72 +425,87 @@
     group = lax.axis_index(DP)
     own_rows = quarter // lax.axis_size(DP)
     inv_tokens = 1.0 / (micro_count * shard_rows * lax.axis_size(TENSOR_DP))
-    meta = jnp.stack([pipe, tensor]).astype(jnp.int32)
-    weights = weights.reshape(weights.shape[0], features, quarter)
+    meta = jnp.stack([pipe, tensor, group]).astype(jnp.int32)
     gains = norm_gains.reshape(norm_gains.shape[0], 4, quarter)
-
-    def start_target(step):
-        def target(p, t, z, y):
-            if p == 0 and step:
-                return (p, (t + step) % SIZES[1], z, y)
-            if p == LAST % PIPES:
-                return (p, (t + step) % SIZES[1], 1 - z, y)
-            return None
-
-        return target
+    weights = held(weights.reshape(weights.shape[0], features, quarter), (meta, gains))
+    weights = pltpu.with_memory_space_constraint(weights, pltpu.VMEM)
 
     given = jnp.where(pipe == LAST % PIPES, cotangent, inputs).reshape(-1, features)
-    arrived = [permuted(given, start_target(step)) for step in range(4)]
-    arrived[0] = jnp.where(pipe == 0, given, arrived[0])
-    first_blocks, last_deltas = ingest(meta, arrived)
-
-    def gather_group(rows):
-        return lax.all_gather(rows, DP, axis=0, tiled=True)
-
-    def pick(tokens):
-        mine = lax.dynamic_slice_in_dim(tokens, group * own_rows, own_rows, 1)
-        return lax.all_gather(mine, "tensor", axis=0, tiled=False)
-
-    def factor_blocks(tokens_list):
-        tokens = jnp.stack(tokens_list)
-        picked = jnp.stack([pick(one) for one in tokens_list])
-        return share_columns(gram(meta, tokens, picked, inv_tokens))
+    *first_blocks, last_deltas = ingest(meta, [given] + [shifted(given, x=k) for k in (1, 2, 3)])
+    last_deltas = shifted(last_deltas, z=1)
+
+    def picked_rows(pieces):
+        mine = own_columns(meta, pieces, own_rows)
+        return [mine] + [shifted(mine, x=k) for k in (1, 2, 3)]
+
+    def over_z(rows):
+        return jnp.concatenate([rows, shifted(rows, z=1)])
+
+    def over_y(rows):
+        return [rows] + [shifted(rows, y=k) for k in (1, 2, 3)]
+
+    def slot_rows(stash, slot):
+        return stash[2 * slot : 2 * slot + 2].reshape(-1, quarter)
+
+    def blocks_of(pieces, picked):
+        return share_columns(gram(pieces, picked, inv_tokens))
 
     hidden_stash = normed_stash = grad_stash = None
-    zeros = jnp.zeros(first_blocks.shape[2:], BF16)
-    received = [first_blocks[0, k] for k in range(4)]
-    back = [jnp.zeros(first_blocks.shape[2:], F32), zeros, zeros, zeros]
-    act_tokens = []
+    received = first_blocks[:4]
+    back = [jnp.zeros(first_blocks[0].shape, F32)] + first_blocks[1:4]
+    after = {}
     for tick in range(2 * LAST + STREAMS):
+        waits = after.get(tick, ())
         if tick <= LAST + 1:
-            blocks = received
-            if 0 < tick < STREAMS:
-                blocks = [jnp.where(pipe == 0, first_blocks[tick, k], received[k]) for k in range(4)]
+            firsts = first_blocks[4 * tick : 4 * tick + 4] if 0 < tick < STREAMS else []
             following, hidden_stash, normed_stash = forward_step(
-                tick, meta, blocks, gains, weights, hidden_stash, normed_stash
+                tick, meta, received, firsts, gains, weights, hidden_stash, normed_stash, waits
             )
             if tick <= LAST:
                 received = fan_out([following] * 4, forward_moves(tick))
-            if tick == PIPES:
-                act_tokens.append(gather_group(normed_stash[:2].reshape(-1, quarter)))
-            if tick == 2 * PIPES:
-                act_tokens.append(gather_group(normed_stash[2:4].reshape(-1, quarter)))
+            if tick == 4:
+                tokens_0 = over_z(slot_rows(normed_stash, 0))
+                after[5] = (tokens_0,)
+            if tick == 5:
+                tokens_0 = over_y(tokens_0)
+                after[6] = tokens_0[1:]
+            if tick == 6:
+                picked_0 = picked_rows(tokens_0)
+                after[7] = picked_0[1:]
+            if tick == 8:
+                tokens_1 = over_z(slot_rows(normed_stash, 1))
+                after[9] = act_0[1:] + [tokens_1]
         if tick >= LAST:
-            own = back[0]
-            if tick < LAST + STREAMS:
-                own = jnp.where(pipe == LAST % PIPES, last_deltas[tick - LAST], own)
             *sent, grad_stash = backward_step(
-                tick, meta, own, back[1:], gains, weights, hidden_stash, grad_stash
+                tick, meta, last_deltas, back[0], back[1:], gains, weights, hidden_stash, grad_stash, waits
             )
             if tick < 2 * LAST + STREAMS - 1:
                 back = fan_out(sent, backward_moves(tick))
-            if tick == LAST + PIPES:
-                late_tokens = gather_group(grad_stash[2:4].reshape(-1, quarter))
-    act_blocks = factor_blocks(act_tokens)
-    act_factor = assemble(meta, [b[0] for b in act_blocks], [b[1] for b in act_blocks])
-    late = factor_blocks([late_tokens])
-    early = factor_blocks([gather_group(grad_stash[:2].reshape(-1, quarter))])
-    grad_factor = assemble(meta, [b[0] for b in early], [b[0] for b in late])
+            if tick == 7:
+                act_0 = blocks_of(tokens_0, picked_0)
+            if tick == 9:
+                tokens_1 = over_y(tokens_1)
+                after[10] = tokens_1[1:]
+            if tick == 10:
+                picked_1 = picked_rows(tokens_1)
+                after[11] = picked_1[1:]
+            if tick == 11:
+                act_1 = blocks_of(tokens_1, picked_1)
+                late = over_z(slot_rows(grad_stash, 1))
+                after[12] = (late,)
+            if tick == 12:
+                late = over_y(late)
+                after[13] = late[1:] + act_1[1:]
+            if tick == 13:
+                late_picked = picked_rows(late)
+                after[14] = late_picked[1:]
+            if tick == 14:
+                grad_1 = blocks_of(late, late_picked)
+                after[15] = grad_1[1:]
+    act_factor = assemble(meta, act_0, act_1)
+    early = over_y(over_z(slot_rows(grad_stash, 0)))
+    grad_0 = blocks_of(early, picked_rows(early))
+    grad_factor = assemble(meta, grad_0, grad_1)
     shape = (own_rows, 2, 1, features)
     return (act_factor.reshape(shape), grad_factor.reshape(shape))
 

time: 669 us -> 478 us (0.71)
  the two profiles are of different devices: /device:TPU:1 before, /device:TPU:3 now
where the time goes in v2:
time: 478 us; the launch traced here: 468 us
  starting transfers between devices  240 us (50%)
  waiting for transfers between devices  161 us (34%)
  Pallas kernels  62.4 us (13%)
    ppermute x108, starting transfers between devices, permuted(): return lax.ppermute(array, AXES, pairs)  240 us
    ppermute x108, waiting for transfers between devices, permuted(): return lax.ppermute(array, AXES, pairs)  161 us
    pallas_call x9, Pallas kernels, backward_step(): pl.pallas_call(kernel, grid_spec=pltpu.PrefetchScalarGridSpec(num_scalar_...  22.5 us
    pallas_call x9, Pallas kernels, forward_step(): pl.pallas_call(kernel, grid_spec=pltpu.PrefetchScalarGridSpec(num_scalar_...  16.2 us
    pallas_call x2, Pallas kernels, assemble(): pl.pallas_call(kernel, in_specs=[pl.BlockSpec(memory_space=pltpu.SMEM)] +...  9.57 us
  transfers between devices with their start and end apart: 108, of which 44 were waited for; matrix products, arithmetic and copies ran while one was open for 0% of the time, Pallas kernels for 6%

profile of v2, /device:TPU:3, one launch (start us, length us, event | category | flops | bytes accessed | tf_op | source)
XLA Modules:
  0.0 468.4 jit_solution(450691753513344863)
XLA Ops:
  1.7 2.4 collective-permute-start.1
  6.6 5.9 %held.1.weight_ref = bf16[2,4096,1024]{2,1,0:T(8,128)(2,1)S(1)} custom-call(bf16[2,4096,1024]{2,1,0:T(8,128)(2,1)} %bitcast.19, s32[3]{0:T(128)S(1)} %pad_add_fusion.meta_ref.refs_0_, f32[2,4,1024]{2,1,0:T(4,128)S(1)} %reshape.32.refs_1_.gain_ref), custom_call_target="tpu_custom_call" | custom-call | tf_op jit(solution)/shard_map/held/pallas_call | solution.py:110
  12.5 2.9 collective-permute-done.1.refs_2_
  22.9 4.2 collective-permute-done.6.b3
  27.1 2.6 collective-permute-done.5.b2
  29.7 2.8 collective-permute-done.4.b1
  32.5 3.0 forward_step.10
  35.5 3.8 collective-permute-start.10
  39.3 4.7 %collective-permute-start.9 = (bf16[64,1024]{1,0:T(8,128)(2,1)S(1)}, bf16[64,1024]{1,0:T(8,128)(2,1)S(1)}, u32[]{:S(2)}, u32[]{:S(2)}) collective-permute-start(bf16[64,1024]{1,0:T(8,128)(2,1)S(1)} %get-tuple-element.105), channel_id=1, source_target_pairs={{0,48},{1,49},{2,50},{3,51},{4,52},{5,53},{6,54},{7,55},{8,56},{9,... | collective-permute-start | bytes 393224 | tf_op jit(solution)/shard_map/ppermute | solution.py:41
  44.0 2.6 collective-permute-start.8
  48.5 2.9 collective-permute-done.8.b1
  51.5 3.0 forward_step.11
  54.5 6.8 %collective-permute-start.14 = (bf16[64,1024]{1,0:T(8,128)(2,1)S(1)}, bf16[64,1024]{1,0:T(8,128)(2,1)S(1)}, u32[]{:S(2)}, u32[]{:S(2)}) collective-permute-start(bf16[64,1024]{1,0:T(8,128)(2,1)S(1)} %get-tuple-element.108), channel_id=1, source_target_pairs={{0,56},{1,57},{2,58},{3,59},{4,60},{5,61},{6,62},{7,63},{8,32},{9,... | collective-permute-start | bytes 393224 | tf_op jit(solution)/shard_map/ppermute | solution.py:41
  78.0 2.5 collective-permute-done.17.b2
  85.9 2.6 collective-permute-done.19
  88.5 2.8 collective-permute-start.22
  92.4 4.7 %collective-permute-done.32.b3 = bf16[64,1024]{1,0:T(8,128)(2,1)S(1)} collective-permute-done((bf16[64,1024]{1,0:T(8,128)(2,1)S(1)}, bf16[64,1024]{1,0:T(8,128)(2,1)S(1)}, u32[]{:S(2)}, u32[]{:S(2)}) %collective-permute-start.32) | collective-permute-done | bytes 131104 | tf_op jit(solution)/shard_map/ppermute | solution.py:41
  100.9 8.0 %collective-permute-done.30.b1 = bf16[64,1024]{1,0:T(8,128)(2,1)S(1)} collective-permute-done((bf16[64,1024]{1,0:T(8,128)(2,1)S(1)}, bf16[64,1024]{1,0:T(8,128)(2,1)S(1)}, u32[]{:S(2)}, u32[]{:S(2)}) %collective-permute-start.30) | collective-permute-done | bytes 131104 | tf_op jit(solution)/shard_map/ppermute | solution.py:41
  108.9 3.0 forward_step.14
  114.0 4.4 collective-permute-start.35
  124.3 5.3 %collective-permute-start.33 = (bf16[64,1024]{1,0:T(8,128)(2,1)S(1)}, bf16[64,1024]{1,0:T(8,128)(2,1)S(1)}, u32[]{:S(2)}, u32[]{:S(2)}) collective-permute-start(bf16[64,1024]{1,0:T(8,128)(2,1)S(1)} %get-tuple-element.121), channel_id=1, source_target_pairs={{0,32},{1,33},{2,34},{3,35},{4,36},{5,37},{6,38},{7,39},{8,40},{9,... | collective-permute-start | bytes 393224 | tf_op jit(solution)/shard_map/ppermute | solution.py:41
  131.5 3.0 forward_step.15
  134.6 6.4 %collective-permute-start.40 = (bf16[64,1024]{1,0:T(8,128)(2,1)S(1)}, bf16[64,1024]{1,0:T(8,128)(2,1)S(1)}, u32[]{:S(2)}, u32[]{:S(2)}) collective-permute-start(bf16[64,1024]{1,0:T(8,128)(2,1)S(1)} %get-tuple-element.124), channel_id=1, source_target_pairs={{0,56},{1,57},{2,58},{3,59},{4,60},{5,61},{6,62},{7,63},{8,32},{9,... | collective-permute-start | bytes 393224 | tf_op jit(solution)/shard_map/ppermute | solution.py:41
  151.3 2.4 collective-permute-start.37
  155.5 3.0 collective-permute-done.24.refs_6_.refs_3_.refs_1_
  162.0 4.7 collective-permute-start.57
  171.9 7.0 %collective-permute-start.58 = (bf16[64,1024]{1,0:T(8,128)(2,1)S(1)}, bf16[64,1024]{1,0:T(8,128)(2,1)S(1)}, u32[]{:S(2)}, u32[]{:S(2)}) collective-permute-start(bf16[64,1024]{1,0:T(8,128)(2,1)S(1)} %get-tuple-element.138), channel_id=1, source_target_pairs={{0,116},{1,117},{2,118},{3,119},{4,112},{5,113},{6,114},{7,115},{8... | collective-permute-start | bytes 393224 | tf_op jit(solution)/shard_map/ppermute | solution.py:41
  178.9 7.5 %collective-permute-start.56 = (f32[64,1024]{1,0:T(8,128)S(1)}, f32[64,1024]{1,0:T(8,128)S(1)}, u32[]{:S(2)}, u32[]{:S(2)}) collective-permute-start(f32[64,1024]{1,0:T(8,128)S(1)} %get-tuple-element.136), channel_id=1, source_target_pairs={{0,100},{1,101},{2,102},{3,103},{4,96},{5,97},{6,98},{7,99},{8,108... | collective-permute-start | bytes 786440 | tf_op jit(solution)/shard_map/ppermute | solution.py:41
  187.8 3.6 collective-permute-start.59
  191.8 2.9 collective-permute-start.27
  197.0 3.2 collective-permute-start.60
  202.3 7.6 %collective-permute-start.62 = (bf16[64,1024]{1,0:T(8,128)(2,1)S(1)}, bf16[64,1024]{1,0:T(8,128)(2,1)S(1)}, u32[]{:S(2)}, u32[]{:S(2)}) collective-permute-start(bf16[64,1024]{1,0:T(8,128)(2,1)S(1)} %get-tuple-element.144), channel_id=1, source_target_pairs={{32,16},{33,17},{34,18},{35,19},{36,20},{37,21},{38,22},{39,23},{4... | collective-permute-start | bytes 393224 | tf_op jit(solution)/shard_map/ppermute | solution.py:41
  209.9 2.9 collective-permute-start.63
  220.0 4.5 backward_step.11
  228.4 5.8 %collective-permute-done.65.c1 = bf16[64,1024]{1,0:T(8,128)(2,1)S(1)} collective-permute-done((bf16[64,1024]{1,0:T(8,128)(2,1)S(1)}, bf16[64,1024]{1,0:T(8,128)(2,1)S(1)}, u32[]{:S(2)}, u32[]{:S(2)}) %collective-permute-start.65) | collective-permute-done | bytes 131104 | tf_op jit(solution)/shard_map/ppermute | solution.py:41
  236.1 3.8 collective-permute-done.66.c2
  241.9 6.5 %collective-permute-done.67.c3 = bf16[64,1024]{1,0:T(8,128)(2,1)S(1)} collective-permute-done((bf16[64,1024]{1,0:T(8,128)(2,1)S(1)}, bf16[64,1024]{1,0:T(8,128)(2,1)S(1)}, u32[]{:S(2)}, u32[]{:S(2)}) %collective-permute-start.67) | collective-permute-done | bytes 131104 | tf_op jit(solution)/shard_map/ppermute | solution.py:41
  248.4 4.5 backward_step.12
  263.5 10.8 %collective-permute-start.71 = (bf16[64,1024]{1,0:T(8,128)(2,1)S(1)}, bf16[64,1024]{1,0:T(8,128)(2,1)S(1)}, u32[]{:S(2)}, u32[]{:S(2)}) collective-permute-start(bf16[64,1024]{1,0:T(8,128)(2,1)S(1)} %get-tuple-element.155), channel_id=1, source_target_pairs={{0,124},{1,125},{2,126},{3,127},{4,120},{5,121},{6,122},{7,123},{8... | collective-permute-start | bytes 393224 | tf_op jit(solution)/shard_map/ppermute | solution.py:41
  276.9 6.1 %collective-permute-start.73 = (bf16[64,1024]{1,0:T(8,128)(2,1)S(1)}, bf16[64,1024]{1,0:T(8,128)(2,1)S(1)}, u32[]{:S(2)}, u32[]{:S(2)}) collective-permute-start(bf16[64,1024]{1,0:T(8,128)(2,1)S(1)} %get-tuple-element.158), channel_id=1, source_target_pairs={{0,108},{1,109},{2,110},{3,111},{4,104},{5,105},{6,106},{7,107},{8... | collective-permute-start | bytes 393224 | tf_op jit(solution)/shard_map/ppermute | solution.py:41
  283.1 7.1 %collective-permute-start.74 = (bf16[64,1024]{1,0:T(8,128)(2,1)S(1)}, bf16[64,1024]{1,0:T(8,128)(2,1)S(1)}, u32[]{:S(2)}, u32[]{:S(2)}) collective-permute-start(bf16[64,1024]{1,0:T(8,128)(2,1)S(1)} %get-tuple-element.159), channel_id=1, source_target_pairs={{0,116},{1,117},{2,118},{3,119},{4,112},{5,113},{6,114},{7,115},{8... | collective-permute-start | bytes 393224 | tf_op jit(solution)/shard_map/ppermute | solution.py:41
  291.6 2.4 collective-permute-start.72
  294.0 2.6 collective-permute-start.53
  302.0 2.3 collective-permute-start.83
  306.6 7.6 %collective-permute-start.78 = (bf16[64,1024]{1,0:T(8,128)(2,1)S(1)}, bf16[64,1024]{1,0:T(8,128)(2,1)S(1)}, u32[]{:S(2)}, u32[]{:S(2)}) collective-permute-start(bf16[64,1024]{1,0:T(8,128)(2,1)S(1)} %get-tuple-element.163), channel_id=1, source_target_pairs={{32,8},{33,9},{34,10},{35,11},{36,12},{37,13},{38,14},{39,15},{40,... | collective-permute-start | bytes 393224 | tf_op jit(solution)/shard_map/ppermute | solution.py:41
  318.3 2.2 collective-permute-start.77
  320.6 3.9 collective-permute-done.79.c2
  326.4 6.5 %collective-permute-done.80.c3 = bf16[64,1024]{1,0:T(8,128)(2,1)S(1)} collective-permute-done((bf16[64,1024]{1,0:T(8,128)(2,1)S(1)}, bf16[64,1024]{1,0:T(8,128)(2,1)S(1)}, u32[]{:S(2)}, u32[]{:S(2)}) %collective-permute-start.80) | collective-permute-done | bytes 131104 | tf_op jit(solution)/shard_map/ppermute | solution.py:41
  332.9 4.5 backward_step.15
  351.7 13.2 %collective-permute-done.87.c3 = bf16[64,1024]{1,0:T(8,128)(2,1)S(1)} collective-permute-done((bf16[64,1024]{1,0:T(8,128)(2,1)S(1)}, bf16[64,1024]{1,0:T(8,128)(2,1)S(1)}, u32[]{:S(2)}, u32[]{:S(2)}) %collective-permute-start.87) | collective-permute-done | bytes 131104 | tf_op jit(solution)/shard_map/ppermute | solution.py:41
  364.9 4.5 backward_step.16
  379.3 8.7 %collective-permute-start.94 = (bf16[64,1024]{1,0:T(8,128)(2,1)S(1)}, bf16[64,1024]{1,0:T(8,128)(2,1)S(1)}, u32[]{:S(2)}, u32[]{:S(2)}) collective-permute-start(bf16[64,1024]{1,0:T(8,128)(2,1)S(1)} %get-tuple-element.175), channel_id=1, source_target_pairs={{0,124},{1,125},{2,126},{3,127},{4,120},{5,121},{6,122},{7,123},{8... | collective-permute-start | bytes 393224 | tf_op jit(solution)/shard_map/ppermute | solution.py:41
  388.1 3.1 collective-permute-done.94.c3
  392.8 5.2 %collective-permute-done.98 = bf16[128,1024]{1,0:T(8,128)(2,1)S(1)} collective-permute-done((bf16[128,1024]{1,0:T(8,128)(2,1)S(1)}, bf16[128,1024]{1,0:T(8,128)(2,1)S(1)}, u32[]{:S(2)}, u32[]{:S(2)}) %collective-permute-start.98) | collective-permute-done | bytes 262176 | tf_op jit(solution)/shard_map/ppermute | solution.py:41
  398.1 2.8 collective-permute-start.101
  401.6 7.4 %collective-permute-done.101.refs_3_ = bf16[256,1024]{1,0:T(8,128)(2,1)S(1)} collective-permute-done((bf16[256,1024]{1,0:T(8,128)(2,1)S(1)}, bf16[256,1024]{1,0:T(8,128)(2,1)S(1)}, u32[]{:S(2)}, u32[]{:S(2)}) %collective-permute-start.101) | collective-permute-done | bytes 524320 | tf_op jit(solution)/shard_map/ppermute | solution.py:41
  409.0 2.6 collective-permute-done.100.refs_2_
  411.5 15.9 %collective-permute-done.99.refs_1_ = bf16[256,1024]{1,0:T(8,128)(2,1)S(1)} collective-permute-done((bf16[256,1024]{1,0:T(8,128)(2,1)S(1)}, bf16[256,1024]{1,0:T(8,128)(2,1)S(1)}, u32[]{:S(2)}, u32[]{:S(2)}) %collective-permute-start.99) | collective-permute-done | bytes 524320 | tf_op jit(solution)/shard_map/ppermute | solution.py:41
  430.2 3.0 collective-permute-start.103
  433.2 5.1 %collective-permute-done.104.refs_7_ = bf16[1024,128]{1,0:T(8,128)(2,1)S(1)} collective-permute-done((bf16[1024,128]{1,0:T(8,128)(2,1)S(1)}, bf16[1024,128]{1,0:T(8,128)(2,1)S(1)}, u32[]{:S(2)}, u32[]{:S(2)}) %collective-permute-start.104) | collective-permute-done | bytes 262176 | tf_op jit(solution)/shard_map/ppermute | solution.py:41
  438.2 6.5 %collective-permute-done.103.refs_6_ = bf16[1024,128]{1,0:T(8,128)(2,1)S(1)} collective-permute-done((bf16[1024,128]{1,0:T(8,128)(2,1)S(1)}, bf16[1024,128]{1,0:T(8,128)(2,1)S(1)}, u32[]{:S(2)}, u32[]{:S(2)}) %collective-permute-start.103) | collective-permute-done | bytes 262176 | tf_op jit(solution)/shard_map/ppermute | solution.py:41
  449.8 4.8 %assemble.2 = bf16[128,2,4096]{2,1,0:T(2,128)(2,1)} custom-call(s32[3]{0:T(128)S(1)} %pad_add_fusion.meta_ref.refs_0_, bf16[128,1024]{1,0:T(8,128)(2,1)S(1)} %get-tuple-element.115.refs_0_, bf16[128,1024]{1,0:T(8,128)(2,1)S(1)} %collective-permute-done.26.refs_1_, bf16[128,1024]{1,0:T(8,128)(2,1)S(1)} %collective-permute-done.27.refs_2_, ...), custom_call_target="tpu_custom_call" | custom-call | tf_op jit(solution)/shard_map/assemble/pallas_call | solution.py:410
  456.1 7.1 %collective-permute-done.107.refs_3_ = bf16[128,1024]{1,0:T(8,128)(2,1)S(1)} collective-permute-done((bf16[128,1024]{1,0:T(8,128)(2,1)S(1)}, bf16[128,1024]{1,0:T(8,128)(2,1)S(1)}, u32[]{:S(2)}, u32[]{:S(2)}) %collective-permute-start.107) | collective-permute-done | bytes 262176 | tf_op jit(solution)/shard_map/ppermute | solution.py:41
  463.2 4.8 %assemble.3 = bf16[128,2,4096]{2,1,0:T(2,128)(2,1)} custom-call(s32[3]{0:T(128)S(1)} %pad_add_fusion.meta_ref.refs_0_, bf16[128,1024]{1,0:T(8,128)(2,1)S(1)} %get-tuple-element.181.refs_0_, bf16[128,1024]{1,0:T(8,128)(2,1)S(1)} %collective-permute-done.105.refs_1_, bf16[128,1024]{1,0:T(8,128)(2,1)S(1)} %collective-permute-done.106.refs_2_, ...), custom_call_target="tpu_custom_call" | custom-call | tf_op jit(solution)/shard_map/assemble/pallas_call | solution.py:410
  (195 shorter events, 155.1 us)
Async XLA Ops:
  1.6 10.9 %collective-permute-start.2 = (bf16[32,4096]{1,0:T(8,128)(2,1)S(1)}, bf16[32,4096]{1,0:T(8,128)(2,1)S(1)}, u32[]{:S(2)}, u32[]{:S(2)}) collective-permute-start(bf16[32,4096]{1,0:T(8,128)(2,1)S(1)} %bitcast.15), channel_id=1, source_target_pairs={{0,24},{1,25},{2,26},{3,27},{4,28},{5,29},{6,30},{7,31},{8,0},{9,1... | collective-permute-start | bytes 786440 | tf_op jit(solution)/shard_map/ppermute | solution.py:41
  1.7 13.7 %collective-permute-start.1 = (bf16[32,4096]{1,0:T(8,128)(2,1)S(1)}, bf16[32,4096]{1,0:T(8,128)(2,1)S(1)}, u32[]{:S(2)}, u32[]{:S(2)}) collective-permute-start(bf16[32,4096]{1,0:T(8,128)(2,1)S(1)} %bitcast.16), channel_id=1, source_target_pairs={{0,16},{1,17},{2,18},{3,19},{4,20},{5,21},{6,22},{7,23},{8,24},{9,... | collective-permute-start | bytes 786440 | tf_op jit(solution)/shard_map/ppermute | solution.py:41
  4.1 12.2 %collective-permute-start = (bf16[32,4096]{1,0:T(8,128)(2,1)S(1)}, bf16[32,4096]{1,0:T(8,128)(2,1)S(1)}, u32[]{:S(2)}, u32[]{:S(2)}) collective-permute-start(bf16[32,4096]{1,0:T(8,128)(2,1)S(1)} %bitcast.17), channel_id=1, source_target_pairs={{0,8},{1,9},{2,10},{3,11},{4,12},{5,13},{6,14},{7,15},{8,16},{9,17... | collective-permute-start | bytes 786440 | tf_op jit(solution)/shard_map/ppermute | solution.py:41
  20.3 12.3 %collective-permute-start.4 = (bf16[64,1024]{1,0:T(8,128)(2,1)S(1)}, bf16[64,1024]{1,0:T(8,128)(2,1)S(1)}, u32[]{:S(2)}, u32[]{:S(2)}) collective-permute-start(bf16[64,1024]{1,0:T(8,128)(2,1)S(1)} %get-tuple-element.98), channel_id=1, source_target_pairs={{0,40},{1,41},{2,42},{3,43},{4,44},{5,45},{6,46},{7,47},{8,48},{9,... | collective-permute-start | bytes 393224 | tf_op jit(solution)/shard_map/ppermute | solution.py:41
  21.6 11.0 %collective-permute-start.3 = (bf16[64,1024]{1,0:T(8,128)(2,1)S(1)}, bf16[64,1024]{1,0:T(8,128)(2,1)S(1)}, u32[]{:S(2)}, u32[]{:S(2)}) collective-permute-start(bf16[64,1024]{1,0:T(8,128)(2,1)S(1)} %get-tuple-element.98), channel_id=1, source_target_pairs={{0,32},{1,33},{2,34},{3,35},{4,36},{5,37},{6,38},{7,39},{8,40},{9,... | collective-permute-start | bytes 393224 | tf_op jit(solution)/shard_map/ppermute | solution.py:41
  35.5 13.0 %collective-permute-start.10 = (bf16[64,1024]{1,0:T(8,128)(2,1)S(1)}, bf16[64,1024]{1,0:T(8,128)(2,1)S(1)}, u32[]{:S(2)}, u32[]{:S(2)}) collective-permute-start(bf16[64,1024]{1,0:T(8,128)(2,1)S(1)} %get-tuple-element.105), channel_id=1, source_target_pairs={{0,56},{1,57},{2,58},{3,59},{4,60},{5,61},{6,62},{7,63},{8,32},{9,... | collective-permute-start | bytes 393224 | tf_op jit(solution)/shard_map/ppermute | solution.py:41
  54.5 12.6 %collective-permute-start.14 = (bf16[64,1024]{1,0:T(8,128)(2,1)S(1)}, bf16[64,1024]{1,0:T(8,128)(2,1)S(1)}, u32[]{:S(2)}, u32[]{:S(2)}) collective-permute-start(bf16[64,1024]{1,0:T(8,128)(2,1)S(1)} %get-tuple-element.108), channel_id=1, source_target_pairs={{0,56},{1,57},{2,58},{3,59},{4,60},{5,61},{6,62},{7,63},{8,32},{9,... | collective-permute-start | bytes 393224 | tf_op jit(solution)/shard_map/ppermute | solution.py:41
  83.3 13.8 %collective-permute-start.32 = (bf16[64,1024]{1,0:T(8,128)(2,1)S(1)}, bf16[64,1024]{1,0:T(8,128)(2,1)S(1)}, u32[]{:S(2)}, u32[]{:S(2)}) collective-permute-start(bf16[64,1024]{1,0:T(8,128)(2,1)S(1)} %get-tuple-element.119), channel_id=1, source_target_pairs={{0,56},{1,57},{2,58},{3,59},{4,60},{5,61},{6,62},{7,63},{8,32},{9,... | collective-permute-start | bytes 393224 | tf_op jit(solution)/shard_map/ppermute | solution.py:41
  84.6 15.0 %collective-permute-start.31 = (bf16[64,1024]{1,0:T(8,128)(2,1)S(1)}, bf16[64,1024]{1,0:T(8,128)(2,1)S(1)}, u32[]{:S(2)}, u32[]{:S(2)}) collective-permute-start(bf16[64,1024]{1,0:T(8,128)(2,1)S(1)} %get-tuple-element.119), channel_id=1, source_target_pairs={{0,48},{1,49},{2,50},{3,51},{4,52},{5,53},{6,54},{7,55},{8,56},{9,... | collective-permute-start | bytes 393224 | tf_op jit(solution)/shard_map/ppermute | solution.py:41
  88.5 43.0 %collective-permute-start.22 = (bf16[256,1024]{1,0:T(8,128)(2,1)S(1)}, bf16[256,1024]{1,0:T(8,128)(2,1)S(1)}, u32[]{:S(2)}, u32[]{:S(2)}) collective-permute-start(bf16[256,1024]{1,0:T(8,128)(2,1)S(1)} %pad_maximum_fusion.refs_0_.refs_2_), channel_id=1, source_target_pairs={{0,3},{1,0},{2,1},{3,2},{4,7},{5,4},{6,5},{7,6},{8,11},{9,8},{10,9... | collective-permute-start | bytes 1572872 | tf_op jit(solution)/shard_map/ppermute | solution.py:41
  91.3 40.2 %collective-permute-start.21 = (bf16[256,1024]{1,0:T(8,128)(2,1)S(1)}, bf16[256,1024]{1,0:T(8,128)(2,1)S(1)}, u32[]{:S(2)}, u32[]{:S(2)}) collective-permute-start(bf16[256,1024]{1,0:T(8,128)(2,1)S(1)} %pad_maximum_fusion.refs_0_.refs_2_), channel_id=1, source_target_pairs={{0,2},{1,3},{2,0},{3,1},{4,6},{5,7},{6,4},{7,5},{8,10},{9,11},{10,... | collective-permute-start | bytes 1572872 | tf_op jit(solution)/shard_map/ppermute | solution.py:41
  91.7 39.9 %collective-permute-start.20 = (bf16[256,1024]{1,0:T(8,128)(2,1)S(1)}, bf16[256,1024]{1,0:T(8,128)(2,1)S(1)}, u32[]{:S(2)}, u32[]{:S(2)}) collective-permute-start(bf16[256,1024]{1,0:T(8,128)(2,1)S(1)} %pad_maximum_fusion.refs_0_.refs_2_), channel_id=1, source_target_pairs={{0,1},{1,2},{2,3},{3,0},{4,5},{5,6},{6,7},{7,4},{8,9},{9,10},{10,1... | collective-permute-start | bytes 1572872 | tf_op jit(solution)/shard_map/ppermute | solution.py:41
  97.1 11.8 %collective-permute-start.30 = (bf16[64,1024]{1,0:T(8,128)(2,1)S(1)}, bf16[64,1024]{1,0:T(8,128)(2,1)S(1)}, u32[]{:S(2)}, u32[]{:S(2)}) collective-permute-start(bf16[64,1024]{1,0:T(8,128)(2,1)S(1)} %get-tuple-element.119), channel_id=1, source_target_pairs={{0,40},{1,41},{2,42},{3,43},{4,44},{5,45},{6,46},{7,47},{8,48},{9,... | collective-permute-start | bytes 393224 | tf_op jit(solution)/shard_map/ppermute | solution.py:41
  134.6 13.3 %collective-permute-start.40 = (bf16[64,1024]{1,0:T(8,128)(2,1)S(1)}, bf16[64,1024]{1,0:T(8,128)(2,1)S(1)}, u32[]{:S(2)}, u32[]{:S(2)}) collective-permute-start(bf16[64,1024]{1,0:T(8,128)(2,1)S(1)} %get-tuple-element.124), channel_id=1, source_target_pairs={{0,56},{1,57},{2,58},{3,59},{4,60},{5,61},{6,62},{7,63},{8,32},{9,... | collective-permute-start | bytes 393224 | tf_op jit(solution)/shard_map/ppermute | solution.py:41
  146.0 12.5 %collective-permute-start.24 = (bf16[1024,128]{1,0:T(8,128)(2,1)S(1)}, bf16[1024,128]{1,0:T(8,128)(2,1)S(1)}, u32[]{:S(2)}, u32[]{:S(2)}) collective-permute-start(bf16[1024,128]{1,0:T(8,128)(2,1)S(1)} %own_columns.4.refs_4_), channel_id=1, source_target_pairs={{0,16},{1,17},{2,18},{3,19},{4,20},{5,21},{6,22},{7,23},{8,24},{9,... | collective-permute-start | bytes 786440 | tf_op jit(solution)/shard_map/ppermute | solution.py:41
  147.9 12.6 %collective-permute-start.23 = (bf16[1024,128]{1,0:T(8,128)(2,1)S(1)}, bf16[1024,128]{1,0:T(8,128)(2,1)S(1)}, u32[]{:S(2)}, u32[]{:S(2)}) collective-permute-start(bf16[1024,128]{1,0:T(8,128)(2,1)S(1)} %own_columns.4.refs_4_), channel_id=1, source_target_pairs={{0,8},{1,9},{2,10},{3,11},{4,12},{5,13},{6,14},{7,15},{8,16},{9,17... | collective-permute-start | bytes 786440 | tf_op jit(solution)/shard_map/ppermute | solution.py:41
  149.4 11.8 %collective-permute-start.55 = (bf16[2,64,1024]{2,1,0:T(8,128)(2,1)S(1)}, bf16[2,64,1024]{2,1,0:T(8,128)(2,1)S(1)}, u32[]{:S(2)}, u32[]{:S(2)}) collective-permute-start(bf16[2,64,1024]{2,1,0:T(8,128)(2,1)S(1)} %get-tuple-element.135), channel_id=1, source_target_pairs={{0,4},{1,5},{2,6},{3,7},{4,0},{5,1},{6,2},{7,3},{8,12},{9,13},{10,... | collective-permute-start | bytes 786440 | tf_op jit(solution)/shard_map/ppermute | solution.py:41
  166.7 12.3 %collective-permute-start.44 = (bf16[64,1024]{1,0:T(8,128)(2,1)S(1)}, bf16[64,1024]{1,0:T(8,128)(2,1)S(1)}, u32[]{:S(2)}, u32[]{:S(2)}) collective-permute-start(bf16[64,1024]{1,0:T(8,128)(2,1)S(1)} %get-tuple-element.127), channel_id=1, source_target_pairs={{0,56},{1,57},{2,58},{3,59},{4,60},{5,61},{6,62},{7,63},{8,32},{9,... | collective-permute-start | bytes 393224 | tf_op jit(solution)/shard_map/ppermute | solution.py:41
  168.0 19.8 %collective-permute-start.43 = (bf16[64,1024]{1,0:T(8,128)(2,1)S(1)}, bf16[64,1024]{1,0:T(8,128)(2,1)S(1)}, u32[]{:S(2)}, u32[]{:S(2)}) collective-permute-start(bf16[64,1024]{1,0:T(8,128)(2,1)S(1)} %get-tuple-element.127), channel_id=1, source_target_pairs={{0,48},{1,49},{2,50},{3,51},{4,52},{5,53},{6,54},{7,55},{8,56},{9,... | collective-permute-start | bytes 393224 | tf_op jit(solution)/shard_map/ppermute | solution.py:41
  169.3 22.1 %collective-permute-start.42 = (bf16[64,1024]{1,0:T(8,128)(2,1)S(1)}, bf16[64,1024]{1,0:T(8,128)(2,1)S(1)}, u32[]{:S(2)}, u32[]{:S(2)}) collective-permute-start(bf16[64,1024]{1,0:T(8,128)(2,1)S(1)} %get-tuple-element.127), channel_id=1, source_target_pairs={{0,40},{1,41},{2,42},{3,43},{4,44},{5,45},{6,46},{7,47},{8,48},{9,... | collective-permute-start | bytes 393224 | tf_op jit(solution)/shard_map/ppermute | solution.py:41
  170.6 21.2 %collective-permute-start.41 = (bf16[64,1024]{1,0:T(8,128)(2,1)S(1)}, bf16[64,1024]{1,0:T(8,128)(2,1)S(1)}, u32[]{:S(2)}, u32[]{:S(2)}) collective-permute-start(bf16[64,1024]{1,0:T(8,128)(2,1)S(1)} %get-tuple-element.127), channel_id=1, source_target_pairs={{0,32},{1,33},{2,34},{3,35},{4,36},{5,37},{6,38},{7,39},{8,40},{9,... | collective-permute-start | bytes 393224 | tf_op jit(solution)/shard_map/ppermute | solution.py:41
  171.9 24.1 %collective-permute-start.58 = (bf16[64,1024]{1,0:T(8,128)(2,1)S(1)}, bf16[64,1024]{1,0:T(8,128)(2,1)S(1)}, u32[]{:S(2)}, u32[]{:S(2)}) collective-permute-start(bf16[64,1024]{1,0:T(8,128)(2,1)S(1)} %get-tuple-element.138), channel_id=1, source_target_pairs={{0,116},{1,117},{2,118},{3,119},{4,112},{5,113},{6,114},{7,115},{8... | collective-permute-start | bytes 393224 | tf_op jit(solution)/shard_map/ppermute | solution.py:41
  178.9 17.3 %collective-permute-start.56 = (f32[64,1024]{1,0:T(8,128)S(1)}, f32[64,1024]{1,0:T(8,128)S(1)}, u32[]{:S(2)}, u32[]{:S(2)}) collective-permute-start(f32[64,1024]{1,0:T(8,128)S(1)} %get-tuple-element.136), channel_id=1, source_target_pairs={{0,100},{1,101},{2,102},{3,103},{4,96},{5,97},{6,98},{7,99},{8,108... | collective-permute-start | bytes 786440 | tf_op jit(solution)/shard_map/ppermute | solution.py:41
  196.0 13.8 %collective-permute-start.45 = (bf16[128,1024]{1,0:T(8,128)(2,1)S(1)}, bf16[128,1024]{1,0:T(8,128)(2,1)S(1)}, u32[]{:S(2)}, u32[]{:S(2)}) collective-permute-start(bf16[128,1024]{1,0:T(8,128)(2,1)S(1)} %bitcast.22), channel_id=1, source_target_pairs={{0,4},{1,5},{2,6},{3,7},{4,0},{5,1},{6,2},{7,3},{8,12},{9,13},{10,... | collective-permute-start | bytes 786440 | tf_op jit(solution)/shard_map/ppermute | solution.py:41
  196.1 16.7 %collective-permute-start.28 = (bf16[128,1024]{1,0:T(8,128)(2,1)S(1)}, bf16[128,1024]{1,0:T(8,128)(2,1)S(1)}, u32[]{:S(2)}, u32[]{:S(2)}) collective-permute-start(bf16[128,1024]{1,0:T(8,128)(2,1)S(1)} %get-tuple-element.118), channel_id=1, source_target_pairs={{0,24},{1,25},{2,26},{3,27},{4,28},{5,29},{6,30},{7,31},{8,0},{9,1... | collective-permute-start | bytes 786440 | tf_op jit(solution)/shard_map/ppermute | solution.py:41
  197.0 23.0 %collective-permute-start.60 = (f32[64,1024]{1,0:T(8,128)S(1)}, f32[64,1024]{1,0:T(8,128)S(1)}, u32[]{:S(2)}, u32[]{:S(2)}) collective-permute-start(f32[64,1024]{1,0:T(8,128)S(1)} %get-tuple-element.142), channel_id=1, source_target_pairs={{32,0},{33,1},{34,2},{35,3},{36,4},{37,5},{38,6},{39,7},{40,8},{41... | collective-permute-start | bytes 786440 | tf_op jit(solution)/shard_map/ppermute | solution.py:41
  200.2 14.7 %collective-permute-start.61 = (bf16[64,1024]{1,0:T(8,128)(2,1)S(1)}, bf16[64,1024]{1,0:T(8,128)(2,1)S(1)}, u32[]{:S(2)}, u32[]{:S(2)}) collective-permute-start(bf16[64,1024]{1,0:T(8,128)(2,1)S(1)} %get-tuple-element.143), channel_id=1, source_target_pairs={{32,8},{33,9},{34,10},{35,11},{36,12},{37,13},{38,14},{39,15},{40,... | collective-permute-start | bytes 393224 | tf_op jit(solution)/shard_map/ppermute | solution.py:41
  202.3 16.0 %collective-permute-start.62 = (bf16[64,1024]{1,0:T(8,128)(2,1)S(1)}, bf16[64,1024]{1,0:T(8,128)(2,1)S(1)}, u32[]{:S(2)}, u32[]{:S(2)}) collective-permute-start(bf16[64,1024]{1,0:T(8,128)(2,1)S(1)} %get-tuple-element.144), channel_id=1, source_target_pairs={{32,16},{33,17},{34,18},{35,19},{36,20},{37,21},{38,22},{39,23},{4... | collective-permute-start | bytes 393224 | tf_op jit(solution)/shard_map/ppermute | solution.py:41
  212.8 35.5 %collective-permute-start.48 = (bf16[256,1024]{1,0:T(8,128)(2,1)S(1)}, bf16[256,1024]{1,0:T(8,128)(2,1)S(1)}, u32[]{:S(2)}, u32[]{:S(2)}) collective-permute-start(bf16[256,1024]{1,0:T(8,128)(2,1)S(1)} %pad_maximum_fusion.1.refs_0_.refs_4_), channel_id=1, source_target_pairs={{0,3},{1,0},{2,1},{3,2},{4,7},{5,4},{6,5},{7,6},{8,11},{9,8},{10,9... | collective-permute-start | bytes 1572872 | tf_op jit(solution)/shard_map/ppermute | solution.py:41
  214.9 33.5 %collective-permute-start.47 = (bf16[256,1024]{1,0:T(8,128)(2,1)S(1)}, bf16[256,1024]{1,0:T(8,128)(2,1)S(1)}, u32[]{:S(2)}, u32[]{:S(2)}) collective-permute-start(bf16[256,1024]{1,0:T(8,128)(2,1)S(1)} %pad_maximum_fusion.1.refs_0_.refs_4_), channel_id=1, source_target_pairs={{0,2},{1,3},{2,0},{3,1},{4,6},{5,7},{6,4},{7,5},{8,10},{9,11},{10,... | collective-permute-start | bytes 1572872 | tf_op jit(solution)/shard_map/ppermute | solution.py:41
  218.3 30.0 %collective-permute-start.46 = (bf16[256,1024]{1,0:T(8,128)(2,1)S(1)}, bf16[256,1024]{1,0:T(8,128)(2,1)S(1)}, u32[]{:S(2)}, u32[]{:S(2)}) collective-permute-start(bf16[256,1024]{1,0:T(8,128)(2,1)S(1)} %pad_maximum_fusion.1.refs_0_.refs_4_), channel_id=1, source_target_pairs={{0,1},{1,2},{2,3},{3,0},{4,5},{5,6},{6,7},{7,4},{8,9},{9,10},{10,1... | collective-permute-start | bytes 1572872 | tf_op jit(solution)/shard_map/ppermute | solution.py:41
  226.5 13.5 %collective-permute-start.66 = (bf16[64,1024]{1,0:T(8,128)(2,1)S(1)}, bf16[64,1024]{1,0:T(8,128)(2,1)S(1)}, u32[]{:S(2)}, u32[]{:S(2)}) collective-permute-start(bf16[64,1024]{1,0:T(8,128)(2,1)S(1)} %get-tuple-element.149), channel_id=1, source_target_pairs={{32,16},{33,17},{34,18},{35,19},{36,20},{37,21},{38,22},{39,23},{4... | collective-permute-start | bytes 393224 | tf_op jit(solution)/shard_map/ppermute | solution.py:41
  234.2 14.2 %collective-permute-start.64 = (f32[64,1024]{1,0:T(8,128)S(1)}, f32[64,1024]{1,0:T(8,128)S(1)}, u32[]{:S(2)}, u32[]{:S(2)}) collective-permute-start(f32[64,1024]{1,0:T(8,128)S(1)} %get-tuple-element.147), channel_id=1, source_target_pairs={{32,0},{33,1},{34,2},{35,3},{36,4},{37,5},{38,6},{39,7},{40,8},{41... | collective-permute-start | bytes 786440 | tf_op jit(solution)/shard_map/ppermute | solution.py:41
  256.7 19.4 %collective-permute-start.51 = (bf16[1024,128]{1,0:T(8,128)(2,1)S(1)}, bf16[1024,128]{1,0:T(8,128)(2,1)S(1)}, u32[]{:S(2)}, u32[]{:S(2)}) collective-permute-start(bf16[1024,128]{1,0:T(8,128)(2,1)S(1)} %own_columns.5.refs_4_), channel_id=1, source_target_pairs={{0,24},{1,25},{2,26},{3,27},{4,28},{5,29},{6,30},{7,31},{8,0},{9,1... | collective-permute-start | bytes 786440 | tf_op jit(solution)/shard_map/ppermute | solution.py:41
  258.7 17.4 %collective-permute-start.50 = (bf16[1024,128]{1,0:T(8,128)(2,1)S(1)}, bf16[1024,128]{1,0:T(8,128)(2,1)S(1)}, u32[]{:S(2)}, u32[]{:S(2)}) collective-permute-start(bf16[1024,128]{1,0:T(8,128)(2,1)S(1)} %own_columns.5.refs_4_), channel_id=1, source_target_pairs={{0,16},{1,17},{2,18},{3,19},{4,20},{5,21},{6,22},{7,23},{8,24},{9,... | collective-permute-start | bytes 786440 | tf_op jit(solution)/shard_map/ppermute | solution.py:41
  260.2 15.9 %collective-permute-start.49 = (bf16[1024,128]{1,0:T(8,128)(2,1)S(1)}, bf16[1024,128]{1,0:T(8,128)(2,1)S(1)}, u32[]{:S(2)}, u32[]{:S(2)}) collective-permute-start(bf16[1024,128]{1,0:T(8,128)(2,1)S(1)} %own_columns.5.refs_4_), channel_id=1, source_target_pairs={{0,8},{1,9},{2,10},{3,11},{4,12},{5,13},{6,14},{7,15},{8,16},{9,17... | collective-permute-start | bytes 786440 | tf_op jit(solution)/shard_map/ppermute | solution.py:41
  262.2 13.9 %collective-permute-start.68 = (f32[64,1024]{1,0:T(8,128)S(1)}, f32[64,1024]{1,0:T(8,128)S(1)}, u32[]{:S(2)}, u32[]{:S(2)}) collective-permute-start(f32[64,1024]{1,0:T(8,128)S(1)} %get-tuple-element.152), channel_id=1, source_target_pairs={{0,100},{1,101},{2,102},{3,103},{4,96},{5,97},{6,98},{7,99},{8,108... | collective-permute-start | bytes 786440 | tf_op jit(solution)/shard_map/ppermute | solution.py:41
  263.5 12.6 %collective-permute-start.71 = (bf16[64,1024]{1,0:T(8,128)(2,1)S(1)}, bf16[64,1024]{1,0:T(8,128)(2,1)S(1)}, u32[]{:S(2)}, u32[]{:S(2)}) collective-permute-start(bf16[64,1024]{1,0:T(8,128)(2,1)S(1)} %get-tuple-element.155), channel_id=1, source_target_pairs={{0,124},{1,125},{2,126},{3,127},{4,120},{5,121},{6,122},{7,123},{8... | collective-permute-start | bytes 393224 | tf_op jit(solution)/shard_map/ppermute | solution.py:41
  276.8 21.3 %collective-permute-start.76 = (bf16[128,1024]{1,0:T(8,128)(2,1)S(1)}, bf16[128,1024]{1,0:T(8,128)(2,1)S(1)}, u32[]{:S(2)}, u32[]{:S(2)}) collective-permute-start(bf16[128,1024]{1,0:T(8,128)(2,1)S(1)} %bitcast.24), channel_id=1, source_target_pairs={{0,4},{1,5},{2,6},{3,7},{4,0},{5,1},{6,2},{7,3},{8,12},{9,13},{10,... | collective-permute-start | bytes 786440 | tf_op jit(solution)/shard_map/ppermute | solution.py:41
  276.9 17.1 %collective-permute-start.73 = (bf16[64,1024]{1,0:T(8,128)(2,1)S(1)}, bf16[64,1024]{1,0:T(8,128)(2,1)S(1)}, u32[]{:S(2)}, u32[]{:S(2)}) collective-permute-start(bf16[64,1024]{1,0:T(8,128)(2,1)S(1)} %get-tuple-element.158), channel_id=1, source_target_pairs={{0,108},{1,109},{2,110},{3,111},{4,104},{5,105},{6,106},{7,107},{8... | collective-permute-start | bytes 393224 | tf_op jit(solution)/shard_map/ppermute | solution.py:41
  283.1 13.6 %collective-permute-start.74 = (bf16[64,1024]{1,0:T(8,128)(2,1)S(1)}, bf16[64,1024]{1,0:T(8,128)(2,1)S(1)}, u32[]{:S(2)}, u32[]{:S(2)}) collective-permute-start(bf16[64,1024]{1,0:T(8,128)(2,1)S(1)} %get-tuple-element.159), channel_id=1, source_target_pairs={{0,116},{1,117},{2,118},{3,119},{4,112},{5,113},{6,114},{7,115},{8... | collective-permute-start | bytes 393224 | tf_op jit(solution)/shard_map/ppermute | solution.py:41
  291.5 12.8 %collective-permute-start.52 = (bf16[128,1024]{1,0:T(8,128)(2,1)S(1)}, bf16[128,1024]{1,0:T(8,128)(2,1)S(1)}, u32[]{:S(2)}, u32[]{:S(2)}) collective-permute-start(bf16[128,1024]{1,0:T(8,128)(2,1)S(1)} %get-tuple-element.132), channel_id=1, source_target_pairs={{0,8},{1,9},{2,10},{3,11},{4,12},{5,13},{6,14},{7,15},{8,16},{9,17... | collective-permute-start | bytes 786440 | tf_op jit(solution)/shard_map/ppermute | solution.py:41
  291.6 14.3 %collective-permute-start.72 = (f32[64,1024]{1,0:T(8,128)S(1)}, f32[64,1024]{1,0:T(8,128)S(1)}, u32[]{:S(2)}, u32[]{:S(2)}) collective-permute-start(f32[64,1024]{1,0:T(8,128)S(1)} %get-tuple-element.157), channel_id=1, source_target_pairs={{0,100},{1,101},{2,102},{3,103},{4,96},{5,97},{6,98},{7,99},{8,108... | collective-permute-start | bytes 786440 | tf_op jit(solution)/shard_map/ppermute | solution.py:41
  294.0 12.6 %collective-permute-start.53 = (bf16[128,1024]{1,0:T(8,128)(2,1)S(1)}, bf16[128,1024]{1,0:T(8,128)(2,1)S(1)}, u32[]{:S(2)}, u32[]{:S(2)}) collective-permute-start(bf16[128,1024]{1,0:T(8,128)(2,1)S(1)} %get-tuple-element.133), channel_id=1, source_target_pairs={{0,16},{1,17},{2,18},{3,19},{4,20},{5,21},{6,22},{7,23},{8,24},{9,... | collective-permute-start | bytes 786440 | tf_op jit(solution)/shard_map/ppermute | solution.py:41
  298.1 16.1 %collective-permute-start.54 = (bf16[128,1024]{1,0:T(8,128)(2,1)S(1)}, bf16[128,1024]{1,0:T(8,128)(2,1)S(1)}, u32[]{:S(2)}, u32[]{:S(2)}) collective-permute-start(bf16[128,1024]{1,0:T(8,128)(2,1)S(1)} %get-tuple-element.134), channel_id=1, source_target_pairs={{0,24},{1,25},{2,26},{3,27},{4,28},{5,29},{6,30},{7,31},{8,0},{9,1... | collective-permute-start | bytes 786440 | tf_op jit(solution)/shard_map/ppermute | solution.py:41
  302.0 30.9 %collective-permute-start.83 = (bf16[256,1024]{1,0:T(8,128)(2,1)S(1)}, bf16[256,1024]{1,0:T(8,128)(2,1)S(1)}, u32[]{:S(2)}, u32[]{:S(2)}) collective-permute-start(bf16[256,1024]{1,0:T(8,128)(2,1)S(1)} %pad_maximum_fusion.2.refs_1_.refs_0_), channel_id=1, source_target_pairs={{0,3},{1,0},{2,1},{3,2},{4,7},{5,4},{6,5},{7,6},{8,11},{9,8},{10,9... | collective-permute-start | bytes 1572872 | tf_op jit(solution)/shard_map/ppermute | solution.py:41
  304.3 28.5 %collective-permute-start.82 = (bf16[256,1024]{1,0:T(8,128)(2,1)S(1)}, bf16[256,1024]{1,0:T(8,128)(2,1)S(1)}, u32[]{:S(2)}, u32[]{:S(2)}) collective-permute-start(bf16[256,1024]{1,0:T(8,128)(2,1)S(1)} %pad_maximum_fusion.2.refs_1_.refs_0_), channel_id=1, source_target_pairs={{0,2},{1,3},{2,0},{3,1},{4,6},{5,7},{6,4},{7,5},{8,10},{9,11},{10,... | collective-permute-start | bytes 1572872 | tf_op jit(solution)/shard_map/ppermute | solution.py:41
  305.9 27.0 %collective-permute-start.81 = (bf16[256,1024]{1,0:T(8,128)(2,1)S(1)}, bf16[256,1024]{1,0:T(8,128)(2,1)S(1)}, u32[]{:S(2)}, u32[]{:S(2)}) collective-permute-start(bf16[256,1024]{1,0:T(8,128)(2,1)S(1)} %pad_maximum_fusion.2.refs_1_.refs_0_), channel_id=1, source_target_pairs={{0,1},{1,2},{2,3},{3,0},{4,5},{5,6},{6,7},{7,4},{8,9},{9,10},{10,1... | collective-permute-start | bytes 1572872 | tf_op jit(solution)/shard_map/ppermute | solution.py:41
  306.6 11.7 %collective-permute-start.78 = (bf16[64,1024]{1,0:T(8,128)(2,1)S(1)}, bf16[64,1024]{1,0:T(8,128)(2,1)S(1)}, u32[]{:S(2)}, u32[]{:S(2)}) collective-permute-start(bf16[64,1024]{1,0:T(8,128)(2,1)S(1)} %get-tuple-element.163), channel_id=1, source_target_pairs={{32,8},{33,9},{34,10},{35,11},{36,12},{37,13},{38,14},{39,15},{40,... | collective-permute-start | bytes 393224 | tf_op jit(solution)/shard_map/ppermute | solution.py:41
  318.3 14.5 %collective-permute-start.77 = (f32[64,1024]{1,0:T(8,128)S(1)}, f32[64,1024]{1,0:T(8,128)S(1)}, u32[]{:S(2)}, u32[]{:S(2)}) collective-permute-start(f32[64,1024]{1,0:T(8,128)S(1)} %get-tuple-element.162), channel_id=1, source_target_pairs={{32,0},{33,1},{34,2},{35,3},{36,4},{37,5},{38,6},{39,7},{40,8},{41... | collective-permute-start | bytes 786440 | tf_op jit(solution)/shard_map/ppermute | solution.py:41
  341.9 23.1 %collective-permute-start.90 = (bf16[1024,128]{1,0:T(8,128)(2,1)S(1)}, bf16[1024,128]{1,0:T(8,128)(2,1)S(1)}, u32[]{:S(2)}, u32[]{:S(2)}) collective-permute-start(bf16[1024,128]{1,0:T(8,128)(2,1)S(1)} %own_columns.6.refs_4_), channel_id=1, source_target_pairs={{0,24},{1,25},{2,26},{3,27},{4,28},{5,29},{6,30},{7,31},{8,0},{9,1... | collective-permute-start | bytes 786440 | tf_op jit(solution)/shard_map/ppermute | solution.py:41
  343.5 21.4 %collective-permute-start.89 = (bf16[1024,128]{1,0:T(8,128)(2,1)S(1)}, bf16[1024,128]{1,0:T(8,128)(2,1)S(1)}, u32[]{:S(2)}, u32[]{:S(2)}) collective-permute-start(bf16[1024,128]{1,0:T(8,128)(2,1)S(1)} %own_columns.6.refs_4_), channel_id=1, source_target_pairs={{0,16},{1,17},{2,18},{3,19},{4,20},{5,21},{6,22},{7,23},{8,24},{9,... | collective-permute-start | bytes 786440 | tf_op jit(solution)/shard_map/ppermute | solution.py:41
  345.2 19.7 %collective-permute-start.88 = (bf16[1024,128]{1,0:T(8,128)(2,1)S(1)}, bf16[1024,128]{1,0:T(8,128)(2,1)S(1)}, u32[]{:S(2)}, u32[]{:S(2)}) collective-permute-start(bf16[1024,128]{1,0:T(8,128)(2,1)S(1)} %own_columns.6.refs_4_), channel_id=1, source_target_pairs={{0,8},{1,9},{2,10},{3,11},{4,12},{5,13},{6,14},{7,15},{8,16},{9,17... | collective-permute-start | bytes 786440 | tf_op jit(solution)/shard_map/ppermute | solution.py:41
  346.0 19.0 %collective-permute-start.84 = (f32[64,1024]{1,0:T(8,128)S(1)}, f32[64,1024]{1,0:T(8,128)S(1)}, u32[]{:S(2)}, u32[]{:S(2)}) collective-permute-start(f32[64,1024]{1,0:T(8,128)S(1)} %get-tuple-element.167), channel_id=1, source_target_pairs={{32,0},{33,1},{34,2},{35,3},{36,4},{37,5},{38,6},{39,7},{40,8},{41... | collective-permute-start | bytes 786440 | tf_op jit(solution)/shard_map/ppermute | solution.py:41
  349.6 15.3 %collective-permute-start.87 = (bf16[64,1024]{1,0:T(8,128)(2,1)S(1)}, bf16[64,1024]{1,0:T(8,128)(2,1)S(1)}, u32[]{:S(2)}, u32[]{:S(2)}) collective-permute-start(bf16[64,1024]{1,0:T(8,128)(2,1)S(1)} %get-tuple-element.170), channel_id=1, source_target_pairs={{32,24},{33,25},{34,26},{35,27},{36,28},{37,29},{38,30},{39,31},{4... | collective-permute-start | bytes 393224 | tf_op jit(solution)/shard_map/ppermute | solution.py:41
  372.0 19.1 %collective-permute-start.95 = (bf16[128,1024]{1,0:T(8,128)(2,1)S(1)}, bf16[128,1024]{1,0:T(8,128)(2,1)S(1)}, u32[]{:S(2)}, u32[]{:S(2)}) collective-permute-start(bf16[128,1024]{1,0:T(8,128)(2,1)S(1)} %get-tuple-element.177), channel_id=1, source_target_pairs={{0,8},{1,9},{2,10},{3,11},{4,12},{5,13},{6,14},{7,15},{8,16},{9,17... | collective-permute-start | bytes 786440 | tf_op jit(solution)/shard_map/ppermute | solution.py:41
  373.4 17.7 %collective-permute-start.96 = (bf16[128,1024]{1,0:T(8,128)(2,1)S(1)}, bf16[128,1024]{1,0:T(8,128)(2,1)S(1)}, u32[]{:S(2)}, u32[]{:S(2)}) collective-permute-start(bf16[128,1024]{1,0:T(8,128)(2,1)S(1)} %get-tuple-element.178), channel_id=1, source_target_pairs={{0,16},{1,17},{2,18},{3,19},{4,20},{5,21},{6,22},{7,23},{8,24},{9,... | collective-permute-start | bytes 786440 | tf_op jit(solution)/shard_map/ppermute | solution.py:41
  375.6 15.5 %collective-permute-start.97 = (bf16[128,1024]{1,0:T(8,128)(2,1)S(1)}, bf16[128,1024]{1,0:T(8,128)(2,1)S(1)}, u32[]{:S(2)}, u32[]{:S(2)}) collective-permute-start(bf16[128,1024]{1,0:T(8,128)(2,1)S(1)} %get-tuple-element.179), channel_id=1, source_target_pairs={{0,24},{1,25},{2,26},{3,27},{4,28},{5,29},{6,30},{7,31},{8,0},{9,1... | collective-permute-start | bytes 786440 | tf_op jit(solution)/shard_map/ppermute | solution.py:41
  377.4 13.8 %collective-permute-start.91 = (f32[64,1024]{1,0:T(8,128)S(1)}, f32[64,1024]{1,0:T(8,128)S(1)}, u32[]{:S(2)}, u32[]{:S(2)}) collective-permute-start(f32[64,1024]{1,0:T(8,128)S(1)} %get-tuple-element.172), channel_id=1, source_target_pairs={{0,100},{1,101},{2,102},{3,103},{4,96},{5,97},{6,98},{7,99},{8,108... | collective-permute-start | bytes 786440 | tf_op jit(solution)/shard_map/ppermute | solution.py:41
  379.3 11.9 %collective-permute-start.94 = (bf16[64,1024]{1,0:T(8,128)(2,1)S(1)}, bf16[64,1024]{1,0:T(8,128)(2,1)S(1)}, u32[]{:S(2)}, u32[]{:S(2)}) collective-permute-start(bf16[64,1024]{1,0:T(8,128)(2,1)S(1)} %get-tuple-element.175), channel_id=1, source_target_pairs={{0,124},{1,125},{2,126},{3,127},{4,120},{5,121},{6,122},{7,123},{8... | collective-permute-start | bytes 393224 | tf_op jit(solution)/shard_map/ppermute | solution.py:41
  401.3 26.2 %collective-permute-start.99 = (bf16[256,1024]{1,0:T(8,128)(2,1)S(1)}, bf16[256,1024]{1,0:T(8,128)(2,1)S(1)}, u32[]{:S(2)}, u32[]{:S(2)}) collective-permute-start(bf16[256,1024]{1,0:T(8,128)(2,1)S(1)} %pad_maximum_fusion.3.refs_0_), channel_id=1, source_target_pairs={{0,1},{1,2},{2,3},{3,0},{4,5},{5,6},{6,7},{7,4},{8,9},{9,10},{10,1... | collective-permute-start | bytes 1572872 | tf_op jit(solution)/shard_map/ppermute | solution.py:41
  430.2 14.6 %collective-permute-start.103 = (bf16[1024,128]{1,0:T(8,128)(2,1)S(1)}, bf16[1024,128]{1,0:T(8,128)(2,1)S(1)}, u32[]{:S(2)}, u32[]{:S(2)}) collective-permute-start(bf16[1024,128]{1,0:T(8,128)(2,1)S(1)} %own_columns.7.refs_4_), channel_id=1, source_target_pairs={{0,16},{1,17},{2,18},{3,19},{4,20},{5,21},{6,22},{7,23},{8,24},{9,... | collective-permute-start | bytes 786440 | tf_op jit(solution)/shard_map/ppermute | solution.py:41
  433.2 12.3 %collective-permute-start.102 = (bf16[1024,128]{1,0:T(8,128)(2,1)S(1)}, bf16[1024,128]{1,0:T(8,128)(2,1)S(1)}, u32[]{:S(2)}, u32[]{:S(2)}) collective-permute-start(bf16[1024,128]{1,0:T(8,128)(2,1)S(1)} %own_columns.7.refs_4_), channel_id=1, source_target_pairs={{0,8},{1,9},{2,10},{3,11},{4,12},{5,13},{6,14},{7,15},{8,16},{9,17... | collective-permute-start | bytes 786440 | tf_op jit(solution)/shard_map/ppermute | solution.py:41
  449.4 13.8 %collective-permute-start.107 = (bf16[128,1024]{1,0:T(8,128)(2,1)S(1)}, bf16[128,1024]{1,0:T(8,128)(2,1)S(1)}, u32[]{:S(2)}, u32[]{:S(2)}) collective-permute-start(bf16[128,1024]{1,0:T(8,128)(2,1)S(1)} %get-tuple-element.184), channel_id=1, source_target_pairs={{0,24},{1,25},{2,26},{3,27},{4,28},{5,29},{6,30},{7,31},{8,0},{9,1... | collective-permute-start | bytes 786440 | tf_op jit(solution)/shard_map/ppermute | solution.py:41
  (44 other events, 368.6 us)
